TPU v7x, 256 devices: a whole 4x4x8 slice. The times are simulated.
256 devices in a mesh: tile: 128 (over x, y_lo, z, core), member: 2 (over y_hi).
Axes of the slice: x: 4, y: 4 (y_hi: 2, y_lo: 2; y = y_hi * 2 + y_lo), z: 8, core: 2. Of those that a mesh axis runs over, the one named last changes fastest.
Arguments:
- inputs: bfloat16 [2, 128, 64, 1024], P('member', 'tile'), may hold values from -6 to 6
- cotangent: bfloat16 [2, 128, 64, 256], P('member', 'tile'), may hold values from -6 to 6
- seam_codes: int32 [128, 4], P('tile'), may hold values from 0 to 3, as said below
- conv_one: bfloat16 [64, 576], replicated, may hold values from -0.25 to 0.25
- conv_two: bfloat16 [64, 576], replicated, may hold values from -0.25 to 0.25
- down_weight: bfloat16 [64, 256], replicated, may hold values from -0.375 to 0.375
Outputs:
- encoded: bfloat16 [2, 128, 64, 256], P('member', 'tile')
- input_grad: bfloat16 [2, 128, 64, 1024], P('member', 'tile')
- conv_one_grad: float32 [64, 576], replicated
- conv_two_grad: float32 [64, 576], replicated
- down_grad: float32 [64, 256], replicated
Inputs may be any that keep to these rules, and one draw needn't show every extreme that they name: `seam_codes`: sides inside a face have code 0; across a face border the two sides of one seam carry reciprocal codes c and (4 - c) mod 4, the same along the whole border between two faces.
All inputs are finite; a program needn't handle non-finite values.
Results may differ from a plain program's by a relative error of at most 0.0061.
Values may be sent and summed in bfloat16 or wider, within the bound.
No kernel may reach another device: no remote copies, remote signals or barrier semaphores. Data moves between devices by JAX's collectives and lax.ppermute only.
A program may use at most 64 MiB of HBM per device.

v0:
```python
import math

import jax
import jax.numpy as jnp
from jax import lax
from jax.experimental import pallas as pl
from jax.experimental.pallas import tpu as pltpu
from jax.sharding import PartitionSpec as P

S = 32
C = 64
ROW_TILES = 8
PITCH = 36
BASE = 128
INNER = S * PITCH
FULL = INNER + 2 * BASE
WIDE = FULL + 2 * BASE
SLOT = 128
CORNER = 64
BF = jnp.bfloat16
F32 = jnp.float32


def call(body, outs, scratch, args, flops, name):
    specs = [
        pl.BlockSpec(memory_space=pltpu.SMEM if a.dtype == jnp.int32 else pltpu.VMEM) for a in args
    ]
    moved = sum(math.prod(o.shape) * o.dtype.itemsize for o in list(outs) + list(args))
    return pl.pallas_call(
        body,
        out_shape=outs,
        in_specs=specs,
        out_specs=[pl.BlockSpec(memory_space=pltpu.VMEM)] * len(outs),
        scratch_shapes=scratch,
        compiler_params=pltpu.CompilerParams(vmem_limit_bytes=24 * 2**20),
        cost_estimate=pl.CostEstimate(flops=flops, bytes_accessed=moved, transcendentals=0),
        name=name,
    )(*args)


def out(shape, dtype):
    return jax.ShapeDtypeStruct(shape, dtype)


def nt(a, b):
    return lax.dot_general(a, b, (((1,), (1,)), ((), ())), preferred_element_type=F32)


def mm(a, b):
    return jnp.dot(a, b, preferred_element_type=F32)


def lanes_of():
    lane = lax.broadcasted_iota(jnp.int32, (1, SLOT), 1)
    part = lane - CORNER
    return lane, lane >> 5, lane & 31, part, part >> 2, part & 3


def corner_offsets(j, width):
    if width == 2:
        return j >> 1, j & 1, j >= 0
    return 0 * j, 0 * j, j == 0


def source_row(facts, group, width, pitch, base):
    lane, depth, along, part, kind, j = lanes_of()
    side, code = facts[0, group], facts[0, 4 + group]
    edge = (side - code + 4) & 3
    along = jnp.where((code & 1) == 1, 31 - along, along)
    level = jnp.where(edge >= 2, depth, depth)
    near = jnp.where((edge == 1) | (edge == 2), 31 - level, level)
    rows = (edge & 1) == 0
    y = jnp.where(rows, near, along)
    x = jnp.where(rows, along, near)
    valid = lane < S * width
    if group >= 2:
        u, v, there = corner_offsets(j, width)
        mine = (part >= 0) & (kind < 4) & ((kind & 1) == group - 2) & there
        cy = jnp.where(kind >= 2, S - width + u, u)
        cx = jnp.where(side == 1, S - width + v, v)
        y = jnp.where(mine, cy, y)
        x = jnp.where(mine, cx, x)
        valid = valid | mine
    return jnp.where(valid, base + pitch * y + x, -1)


def rim_row(facts, group, width):
    lane, depth, along, part, kind, j = lanes_of()
    side, second = facts[0, group], facts[0, 2]
    beyond = jnp.where((side == 0) | (side == 3), -1 - depth, S + depth)
    rows = (side & 1) == 0
    y = jnp.where(rows, beyond, along)
    x = jnp.where(rows, along, beyond)
    valid = lane < S * width
    if group < 2:
        u, v, there = corner_offsets(j, width)
        south = jnp.where(side == 0, 1, 0)
        mine = (part >= 0) & (kind < 4) & ((kind >> 1) == south) & there
        east = jnp.where((kind & 1) == 0, second, 4 - second) == 1
        cy = jnp.where(side == 0, u - width, S + u)
        cx = jnp.where(east, S + v, v - width)
        y = jnp.where(mine, cy, y)
        x = jnp.where(mine, cx, x)
        valid = valid | mine
    return jnp.where(valid, BASE + PITCH * y + x, -1)


def pick(rows, start, count):
    row = jnp.concatenate(rows, axis=1)
    place = start + lax.broadcasted_iota(jnp.int32, (count, row.shape[1]), 0)
    return jnp.where(place == row, 1.0, 0.0).astype(BF)


def sources(facts, width, pitch=PITCH, base=BASE):
    return [source_row(facts, g, width, pitch, base) for g in range(4)]


def rims(facts, width):
    return [rim_row(facts, g, width) for g in range(4)]


def write_slots(refs, messages):
    for g, ref in enumerate(refs):
        ref[...] = messages[:, g * SLOT : (g + 1) * SLOT].astype(BF)


def read_slots(refs):
    return jnp.concatenate([r[...] for r in refs], axis=1)


def columns_mask():
    lane = lax.broadcasted_iota(jnp.int32, (1, INNER), 1)
    return lax.rem(lane, PITCH) < S


def taps(reach):
    return [(a - 1) * PITCH * reach + (b - 1) * reach for a in range(3) for b in range(3)]


def gelu_parts(x):
    k = math.sqrt(2.0 / math.pi)
    sq = x * x
    t = jnp.tanh(k * x * (1.0 + 0.044715 * sq))
    half = 0.5 * (1.0 + t)
    slope = half + 0.5 * x * (1.0 - t * t) * (k * (1.0 + 3.0 * 0.044715 * sq))
    return x * half, slope


def gather_taps(col, wide, reach, sign, start, count):
    for n, off in enumerate(taps(reach)):
        lo = BASE + start + sign * off
        col[C * n : C * (n + 1), :] = wide[:, lo : lo + count]


def up_matrix():
    m = lax.broadcasted_iota(jnp.int32, (1, 256), 1)
    place = lax.broadcasted_iota(jnp.int32, (INNER, 256), 0)
    return jnp.where(place == 72 * (m >> 4) + 2 * (m & 15), 1.0, 0.0).astype(BF)


def send_inputs_body(facts, x, *slots):
    hot = pick(sources(facts, 1, S, 0), 0, S * S)
    write_slots(slots, mm(x[...], hot))


def prepare_body(x, cot, down_t, spread, upstream, grad_two, wide, col):
    spread[...] = jnp.zeros_like(spread)
    for y in range(S):
        spread[:, BASE + PITCH * y : BASE + PITCH * y + S] = x[:, S * y : S * y + S]
    wide[...] = jnp.zeros_like(wide)
    wide[:, BASE : BASE + INNER] = nt(cot[...], up_matrix()).astype(BF)
    for n in range(4):
        lo = BASE - (n // 2) * PITCH - n % 2
        col[C * n : C * (n + 1), :] = wide[:, lo : lo + INNER]
    upstream[...] = wide[:, BASE : BASE + INNER]
    grad_two[...] = mm(down_t[...], col[...])


def first_body(facts, spread, r0, r1, r2, r3, w, ext, hidden, slope, m0, m1, m2, m3, wide, col):
    halo = nt(read_slots((r0, r1, r2, r3)), pick(rims(facts, 1), 0, FULL)).astype(BF)
    full = spread[...] + halo
    ext[...] = full
    wide[...] = jnp.zeros_like(wide)
    wide[:, BASE : BASE + FULL] = full
    gather_taps(col, wide, 1, 1, BASE, INNER)
    value, grad = gelu_parts(mm(w[...], col[...]))
    value = jnp.where(columns_mask(), value, 0.0).astype(BF)
    hidden[...] = value
    slope[...] = grad
    write_slots((m0, m1, m2, m3), mm(value, pick(sources(facts, 2), BASE, INNER)))


def second_body(
    facts, hidden, r0, r1, r2, r3, w, wt, grad_two,
    ext, hidden_two, delta, grad_mid, m0, m1, m2, m3, wide, col, col_full,
):
    rim = pick(rims(facts, 2), 0, FULL)
    halo = nt(read_slots((r0, r1, r2, r3)), rim).astype(BF)
    wide[...] = jnp.zeros_like(wide)
    wide[:, BASE : BASE + FULL] = halo
    wide[:, 2 * BASE : 2 * BASE + INNER] = halo[:, BASE : BASE + INNER] + hidden[...]
    ext[...] = wide[:, BASE : BASE + FULL]
    gather_taps(col, wide, 2, 1, BASE, INNER)
    value, grad = gelu_parts(mm(w[...], col[...]))
    hidden_two[...] = value.astype(BF)
    back = jnp.where(columns_mask(), grad * grad_two[...], 0.0).astype(BF)
    delta[...] = back
    wide[...] = jnp.zeros_like(wide)
    wide[:, 2 * BASE : 2 * BASE + INNER] = back
    gather_taps(col_full, wide, 2, -1, 0, FULL)
    pad = mm(wt[...], col_full[...])
    grad_mid[...] = pad[:, BASE : BASE + INNER]
    write_slots((m0, m1, m2, m3), mm(pad.astype(BF), rim))


def second_sums_body(scale, ext, hidden_two, delta, upstream, down, encoded, grad, grad_down, wide, col):
    wide[...] = jnp.zeros_like(wide)
    wide[:, BASE : BASE + FULL] = ext[...]
    gather_taps(col, wide, 2, 1, BASE, INNER)
    grad[...] = nt(delta[...], col[...]) * scale
    wide[:, 2 * BASE : 2 * BASE + INNER] = hidden_two[...]
    for n in range(4):
        lo = 2 * BASE + (n // 2) * PITCH + n % 2
        col[C * n : C * (n + 1), :] = wide[:, lo : lo + INNER]
    four = col[: 4 * C, :]
    grad_down[...] = nt(upstream[...], four) * scale
    encoded[...] = mm(mm(down[...], four).astype(BF), up_matrix()).astype(BF)


def third_body(scale, facts, grad_mid, r0, r1, r2, r3, slope, ext, delta, grad, wide, col):
    back = nt(read_slots((r0, r1, r2, r3)), pick(sources(facts, 2), BASE, INNER))
    back = (grad_mid[...] + back) * slope[...]
    back = jnp.where(columns_mask(), back, 0.0).astype(BF)
    delta[...] = back
    wide[...] = jnp.zeros_like(wide)
    wide[:, BASE : BASE + FULL] = ext[...]
    gather_taps(col, wide, 1, 1, BASE, INNER)
    grad[...] = nt(back, col[...]) * scale


def fourth_body(facts, delta, wt, grad, m0, m1, m2, m3, wide, col_full):
    wide[...] = jnp.zeros_like(wide)
    wide[:, 2 * BASE : 2 * BASE + INNER] = delta[...]
    gather_taps(col_full, wide, 1, -1, 0, FULL)
    pad = mm(wt[...], col_full[...])
    grad[...] = pad[:, BASE : BASE + INNER]
    write_slots((m0, m1, m2, m3), mm(pad.astype(BF), pick(rims(facts, 1), 0, FULL)))


def last_body(facts, grad, r0, r1, r2, r3, o):
    back = nt(read_slots((r0, r1, r2, r3)), pick(sources(facts, 1), BASE, INNER))
    back = (grad[...] + back).astype(BF)
    for y in range(S):
        o[:, S * y : S * y + S] = back[:, PITCH * y : PITCH * y + S]


def swap(value, step, parity):
    count = lax.axis_size("tile")
    pairs = []
    for t in range(count):
        if (t // step) % 2 == parity:
            u = (t + step) % count
            pairs += [(t, u), (u, t)]
    return lax.ppermute(value, "tile", pairs)


def lane():
    return lax.broadcasted_iota(jnp.int32, (C, SLOT), 1)


def exchange(m):
    r3 = swap(m[3], 1, 1)
    r2 = swap(m[2], 1, 0)
    corners = jnp.where(((lane() >> 2) & 1) == 0, r2, r3)
    r1 = swap(jnp.where(lane() < CORNER, m[1], corners), ROW_TILES, 1)
    r0 = swap(jnp.where(lane() < CORNER, m[0], corners), ROW_TILES, 0)
    return r0, r1, r2, r3


def exchange_back(m):
    r1 = swap(m[1], ROW_TILES, 1)
    r0 = swap(m[0], ROW_TILES, 0)
    corners = r0 + r1
    r3 = swap(jnp.where(lane() < CORNER, m[3], corners), 1, 1)
    r2 = swap(jnp.where(lane() < CORNER, m[2], corners), 1, 0)
    return r0, r1, r2, r3


def add_up(values):
    count = lax.axis_size("tile")
    core = lax.axis_index("tile") % 2
    half = values.shape[0] // 2
    low, high = values[:half], values[half:]

    def across(v, axis, bit, n):
        return lax.ppermute(v, axis, [(i, i ^ bit) for i in range(n)])

    got = across(jnp.where(core == 0, high, low), "tile", 1, count)
    part = jnp.where(core == 0, low, high) + got
    for axis, bit in [("member", 1)] + [("tile", 2**k) for k in range(4, 7)] + [("tile", 2**k) for k in range(1, 4)]:
        part = part.astype(BF)
        got = across(part, axis, bit, lax.axis_size(axis))
        part = part.astype(F32) + got.astype(F32)
    other = across(part, "tile", 1, count)
    first, then = jnp.where(core == 0, part, other), jnp.where(core == 0, other, part)
    return jnp.concatenate([first, then], axis=0)


def per_device(inputs, cotangent, seam_codes, conv_one, conv_two, down_weight):
    x, cot = inputs[0, 0], cotangent[0, 0]
    tile = lax.axis_index("tile").astype(jnp.int32)
    down_row = (tile // ROW_TILES) % 2 == 0
    even = tile % 2 == 0
    sides = jnp.stack(
        [jnp.where(down_row, 2, 0), jnp.where(down_row, 0, 2), jnp.where(even, 1, 3), jnp.where(even, 3, 1)]
    ).astype(jnp.int32)
    facts = jnp.concatenate([sides, seam_codes[0][sides]]).reshape(1, 8)
    count = lax.axis_size("tile") * lax.axis_size("member")
    scale = 1.0 / math.sqrt(count * S * S)

    def flip(w, n):
        return jnp.transpose(w.reshape(C, n, C), (2, 1, 0)).reshape(C, n * C)

    one_t, two_t, down_t = flip(conv_one, 9), flip(conv_two, 9), flip(down_weight, 4)
    slots = [out((C, SLOT), BF)] * 4
    wide, col = pltpu.VMEM((C, WIDE), BF), pltpu.VMEM((9 * C, INNER), BF)
    col_full = pltpu.VMEM((9 * C, FULL), BF)
    dense = 2 * C * 9 * C * INNER

    sent = call(send_inputs_body, slots, [], [facts, x], 2 * C * 1024 * 512, "send_inputs")
    spread, upstream, grad_two = call(
        prepare_body,
        [out((C, FULL), BF), out((C, INNER), BF), out((C, INNER), F32)],
        [wide, pltpu.VMEM((4 * C, INNER), BF)],
        [x, cot, down_t],
        dense,
        "prepare",
    )
    got = exchange(sent)
    ext, hidden, slope, *sent = call(
        first_body,
        [out((C, FULL), BF), out((C, INNER), BF), out((C, INNER), F32)] + slots,
        [wide, col],
        [facts, spread, *got, conv_one],
        2 * dense,
        "first",
    )
    got = exchange(sent)
    ext_two, hidden_two, delta_two, grad_mid, *sent = call(
        second_body,
        [out((C, FULL), BF), out((C, INNER), BF), out((C, INNER), BF), out((C, INNER), F32)] + slots,
        [wide, col, col_full],
        [facts, hidden, *got, conv_two, two_t, grad_two],
        3 * dense,
        "second",
    )
    got = exchange_back(sent)
    encoded, sum_two, sum_down = call(
        lambda *refs: second_sums_body(scale, *refs),
        [out((C, 256), BF), out((C, 9 * C), F32), out((C, 4 * C), F32)],
        [wide, col],
        [ext_two, hidden_two, delta_two, upstream, down_weight],
        2 * dense,
        "second_sums",
    )
    delta_one, sum_one = call(
        lambda *refs: third_body(scale, *refs),
        [out((C, INNER), BF), out((C, 9 * C), F32)],
        [wide, col],
        [facts, grad_mid, *got, slope, ext],
        2 * dense,
        "third",
    )
    grad_in, *sent = call(
        fourth_body,
        [out((C, INNER), F32)] + slots,
        [wide, col_full],
        [facts, delta_one, one_t],
        2 * dense,
        "fourth",
    )
    got = exchange_back(sent)
    (input_grad,) = call(
        last_body, [out((C, S * S), BF)], [], [facts, grad_in, *got], dense, "last"
    )
    total = add_up(jnp.concatenate([sum_one, sum_two, sum_down], axis=1))
    return (
        encoded.reshape(1, 1, C, 256),
        input_grad.reshape(1, 1, C, S * S),
        total[:, : 9 * C],
        total[:, 9 * C : 18 * C],
        total[:, 18 * C :],
    )


def solution(mesh):
    split = P("member", "tile", None, None)
    return jax.shard_map(
        per_device,
        mesh=mesh,
        in_specs=(split, split, P("tile", None), P(), P(), P()),
        out_specs=(split, split, P(), P(), P()),
        check_vma=False,
    )
```

profile of v0, /device:TPU:16, one launch (start us, length us, event | category | flops | bytes accessed | tf_op | source)
XLA Modules:
  0.0 138.2 jit_solution(10652676929355621350)
XLA Ops:
  3.2 8.9 %collective-permute-start.1 = (bf16[64,128]{1,0:T(8,128)(2,1)S(1)}, bf16[64,128]{1,0:T(8,128)(2,1)S(1)}, u32[]{:S(2)}, u32[]{:S(2)}) collective-permute-start(bf16[64,128]{1,0:T(8,128)(2,1)S(1)} %get-tuple-element.40), channel_id=1, source_target_pairs={{2,4},{4,2},{6,8},{8,6},{10,12},{12,10},{14,16},{16,14},{18,20},{2... | collective-permute-start | bytes 49160 | tf_op jit(solution)/shard_map/ppermute | solution.py:264
  12.0 1.4 %collective-permute-done.1.r3 = bf16[64,128]{1,0:T(8,128)(2,1)S(1)} collective-permute-done((bf16[64,128]{1,0:T(8,128)(2,1)S(1)}, bf16[64,128]{1,0:T(8,128)(2,1)S(1)}, u32[]{:S(2)}, u32[]{:S(2)}) %collective-permute-start.1) | collective-permute-done | bytes 16416 | tf_op jit(solution)/shard_map/ppermute | solution.py:264
  13.5 1.4 %collective-permute-start.2 = (bf16[64,128]{1,0:T(8,128)(2,1)S(1)}, bf16[64,128]{1,0:T(8,128)(2,1)S(1)}, u32[]{:S(2)}, u32[]{:S(2)}) collective-permute-start(bf16[64,128]{1,0:T(8,128)(2,1)S(1)} %get-tuple-element.76), channel_id=1, source_target_pairs={{0,16},{16,0},{2,18},{18,2},{4,20},{20,4},{6,22},{22,6},{8,24},{24... | collective-permute-start | bytes 49160 | tf_op jit(solution)/shard_map/ppermute | solution.py:264
  14.9 4.3 %collective-permute-start.3 = (bf16[64,128]{1,0:T(8,128)(2,1)S(1)}, bf16[64,128]{1,0:T(8,128)(2,1)S(1)}, u32[]{:S(2)}, u32[]{:S(2)}) collective-permute-start(bf16[64,128]{1,0:T(8,128)(2,1)S(1)} %get-tuple-element.75), channel_id=1, source_target_pairs={{16,32},{32,16},{18,34},{34,18},{20,36},{36,20},{22,38},{38,22},{2... | collective-permute-start | bytes 49160 | tf_op jit(solution)/shard_map/ppermute | solution.py:264
  21.5 4.1 %collective-permute-done.3.r1 = bf16[64,128]{1,0:T(8,128)(2,1)S(1)} collective-permute-done((bf16[64,128]{1,0:T(8,128)(2,1)S(1)}, bf16[64,128]{1,0:T(8,128)(2,1)S(1)}, u32[]{:S(2)}, u32[]{:S(2)}) %collective-permute-start.3) | collective-permute-done | bytes 16416 | tf_op jit(solution)/shard_map/ppermute | solution.py:264
  25.6 1.9 %first.1 = (bf16[64,1408]{1,0:T(8,128)(2,1)S(1)}, bf16[64,1152]{1,0:T(8,128)(2,1)S(1)}, f32[64,1152]{1,0:T(8,128)S(1)}, bf16[64,128]{1,0:T(8,128)(2,1)S(1)}, bf1...) custom-call(s32[1,8]{1,0:T(1,128)S(1)} %bitcast.27, ...), custom_call_target="tpu_custom_call" | custom-call | flops 169869312 | bytes 1007648 | tf_op jit(solution)/shard_map/first/pallas_call | solution.py:29
  27.6 3.6 %collective-permute-start.5 = (bf16[64,128]{1,0:T(8,128)(2,1)S(1)}, bf16[64,128]{1,0:T(8,128)(2,1)S(1)}, u32[]{:S(2)}, u32[]{:S(2)}) collective-permute-start(bf16[64,128]{1,0:T(8,128)(2,1)S(1)} %get-tuple-element.45), channel_id=1, source_target_pairs={{2,4},{4,2},{6,8},{8,6},{10,12},{12,10},{14,16},{16,14},{18,20},{2... | collective-permute-start | bytes 49160 | tf_op jit(solution)/shard_map/ppermute | solution.py:264
  31.2 3.8 %collective-permute-done.5.r3 = bf16[64,128]{1,0:T(8,128)(2,1)S(1)} collective-permute-done((bf16[64,128]{1,0:T(8,128)(2,1)S(1)}, bf16[64,128]{1,0:T(8,128)(2,1)S(1)}, u32[]{:S(2)}, u32[]{:S(2)}) %collective-permute-start.5) | collective-permute-done | bytes 16416 | tf_op jit(solution)/shard_map/ppermute | solution.py:264
  35.2 4.6 %collective-permute-start.7 = (bf16[64,128]{1,0:T(8,128)(2,1)S(1)}, bf16[64,128]{1,0:T(8,128)(2,1)S(1)}, u32[]{:S(2)}, u32[]{:S(2)}) collective-permute-start(bf16[64,128]{1,0:T(8,128)(2,1)S(1)} %get-tuple-element.73), channel_id=1, source_target_pairs={{16,32},{32,16},{18,34},{34,18},{20,36},{36,20},{22,38},{38,22},{2... | collective-permute-start | bytes 49160 | tf_op jit(solution)/shard_map/ppermute | solution.py:264
  40.2 2.7 %collective-permute-done.6.r0 = bf16[64,128]{1,0:T(8,128)(2,1)S(1)} collective-permute-done((bf16[64,128]{1,0:T(8,128)(2,1)S(1)}, bf16[64,128]{1,0:T(8,128)(2,1)S(1)}, u32[]{:S(2)}, u32[]{:S(2)}) %collective-permute-start.6) | collective-permute-done | bytes 16416 | tf_op jit(solution)/shard_map/ppermute | solution.py:264
  43.0 2.9 %collective-permute-done.7.r1 = bf16[64,128]{1,0:T(8,128)(2,1)S(1)} collective-permute-done((bf16[64,128]{1,0:T(8,128)(2,1)S(1)}, bf16[64,128]{1,0:T(8,128)(2,1)S(1)}, u32[]{:S(2)}, u32[]{:S(2)}) %collective-permute-start.7) | collective-permute-done | bytes 16416 | tf_op jit(solution)/shard_map/ppermute | solution.py:264
  45.9 2.5 %second.1 = (bf16[64,1408]{1,0:T(8,128)(2,1)S(1)}, bf16[64,1152]{1,0:T(8,128)(2,1)S(1)}, bf16[64,1152]{1,0:T(8,128)(2,1)S(1)}, f32[64,1152]{1,0:T(8,128)S(1)}, b...) custom-call(s32[1,8]{1,0:T(1,128)S(1)} %bitcast.28, ...), custom_call_target="tpu_custom_call" | custom-call | flops 254803968 | bytes 1490976 | tf_op jit(solution)/shard_map/second/pallas_call | solution.py:29
  48.4 3.8 %collective-permute-start.8 = (bf16[64,128]{1,0:T(8,128)(2,1)S(1)}, bf16[64,128]{1,0:T(8,128)(2,1)S(1)}, u32[]{:S(2)}, u32[]{:S(2)}) collective-permute-start(bf16[64,128]{1,0:T(8,128)(2,1)S(1)} %get-tuple-element.54), channel_id=1, source_target_pairs={{0,16},{16,0},{2,18},{18,2},{4,20},{20,4},{6,22},{22,6},{8,24},{24... | collective-permute-start | bytes 49160 | tf_op jit(solution)/shard_map/ppermute | solution.py:264
  52.2 1.3 collective-permute-start.9
  53.5 2.7 %collective-permute-done.8.refs_2_ = bf16[64,128]{1,0:T(8,128)(2,1)S(1)} collective-permute-done((bf16[64,128]{1,0:T(8,128)(2,1)S(1)}, bf16[64,128]{1,0:T(8,128)(2,1)S(1)}, u32[]{:S(2)}, u32[]{:S(2)}) %collective-permute-start.8) | collective-permute-done | bytes 16416 | tf_op jit(solution)/shard_map/ppermute | solution.py:264
  56.2 6.7 %collective-permute-done.9.refs_3_ = bf16[64,128]{1,0:T(8,128)(2,1)S(1)} collective-permute-done((bf16[64,128]{1,0:T(8,128)(2,1)S(1)}, bf16[64,128]{1,0:T(8,128)(2,1)S(1)}, u32[]{:S(2)}, u32[]{:S(2)}) %collective-permute-start.9) | collective-permute-done | bytes 16416 | tf_op jit(solution)/shard_map/ppermute | solution.py:264
  64.0 1.6 %second_sums.1 = (bf16[64,256]{1,0:T(8,128)(2,1)}, f32[64,576]{1,0:T(8,128)S(1)}, f32[64,256]{1,0:T(8,128)S(1)}) custom-call(bf16[64,1408]{1,0:T(8,128)(2,1)S(1)} %get-tuple-element.48.refs_0_, bf16[64,1152]{1,0:T(8,128)(2,1)S(1)} %get-tuple-element.49.refs_1_, bf16[64,1152]{1,0:T(8,128)(2,1)S(1)} %get-tuple-element.50.refs_2_, ...), custom_call_target="tpu_custom_call" | custom-call | flops 169869312 | bytes 901120 | tf_op jit(solution)/shard_map/second_sums/pallas_call | solution.py:29
  65.6 5.2 %collective-permute-done.11.refs_5_ = bf16[64,128]{1,0:T(8,128)(2,1)S(1)} collective-permute-done((bf16[64,128]{1,0:T(8,128)(2,1)S(1)}, bf16[64,128]{1,0:T(8,128)(2,1)S(1)}, u32[]{:S(2)}, u32[]{:S(2)}) %collective-permute-start.11) | collective-permute-done | bytes 16416 | tf_op jit(solution)/shard_map/ppermute | solution.py:264
  70.8 1.5 %third.1 = (bf16[64,1152]{1,0:T(8,128)(2,1)S(1)}, f32[64,576]{1,0:T(8,128)S(1)}) custom-call(s32[1,8]{1,0:T(1,128)S(1)} %bitcast.29, f32[64,1152]{1,0:T(8,128)S(1)} %get-tuple-element.53.refs_1_, bf16[64,128]{1,0:T(8,128)(2,1)S(1)} %collective-permute-done.8.refs_2_, bf16[64,128]{1,0:T(8,128)(2,1)S(1)} %collective-permute-done.9.refs_3_, ...), custom_call_target="tpu_custom_call" | custom-call | flops 169869312 | bytes 1130528 | tf_op jit(solution)/shard_map/third/pallas_call | solution.py:29
  72.5 1.4 %collective-permute-done.16 = f32[32,1408]{1,0:T(8,128)S(1)} collective-permute-done((f32[32,1408]{1,0:T(8,128)S(1)}, f32[32,1408]{1,0:T(8,128)S(1)}, u32[]{:S(2)}, u32[]{:S(2)}) %collective-permute-start.16) | collective-permute-done | bytes 180256 | tf_op jit(solution)/shard_map/ppermute | solution.py:296
  74.3 5.9 %collective-permute-done.17 = bf16[32,1408]{1,0:T(8,128)(2,1)S(1)} collective-permute-done((bf16[32,1408]{1,0:T(8,128)(2,1)S(1)}, bf16[32,1408]{1,0:T(8,128)(2,1)S(1)}, u32[]{:S(2)}, u32[]{:S(2)}) %collective-permute-start.17) | collective-permute-done | bytes 90144 | tf_op jit(solution)/shard_map/ppermute | solution.py:296
  80.3 4.5 %collective-permute-done.18 = bf16[32,1408]{1,0:T(8,128)(2,1)S(1)} collective-permute-done((bf16[32,1408]{1,0:T(8,128)(2,1)S(1)}, bf16[32,1408]{1,0:T(8,128)(2,1)S(1)}, u32[]{:S(2)}, u32[]{:S(2)}) %collective-permute-start.18) | collective-permute-done | bytes 90144 | tf_op jit(solution)/shard_map/ppermute | solution.py:296
  85.0 4.7 %collective-permute-done.19 = bf16[32,1408]{1,0:T(8,128)(2,1)S(1)} collective-permute-done((bf16[32,1408]{1,0:T(8,128)(2,1)S(1)}, bf16[32,1408]{1,0:T(8,128)(2,1)S(1)}, u32[]{:S(2)}, u32[]{:S(2)}) %collective-permute-start.19) | collective-permute-done | bytes 90144 | tf_op jit(solution)/shard_map/ppermute | solution.py:296
  89.8 6.0 %collective-permute-done.20 = bf16[32,1408]{1,0:T(8,128)(2,1)S(1)} collective-permute-done((bf16[32,1408]{1,0:T(8,128)(2,1)S(1)}, bf16[32,1408]{1,0:T(8,128)(2,1)S(1)}, u32[]{:S(2)}, u32[]{:S(2)}) %collective-permute-start.20) | collective-permute-done | bytes 90144 | tf_op jit(solution)/shard_map/ppermute | solution.py:296
  96.0 5.8 %collective-permute-done.21 = bf16[32,1408]{1,0:T(8,128)(2,1)S(1)} collective-permute-done((bf16[32,1408]{1,0:T(8,128)(2,1)S(1)}, bf16[32,1408]{1,0:T(8,128)(2,1)S(1)}, u32[]{:S(2)}, u32[]{:S(2)}) %collective-permute-start.21) | collective-permute-done | bytes 90144 | tf_op jit(solution)/shard_map/ppermute | solution.py:296
  101.9 6.7 %collective-permute-done.22 = bf16[32,1408]{1,0:T(8,128)(2,1)S(1)} collective-permute-done((bf16[32,1408]{1,0:T(8,128)(2,1)S(1)}, bf16[32,1408]{1,0:T(8,128)(2,1)S(1)}, u32[]{:S(2)}, u32[]{:S(2)}) %collective-permute-start.22) | collective-permute-done | bytes 90144 | tf_op jit(solution)/shard_map/ppermute | solution.py:296
  109.2 1.4 %fourth.1 = (f32[64,1152]{1,0:T(8,128)S(1)}, bf16[64,128]{1,0:T(8,128)(2,1)S(1)}, bf16[64,128]{1,0:T(8,128)(2,1)S(1)}, bf16[64,128]{1,0:T(8,128)(2,1)S(1)}, bf16[64,128]{1,0:T(8,128)(2,1)S(1)}) custom-call(s32[1,8]{1,0:T(1,128)S(1)} %bitcast.30, bf16[64,1152]{1,0:T(8,128)(2,1)S(1)} %get-tuple-element.60.delta, bf16[64,576]{1,0:T(8,128)(2,1)S(1)} %copy.20.wt), custom_call_target="tpu_custom_call" | custom-call | flops 169869312 | bytes 581664 | tf_op jit(solution)/shard_map/fourth/pallas_call | solution.py:29
  110.6 6.0 %collective-permute-start.12 = (bf16[64,128]{1,0:T(8,128)(2,1)S(1)}, bf16[64,128]{1,0:T(8,128)(2,1)S(1)}, u32[]{:S(2)}, u32[]{:S(2)}) collective-permute-start(bf16[64,128]{1,0:T(8,128)(2,1)S(1)} %get-tuple-element.62), channel_id=1, source_target_pairs={{0,16},{16,0},{2,18},{18,2},{4,20},{20,4},{6,22},{22,6},{8,24},{24... | collective-permute-start | bytes 49160 | tf_op jit(solution)/shard_map/ppermute | solution.py:264
  118.3 8.9 %collective-permute-done.13.r1 = bf16[64,128]{1,0:T(8,128)(2,1)S(1)} collective-permute-done((bf16[64,128]{1,0:T(8,128)(2,1)S(1)}, bf16[64,128]{1,0:T(8,128)(2,1)S(1)}, u32[]{:S(2)}, u32[]{:S(2)}) %collective-permute-start.13) | collective-permute-done | bytes 16416 | tf_op jit(solution)/shard_map/ppermute | solution.py:264
  127.4 1.4 %collective-permute-start.15 = (bf16[64,128]{1,0:T(8,128)(2,1)S(1)}, bf16[64,128]{1,0:T(8,128)(2,1)S(1)}, u32[]{:S(2)}, u32[]{:S(2)}) collective-permute-start(bf16[64,128]{1,0:T(8,128)(2,1)S(1)} %get-tuple-element.77), channel_id=1, source_target_pairs={{2,4},{4,2},{6,8},{8,6},{10,12},{12,10},{14,16},{16,14},{18,20},{2... | collective-permute-start | bytes 49160 | tf_op jit(solution)/shard_map/ppermute | solution.py:264
  128.8 6.1 %collective-permute-done.15.r3 = bf16[64,128]{1,0:T(8,128)(2,1)S(1)} collective-permute-done((bf16[64,128]{1,0:T(8,128)(2,1)S(1)}, bf16[64,128]{1,0:T(8,128)(2,1)S(1)}, u32[]{:S(2)}, u32[]{:S(2)}) %collective-permute-start.15) | collective-permute-done | bytes 16416 | tf_op jit(solution)/shard_map/ppermute | solution.py:264
  134.8 1.9 %last.1 = bf16[64,1024]{1,0:T(8,128)(2,1)} custom-call(s32[1,8]{1,0:T(1,128)S(1)} %bitcast.31, f32[64,1152]{1,0:T(8,128)S(1)} %get-tuple-element.61.grad, bf16[64,128]{1,0:T(8,128)(2,1)S(1)} %collective-permute-done.12.r0, bf16[64,128]{1,0:T(8,128)(2,1)S(1)} %collective-permute-done.13.r1, bf16[64,128]{1,0:T(8,128)(2,1)S(1)} %collective-permute-done.14.r2, ...), custom_call_target="tpu_custom_call" | custom-call | flops 84934656 | bytes 491552 | tf_op jit(solution)/shard_map/last/pallas_call | solution.py:29
  (69 shorter events, 11.5 us)
Async XLA Ops:
  0.6 0.7 copy-start
  1.3 0.9 copy-start.4
  3.1 9.0 %collective-permute-start = (bf16[64,128]{1,0:T(8,128)(2,1)S(1)}, bf16[64,128]{1,0:T(8,128)(2,1)S(1)}, u32[]{:S(2)}, u32[]{:S(2)}) collective-permute-start(bf16[64,128]{1,0:T(8,128)(2,1)S(1)} %get-tuple-element.39), channel_id=1, source_target_pairs={{0,2},{2,0},{4,6},{6,4},{8,10},{10,8},{12,14},{14,12},{16,18},{18,... | collective-permute-start | bytes 49160 | tf_op jit(solution)/shard_map/ppermute | solution.py:264
  3.2 10.3 %collective-permute-start.1 = (bf16[64,128]{1,0:T(8,128)(2,1)S(1)}, bf16[64,128]{1,0:T(8,128)(2,1)S(1)}, u32[]{:S(2)}, u32[]{:S(2)}) collective-permute-start(bf16[64,128]{1,0:T(8,128)(2,1)S(1)} %get-tuple-element.40), channel_id=1, source_target_pairs={{2,4},{4,2},{6,8},{8,6},{10,12},{12,10},{14,16},{16,14},{18,20},{2... | collective-permute-start | bytes 49160 | tf_op jit(solution)/shard_map/ppermute | solution.py:264
  13.5 5.7 %copy-start.1 = (bf16[64,256]{1,0:T(8,128)(2,1)S(1)}, bf16[64,256]{1,0:T(8,128)(2,1)}, u32[]{:S(2)}) copy-start(bf16[64,256]{1,0:T(8,128)(2,1)} %refs_4_.1) | copy-start | bytes 98308
  13.5 8.0 %collective-permute-start.2 = (bf16[64,128]{1,0:T(8,128)(2,1)S(1)}, bf16[64,128]{1,0:T(8,128)(2,1)S(1)}, u32[]{:S(2)}, u32[]{:S(2)}) collective-permute-start(bf16[64,128]{1,0:T(8,128)(2,1)S(1)} %get-tuple-element.76), channel_id=1, source_target_pairs={{0,16},{16,0},{2,18},{18,2},{4,20},{20,4},{6,22},{22,6},{8,24},{24... | collective-permute-start | bytes 49160 | tf_op jit(solution)/shard_map/ppermute | solution.py:264
  14.9 10.7 %collective-permute-start.3 = (bf16[64,128]{1,0:T(8,128)(2,1)S(1)}, bf16[64,128]{1,0:T(8,128)(2,1)S(1)}, u32[]{:S(2)}, u32[]{:S(2)}) collective-permute-start(bf16[64,128]{1,0:T(8,128)(2,1)S(1)} %get-tuple-element.75), channel_id=1, source_target_pairs={{16,32},{32,16},{18,34},{34,18},{20,36},{36,20},{22,38},{38,22},{2... | collective-permute-start | bytes 49160 | tf_op jit(solution)/shard_map/ppermute | solution.py:264
  19.4 0.8 copy-start.5
  20.2 5.4 %copy-start.3 = (bf16[64,576]{1,0:T(8,128)(2,1)S(1)}, bf16[64,576]{1,0:T(8,128)(2,1)}, u32[]{:S(2)}) copy-start(bf16[64,576]{1,0:T(8,128)(2,1)} %w.2) | copy-start | bytes 221188
  27.5 12.3 %copy-start.2 = (bf16[64,576]{1,0:T(8,128)(2,1)S(1)}, bf16[64,576]{1,0:T(8,128)(2,1)}, u32[]{:S(2)}) copy-start(bf16[64,576]{1,0:T(8,128)(2,1)} %w.3) | copy-start | bytes 221188
  27.5 3.7 %collective-permute-start.4 = (bf16[64,128]{1,0:T(8,128)(2,1)S(1)}, bf16[64,128]{1,0:T(8,128)(2,1)S(1)}, u32[]{:S(2)}, u32[]{:S(2)}) collective-permute-start(bf16[64,128]{1,0:T(8,128)(2,1)S(1)} %get-tuple-element.44), channel_id=1, source_target_pairs={{0,2},{2,0},{4,6},{6,4},{8,10},{10,8},{12,14},{14,12},{16,18},{18,... | collective-permute-start | bytes 49160 | tf_op jit(solution)/shard_map/ppermute | solution.py:264
  27.6 7.5 %collective-permute-start.5 = (bf16[64,128]{1,0:T(8,128)(2,1)S(1)}, bf16[64,128]{1,0:T(8,128)(2,1)S(1)}, u32[]{:S(2)}, u32[]{:S(2)}) collective-permute-start(bf16[64,128]{1,0:T(8,128)(2,1)S(1)} %get-tuple-element.45), channel_id=1, source_target_pairs={{2,4},{4,2},{6,8},{8,6},{10,12},{12,10},{14,16},{16,14},{18,20},{2... | collective-permute-start | bytes 49160 | tf_op jit(solution)/shard_map/ppermute | solution.py:264
  35.1 7.9 %collective-permute-start.6 = (bf16[64,128]{1,0:T(8,128)(2,1)S(1)}, bf16[64,128]{1,0:T(8,128)(2,1)S(1)}, u32[]{:S(2)}, u32[]{:S(2)}) collective-permute-start(bf16[64,128]{1,0:T(8,128)(2,1)S(1)} %get-tuple-element.74), channel_id=1, source_target_pairs={{0,16},{16,0},{2,18},{18,2},{4,20},{20,4},{6,22},{22,6},{8,24},{24... | collective-permute-start | bytes 49160 | tf_op jit(solution)/shard_map/ppermute | solution.py:264
  35.2 10.7 %collective-permute-start.7 = (bf16[64,128]{1,0:T(8,128)(2,1)S(1)}, bf16[64,128]{1,0:T(8,128)(2,1)S(1)}, u32[]{:S(2)}, u32[]{:S(2)}) collective-permute-start(bf16[64,128]{1,0:T(8,128)(2,1)S(1)} %get-tuple-element.73), channel_id=1, source_target_pairs={{16,32},{32,16},{18,34},{34,18},{20,36},{36,20},{22,38},{38,22},{2... | collective-permute-start | bytes 49160 | tf_op jit(solution)/shard_map/ppermute | solution.py:264
  48.4 7.7 %collective-permute-start.8 = (bf16[64,128]{1,0:T(8,128)(2,1)S(1)}, bf16[64,128]{1,0:T(8,128)(2,1)S(1)}, u32[]{:S(2)}, u32[]{:S(2)}) collective-permute-start(bf16[64,128]{1,0:T(8,128)(2,1)S(1)} %get-tuple-element.54), channel_id=1, source_target_pairs={{0,16},{16,0},{2,18},{18,2},{4,20},{20,4},{6,22},{22,6},{8,24},{24... | collective-permute-start | bytes 49160 | tf_op jit(solution)/shard_map/ppermute | solution.py:264
  52.2 10.7 %collective-permute-start.9 = (bf16[64,128]{1,0:T(8,128)(2,1)S(1)}, bf16[64,128]{1,0:T(8,128)(2,1)S(1)}, u32[]{:S(2)}, u32[]{:S(2)}) collective-permute-start(bf16[64,128]{1,0:T(8,128)(2,1)S(1)} %get-tuple-element.55), channel_id=1, source_target_pairs={{16,32},{32,16},{18,34},{34,18},{20,36},{36,20},{22,38},{38,22},{2... | collective-permute-start | bytes 49160 | tf_op jit(solution)/shard_map/ppermute | solution.py:264
  62.9 2.7 %collective-permute-start.10 = (bf16[64,128]{1,0:T(8,128)(2,1)S(1)}, bf16[64,128]{1,0:T(8,128)(2,1)S(1)}, u32[]{:S(2)}, u32[]{:S(2)}) collective-permute-start(bf16[64,128]{1,0:T(8,128)(2,1)S(1)} %get-tuple-element.80), channel_id=1, source_target_pairs={{0,2},{2,0},{4,6},{6,4},{8,10},{10,8},{12,14},{14,12},{16,18},{18,... | collective-permute-start | bytes 49160 | tf_op jit(solution)/shard_map/ppermute | solution.py:264
  63.0 7.8 %collective-permute-start.11 = (bf16[64,128]{1,0:T(8,128)(2,1)S(1)}, bf16[64,128]{1,0:T(8,128)(2,1)S(1)}, u32[]{:S(2)}, u32[]{:S(2)}) collective-permute-start(bf16[64,128]{1,0:T(8,128)(2,1)S(1)} %get-tuple-element.79), channel_id=1, source_target_pairs={{2,4},{4,2},{6,8},{8,6},{10,12},{12,10},{14,16},{16,14},{18,20},{2... | collective-permute-start | bytes 49160 | tf_op jit(solution)/shard_map/ppermute | solution.py:264
  72.4 1.5 %collective-permute-start.16 = (f32[32,1408]{1,0:T(8,128)S(1)}, f32[32,1408]{1,0:T(8,128)S(1)}, u32[]{:S(2)}, u32[]{:S(2)}) collective-permute-start(f32[32,1408]{1,0:T(8,128)S(1)} %slice_select_fusion), channel_id=1, source_target_pairs={{0,2},{2,0},{4,6},{6,4},{8,10},{10,8},{12,14},{14,12},{16,18},{18,... | collective-permute-start | bytes 540680 | tf_op jit(solution)/shard_map/ppermute | solution.py:296
  73.9 6.3 %collective-permute-start.17 = (bf16[32,1408]{1,0:T(8,128)(2,1)S(1)}, bf16[32,1408]{1,0:T(8,128)(2,1)S(1)}, u32[]{:S(2)}, u32[]{:S(2)}) collective-permute-start(bf16[32,1408]{1,0:T(8,128)(2,1)S(1)} %add_convert_fusion.6), channel_id=1, source_target_pairs={{0,1},{1,0},{2,3},{3,2},{4,5},{5,4},{6,7},{7,6},{8,9},{9,8},{10,11... | collective-permute-start | bytes 270344 | tf_op jit(solution)/shard_map/ppermute | solution.py:296
  80.2 4.6 %collective-permute-start.18 = (bf16[32,1408]{1,0:T(8,128)(2,1)S(1)}, bf16[32,1408]{1,0:T(8,128)(2,1)S(1)}, u32[]{:S(2)}, u32[]{:S(2)}) collective-permute-start(bf16[32,1408]{1,0:T(8,128)(2,1)S(1)} %add_convert_fusion.5), channel_id=1, source_target_pairs={{0,32},{2,34},{4,36},{6,38},{8,40},{10,42},{12,44},{14,46},{16,48}... | collective-permute-start | bytes 270344 | tf_op jit(solution)/shard_map/ppermute | solution.py:296
  84.9 4.8 %collective-permute-start.19 = (bf16[32,1408]{1,0:T(8,128)(2,1)S(1)}, bf16[32,1408]{1,0:T(8,128)(2,1)S(1)}, u32[]{:S(2)}, u32[]{:S(2)}) collective-permute-start(bf16[32,1408]{1,0:T(8,128)(2,1)S(1)} %add_convert_fusion.4), channel_id=1, source_target_pairs={{0,64},{2,66},{4,68},{6,70},{8,72},{10,74},{12,76},{14,78},{16,80}... | collective-permute-start | bytes 270344 | tf_op jit(solution)/shard_map/ppermute | solution.py:296
  89.7 6.1 %collective-permute-start.20 = (bf16[32,1408]{1,0:T(8,128)(2,1)S(1)}, bf16[32,1408]{1,0:T(8,128)(2,1)S(1)}, u32[]{:S(2)}, u32[]{:S(2)}) collective-permute-start(bf16[32,1408]{1,0:T(8,128)(2,1)S(1)} %add_convert_fusion.3), channel_id=1, source_target_pairs={{0,128},{2,130},{4,132},{6,134},{8,136},{10,138},{12,140},{14,142}... | collective-permute-start | bytes 270344 | tf_op jit(solution)/shard_map/ppermute | solution.py:296
  95.9 5.9 %collective-permute-start.21 = (bf16[32,1408]{1,0:T(8,128)(2,1)S(1)}, bf16[32,1408]{1,0:T(8,128)(2,1)S(1)}, u32[]{:S(2)}, u32[]{:S(2)}) collective-permute-start(bf16[32,1408]{1,0:T(8,128)(2,1)S(1)} %add_convert_fusion.2), channel_id=1, source_target_pairs={{0,4},{2,6},{4,0},{6,2},{8,12},{10,14},{12,8},{14,10},{16,20},{18,... | collective-permute-start | bytes 270344 | tf_op jit(solution)/shard_map/ppermute | solution.py:296
  101.8 6.8 %collective-permute-start.22 = (bf16[32,1408]{1,0:T(8,128)(2,1)S(1)}, bf16[32,1408]{1,0:T(8,128)(2,1)S(1)}, u32[]{:S(2)}, u32[]{:S(2)}) collective-permute-start(bf16[32,1408]{1,0:T(8,128)(2,1)S(1)} %add_convert_fusion.1), channel_id=1, source_target_pairs={{0,8},{2,10},{4,12},{6,14},{8,0},{10,2},{12,4},{14,6},{16,24},{18,... | collective-permute-start | bytes 270344 | tf_op jit(solution)/shard_map/ppermute | solution.py:296
  108.6 8.5 %collective-permute-start.23 = (bf16[32,1408]{1,0:T(8,128)(2,1)S(1)}, bf16[32,1408]{1,0:T(8,128)(2,1)S(1)}, u32[]{:S(2)}, u32[]{:S(2)}) collective-permute-start(bf16[32,1408]{1,0:T(8,128)(2,1)S(1)} %add_convert_fusion), channel_id=1, source_target_pairs={{0,16},{2,18},{4,20},{6,22},{8,24},{10,26},{12,28},{14,30},{16,0},... | collective-permute-start | bytes 270344 | tf_op jit(solution)/shard_map/ppermute | solution.py:296
  110.6 7.7 %collective-permute-start.12 = (bf16[64,128]{1,0:T(8,128)(2,1)S(1)}, bf16[64,128]{1,0:T(8,128)(2,1)S(1)}, u32[]{:S(2)}, u32[]{:S(2)}) collective-permute-start(bf16[64,128]{1,0:T(8,128)(2,1)S(1)} %get-tuple-element.62), channel_id=1, source_target_pairs={{0,16},{16,0},{2,18},{18,2},{4,20},{20,4},{6,22},{22,6},{8,24},{24... | collective-permute-start | bytes 49160 | tf_op jit(solution)/shard_map/ppermute | solution.py:264
  116.6 10.7 %collective-permute-start.13 = (bf16[64,128]{1,0:T(8,128)(2,1)S(1)}, bf16[64,128]{1,0:T(8,128)(2,1)S(1)}, u32[]{:S(2)}, u32[]{:S(2)}) collective-permute-start(bf16[64,128]{1,0:T(8,128)(2,1)S(1)} %get-tuple-element.63), channel_id=1, source_target_pairs={{16,32},{32,16},{18,34},{34,18},{20,36},{36,20},{22,38},{38,22},{2... | collective-permute-start | bytes 49160 | tf_op jit(solution)/shard_map/ppermute | solution.py:264
  117.2 19.5 %collective-permute-start.24 = (f32[32,1408]{1,0:T(8,128)S(1)}, f32[32,1408]{1,0:T(8,128)S(1)}, u32[]{:S(2)}, u32[]{:S(2)}) collective-permute-start(f32[32,1408]{1,0:T(8,128)S(1)} %convert_add_fusion), channel_id=1, source_target_pairs={{0,2},{2,0},{4,6},{6,4},{8,10},{10,8},{12,14},{14,12},{16,18},{18,... | collective-permute-start | bytes 540680 | tf_op jit(solution)/shard_map/ppermute | solution.py:296
  127.3 1.5 %collective-permute-start.14 = (bf16[64,128]{1,0:T(8,128)(2,1)S(1)}, bf16[64,128]{1,0:T(8,128)(2,1)S(1)}, u32[]{:S(2)}, u32[]{:S(2)}) collective-permute-start(bf16[64,128]{1,0:T(8,128)(2,1)S(1)} %get-tuple-element.78), channel_id=1, source_target_pairs={{0,2},{2,0},{4,6},{6,4},{8,10},{10,8},{12,14},{14,12},{16,18},{18,... | collective-permute-start | bytes 49160 | tf_op jit(solution)/shard_map/ppermute | solution.py:264
  127.4 7.5 %collective-permute-start.15 = (bf16[64,128]{1,0:T(8,128)(2,1)S(1)}, bf16[64,128]{1,0:T(8,128)(2,1)S(1)}, u32[]{:S(2)}, u32[]{:S(2)}) collective-permute-start(bf16[64,128]{1,0:T(8,128)(2,1)S(1)} %get-tuple-element.77), channel_id=1, source_target_pairs={{2,4},{4,2},{6,8},{8,6},{10,12},{12,10},{14,16},{16,14},{18,20},{2... | collective-permute-start | bytes 49160 | tf_op jit(solution)/shard_map/ppermute | solution.py:264
where the time goes:
time: 138 us
  waiting for transfers between devices  82 us (59%)
  starting transfers between devices  37.8 us (27%)
  Pallas kernels  12.2 us (9%)
  local copies, waits for them, and re-layouts  3.42 us (2%)
  other arithmetic  1.8 us (1%)
    ppermute x16, waiting for transfers between devices, swap(): return lax.ppermute(value, 'tile', pairs)  46.3 us
    ppermute x16, starting transfers between devices, swap(): return lax.ppermute(value, 'tile', pairs)  36.7 us
    ppermute x9, waiting for transfers between devices, across(): return lax.ppermute(v, axis, [(i, i ^ bit) for i in range(n)])  35.7 us
    pallas_call x8, Pallas kernels, call(): pl.pallas_call(body, out_shape=outs, in_specs=specs, out_specs=[pl.BlockS...  12.2 us
  transfers between devices with their start and end apart: 25, of which 20 were waited for; matrix products, arithmetic and copies ran while one was open for 1% of the time, Pallas kernels for 4%

commit v1 on v0

--- a/solution.py
+++ b/solution.py
@@ -5,7 +5,7 @@
 from jax import lax
 from jax.experimental import pallas as pl
 from jax.experimental.pallas import tpu as pltpu
-from jax.sharding import PartitionSpec as P
+from jax.sharding import Mesh, PartitionSpec as P
 
 S = 32
 C = 64
@@ -16,6 +16,13 @@
 FULL = INNER + 2 * BASE
 WIDE = FULL + 2 * BASE
 SLOT = 128
+PACKED = 12 * C
+TILE = ("x", "y", "z", "core")
+MEMBER = ("member",)
+NEAR = ("z", "core")
+FAR = ("x", "y", "member")
+CODES = S * S + 256
+LOAD = CODES + SLOT
 CORNER = 64
 BF = jnp.bfloat16
 F32 = jnp.float32
@@ -23,7 +30,7 @@
 
 def call(body, outs, scratch, args, flops, name):
     specs = [
-        pl.BlockSpec(memory_space=pltpu.SMEM if a.dtype == jnp.int32 else pltpu.VMEM) for a in args
+        pl.BlockSpec(memory_space=pltpu.SMEM if a.shape == (1, 4) else pltpu.VMEM) for a in args
     ]
     moved = sum(math.prod(o.shape) * o.dtype.itemsize for o in list(outs) + list(args))
     return pl.pallas_call(
@@ -64,11 +71,10 @@
 
 def source_row(facts, group, width, pitch, base):
     lane, depth, along, part, kind, j = lanes_of()
-    side, code = facts[0, group], facts[0, 4 + group]
+    side, code = facts[group : group + 1, :], facts[4 + group : 5 + group, :]
     edge = (side - code + 4) & 3
     along = jnp.where((code & 1) == 1, 31 - along, along)
-    level = jnp.where(edge >= 2, depth, depth)
-    near = jnp.where((edge == 1) | (edge == 2), 31 - level, level)
+    near = jnp.where((edge == 1) | (edge == 2), 31 - depth, depth)
     rows = (edge & 1) == 0
     y = jnp.where(rows, near, along)
     x = jnp.where(rows, along, near)
@@ -86,7 +92,7 @@
 
 def rim_row(facts, group, width):
     lane, depth, along, part, kind, j = lanes_of()
-    side, second = facts[0, group], facts[0, 2]
+    side, second = facts[group : group + 1, :], facts[2:3, :]
     beyond = jnp.where((side == 0) | (side == 3), -1 - depth, S + depth)
     rows = (side & 1) == 0
     y = jnp.where(rows, beyond, along)
@@ -158,17 +164,43 @@
     return jnp.where(place == 72 * (m >> 4) + 2 * (m & 15), 1.0, 0.0).astype(BF)
 
 
-def send_inputs_body(facts, x, *slots):
+def load_body(codes, x, cot, load):
+    load[:, : S * S] = x[...]
+    load[:, S * S : CODES] = cot[...]
+    row = lax.broadcasted_iota(jnp.int32, (C, SLOT), 0)
+    value = jnp.where(row == 0, codes[0, 0], jnp.where(row == 1, codes[0, 1], jnp.where(row == 2, codes[0, 2], codes[0, 3])))
+    load[:, CODES:] = value.astype(F32).astype(BF)
+
+
+def send_inputs_body(load, facts, *slots):
+    codes = load[:16, CODES:].astype(F32).astype(jnp.int32)
+    row, column = lax.axis_index("core"), lax.axis_index("z") & 1
+    sides = [2 - 2 * row, 2 * row, 1 + 2 * column, 3 - 2 * column]
+    for g, side in enumerate(sides):
+        code = jnp.where(side == 2, codes[2:3, :], codes[3:4, :])
+        code = jnp.where(side == 1, codes[1:2, :], code)
+        code = jnp.where(side == 0, codes[0:1, :], code)
+        facts[g : g + 1, :] = jnp.full((1, SLOT), side, jnp.int32)
+        facts[4 + g : 5 + g, :] = code
     hot = pick(sources(facts, 1, S, 0), 0, S * S)
-    write_slots(slots, mm(x[...], hot))
-
-
-def prepare_body(x, cot, down_t, spread, upstream, grad_two, wide, col):
+    write_slots(slots, mm(load[:, : S * S], hot))
+
+
+def transpose_taps(src, dst, count):
+    for n in range(count):
+        block = src[:, C * n : C * (n + 1)].astype(F32)
+        dst[:, C * n : C * (n + 1)] = jnp.transpose(block).astype(BF)
+
+
+def prepare_body(load, down, one, two, spread, upstream, grad_two, one_t, two_t, wide, col, down_t):
+    transpose_taps(one, one_t, 9)
+    transpose_taps(two, two_t, 9)
+    transpose_taps(down, down_t, 4)
     spread[...] = jnp.zeros_like(spread)
     for y in range(S):
-        spread[:, BASE + PITCH * y : BASE + PITCH * y + S] = x[:, S * y : S * y + S]
-    wide[...] = jnp.zeros_like(wide)
-    wide[:, BASE : BASE + INNER] = nt(cot[...], up_matrix()).astype(BF)
+        spread[:, BASE + PITCH * y : BASE + PITCH * y + S] = load[:, S * y : S * y + S]
+    wide[...] = jnp.zeros_like(wide)
+    wide[:, BASE : BASE + INNER] = nt(load[:, S * S : CODES], up_matrix()).astype(BF)
     for n in range(4):
         lo = BASE - (n // 2) * PITCH - n % 2
         col[C * n : C * (n + 1), :] = wide[:, lo : lo + INNER]
@@ -227,7 +259,7 @@
     encoded[...] = mm(mm(down[...], four).astype(BF), up_matrix()).astype(BF)
 
 
-def third_body(scale, facts, grad_mid, r0, r1, r2, r3, slope, ext, delta, grad, wide, col):
+def third_body(scale, facts, grad_mid, r0, r1, r2, r3, slope, ext, sum_two, sum_down, delta, packed, wide, col):
     back = nt(read_slots((r0, r1, r2, r3)), pick(sources(facts, 2), BASE, INNER))
     back = (grad_mid[...] + back) * slope[...]
     back = jnp.where(columns_mask(), back, 0.0).astype(BF)
@@ -235,7 +267,18 @@
     wide[...] = jnp.zeros_like(wide)
     wide[:, BASE : BASE + FULL] = ext[...]
     gather_taps(col, wide, 1, 1, BASE, INNER)
-    grad[...] = nt(back, col[...]) * scale
+    sums = [nt(back, col[...]) * scale, sum_two[...], sum_down[...], jnp.zeros((C, SLOT), F32)]
+    sums = jnp.concatenate(sums, axis=1)
+    for n in range(PACKED // C):
+        packed[C * n : C * (n + 1), :] = sums[:, SLOT * n : SLOT * (n + 1)].astype(BF)
+
+
+def unpack_body(packed, one, two, down):
+    sums = [packed[C * n : C * (n + 1), :].astype(F32) for n in range(PACKED // C - 1)]
+    sums = jnp.concatenate(sums, axis=1)
+    one[...] = sums[:, : 9 * C]
+    two[...] = sums[:, 9 * C : 18 * C]
+    down[...] = sums[:, 18 * C :]
 
 
 def fourth_body(facts, delta, wt, grad, m0, m1, m2, m3, wide, col_full):
@@ -247,21 +290,33 @@
     write_slots((m0, m1, m2, m3), mm(pad.astype(BF), pick(rims(facts, 1), 0, FULL)))
 
 
-def last_body(facts, grad, r0, r1, r2, r3, o):
+def last_body(facts, grad, r0, r1, r2, r3, encoded, o):
+    o[:, S * S :] = encoded[...]
     back = nt(read_slots((r0, r1, r2, r3)), pick(sources(facts, 1), BASE, INNER))
     back = (grad[...] + back).astype(BF)
     for y in range(S):
         o[:, S * y : S * y + S] = back[:, PITCH * y : PITCH * y + S]
 
 
+def home(t):
+    row, column = t // ROW_TILES, t % ROW_TILES
+    x = row // 4
+    y = (row // 2 % 2) ^ (x % 2)
+    return ((x * 2 + y) * 8 + column) * 2 + row % 2
+
+
+def move(value, pairs):
+    return lax.ppermute(value, TILE, pairs)
+
+
 def swap(value, step, parity):
-    count = lax.axis_size("tile")
+    count = lax.axis_size(TILE)
     pairs = []
     for t in range(count):
         if (t // step) % 2 == parity:
-            u = (t + step) % count
-            pairs += [(t, u), (u, t)]
-    return lax.ppermute(value, "tile", pairs)
+            here, there = home(t), home((t + step) % count)
+            pairs += [(here, there), (there, here)]
+    return move(value, pairs)
 
 
 def lane():
@@ -286,53 +341,43 @@
     return r0, r1, r2, r3
 
 
-def add_up(values):
-    count = lax.axis_size("tile")
-    core = lax.axis_index("tile") % 2
-    half = values.shape[0] // 2
-    low, high = values[:half], values[half:]
-
-    def across(v, axis, bit, n):
-        return lax.ppermute(v, axis, [(i, i ^ bit) for i in range(n)])
-
-    got = across(jnp.where(core == 0, high, low), "tile", 1, count)
-    part = jnp.where(core == 0, low, high) + got
-    for axis, bit in [("member", 1)] + [("tile", 2**k) for k in range(4, 7)] + [("tile", 2**k) for k in range(1, 4)]:
-        part = part.astype(BF)
-        got = across(part, axis, bit, lax.axis_size(axis))
-        part = part.astype(F32) + got.astype(F32)
-    other = across(part, "tile", 1, count)
-    first, then = jnp.where(core == 0, part, other), jnp.where(core == 0, other, part)
-    return jnp.concatenate([first, then], axis=0)
+def add_up(packed):
+    share = PACKED // lax.axis_size(NEAR)
+
+    def trade(v, axes):
+        return lax.all_to_all(v, axes, 0, 0, tiled=True)
+
+    def total(v):
+        return jnp.sum(v.astype(F32), axis=0).astype(BF)
+
+    def everyone(v, axes):
+        return jnp.broadcast_to(v[None], (lax.axis_size(axes),) + v.shape)
+
+    part = total(trade(packed.reshape(-1, share, SLOT), NEAR))
+    part = total(trade(everyone(part, FAR), FAR))
+    return trade(everyone(part, NEAR), NEAR).reshape(PACKED, SLOT)
 
 
 def per_device(inputs, cotangent, seam_codes, conv_one, conv_two, down_weight):
     x, cot = inputs[0, 0], cotangent[0, 0]
-    tile = lax.axis_index("tile").astype(jnp.int32)
-    down_row = (tile // ROW_TILES) % 2 == 0
-    even = tile % 2 == 0
-    sides = jnp.stack(
-        [jnp.where(down_row, 2, 0), jnp.where(down_row, 0, 2), jnp.where(even, 1, 3), jnp.where(even, 3, 1)]
-    ).astype(jnp.int32)
-    facts = jnp.concatenate([sides, seam_codes[0][sides]]).reshape(1, 8)
-    count = lax.axis_size("tile") * lax.axis_size("member")
-    scale = 1.0 / math.sqrt(count * S * S)
-
-    def flip(w, n):
-        return jnp.transpose(w.reshape(C, n, C), (2, 1, 0)).reshape(C, n * C)
-
-    one_t, two_t, down_t = flip(conv_one, 9), flip(conv_two, 9), flip(down_weight, 4)
+    assert lax.axis_size(TILE) == 128
+    scale = 1.0 / math.sqrt(lax.axis_size(TILE + MEMBER) * S * S)
+
     slots = [out((C, SLOT), BF)] * 4
     wide, col = pltpu.VMEM((C, WIDE), BF), pltpu.VMEM((9 * C, INNER), BF)
     col_full = pltpu.VMEM((9 * C, FULL), BF)
     dense = 2 * C * 9 * C * INNER
 
-    sent = call(send_inputs_body, slots, [], [facts, x], 2 * C * 1024 * 512, "send_inputs")
-    spread, upstream, grad_two = call(
+    (load,) = call(load_body, [out((C, LOAD), BF)], [], [seam_codes, x, cot], C * LOAD, "load")
+    load = move(load, [(t, home(t)) for t in range(128)])
+    facts, *sent = call(
+        send_inputs_body, [out((8, SLOT), jnp.int32)] + slots, [], [load], 2 * C * 1024 * 512, "send_inputs"
+    )
+    spread, upstream, grad_two, one_t, two_t = call(
         prepare_body,
-        [out((C, FULL), BF), out((C, INNER), BF), out((C, INNER), F32)],
-        [wide, pltpu.VMEM((4 * C, INNER), BF)],
-        [x, cot, down_t],
+        [out((C, FULL), BF), out((C, INNER), BF), out((C, INNER), F32)] + [out((C, 9 * C), BF)] * 2,
+        [wide, pltpu.VMEM((4 * C, INNER), BF), pltpu.VMEM((C, 4 * C), BF)],
+        [load, down_weight, conv_one, conv_two],
         dense,
         "prepare",
     )
@@ -363,11 +408,11 @@
         2 * dense,
         "second_sums",
     )
-    delta_one, sum_one = call(
+    delta_one, packed = call(
         lambda *refs: third_body(scale, *refs),
-        [out((C, INNER), BF), out((C, 9 * C), F32)],
+        [out((C, INNER), BF), out((PACKED, SLOT), BF)],
         [wide, col],
-        [facts, grad_mid, *got, slope, ext],
+        [facts, grad_mid, *got, slope, ext, sum_two, sum_down],
         2 * dense,
         "third",
     )
@@ -380,25 +425,32 @@
         "fourth",
     )
     got = exchange_back(sent)
-    (input_grad,) = call(
-        last_body, [out((C, S * S), BF)], [], [facts, grad_in, *got], dense, "last"
-    )
-    total = add_up(jnp.concatenate([sum_one, sum_two, sum_down], axis=1))
+    (results,) = call(
+        last_body, [out((C, CODES), BF)], [], [facts, grad_in, *got, encoded], dense, "last"
+    )
+    results = move(results, [(home(t), t) for t in range(128)])
+    sums = call(
+        unpack_body,
+        [out((C, 9 * C), F32), out((C, 9 * C), F32), out((C, 4 * C), F32)],
+        [],
+        [add_up(packed)],
+        C * C,
+        "unpack",
+    )
     return (
-        encoded.reshape(1, 1, C, 256),
-        input_grad.reshape(1, 1, C, S * S),
-        total[:, : 9 * C],
-        total[:, 9 * C : 18 * C],
-        total[:, 18 * C :],
+        results[:, S * S :].reshape(1, 1, C, 256),
+        results[:, : S * S].reshape(1, 1, C, S * S),
+        *sums,
     )
 
 
 def solution(mesh):
-    split = P("member", "tile", None, None)
+    axes = Mesh(mesh.devices.reshape(4, 2, 8, 2, 2), TILE + MEMBER)
+    split = P(MEMBER, TILE, None, None)
     return jax.shard_map(
         per_device,
-        mesh=mesh,
-        in_specs=(split, split, P("tile", None), P(), P(), P()),
+        mesh=axes,
+        in_specs=(split, split, P(TILE, None), P(), P(), P()),
         out_specs=(split, split, P(), P(), P()),
         check_vma=False,
     )

time: 138 us -> 105 us (0.76)
  the two profiles are of different devices: /device:TPU:16 before, /device:TPU:1 now
where the time goes in v1:
time: 105 us; the launch traced here: 104 us
  starting transfers between devices  51 us (49%)
  waiting for transfers between devices  36.4 us (35%)
  Pallas kernels  10.7 us (10%)
  local copies, waits for them, and re-layouts  4.99 us (5%)
    ppermute x18, starting transfers between devices, move(): return lax.ppermute(value, TILE, pairs)  34.7 us
    ppermute x18, waiting for transfers between devices, move(): return lax.ppermute(value, TILE, pairs)  21.7 us
    all_to_all x3, starting transfers between devices, trade(): return lax.all_to_all(v, axes, 0, 0, tiled=True)  16.3 us
    all_to_all x3, waiting for transfers between devices, trade(): return lax.all_to_all(v, axes, 0, 0, tiled=True)  14.6 us
    pallas_call x10, Pallas kernels, call(): pl.pallas_call(body, out_shape=outs, in_specs=specs, out_specs=[pl.BlockS...  10.7 us
    unnamed x12, local copies, waits for them, and re-layouts  2.32 us
  transfers between devices with their start and end apart: 21, of which 14 were waited for; matrix products, arithmetic and copies ran while one was open for 3% of the time, Pallas kernels for 4%

profile of v1, /device:TPU:1, one launch (start us, length us, event | category | flops | bytes accessed | tf_op | source)
XLA Modules:
  0.0 104.1 jit_solution(6691605058642442335)
XLA Ops:
  1.3 0.9 copy-done.1
  3.5 4.9 %collective-permute-start = (bf16[64,1408]{1,0:T(8,128)(2,1)S(1)}, bf16[64,1408]{1,0:T(8,128)(2,1)S(1)}, u32[]{:S(2)}, u32[]{:S(2)}) collective-permute-start(bf16[64,1408]{1,0:T(8,128)(2,1)S(1)} %load.1), channel_id=1, source_target_pairs={{0,0},{2,4},{4,8},{6,12},{8,16},{10,20},{12,24},{14,28},{16,2},{18... | collective-permute-start | bytes 540680 | tf_op jit(solution)/shard_map/ppermute | solution.py:309
  8.5 8.4 %collective-permute-done.load = bf16[64,1408]{1,0:T(8,128)(2,1)S(1)} collective-permute-done((bf16[64,1408]{1,0:T(8,128)(2,1)S(1)}, bf16[64,1408]{1,0:T(8,128)(2,1)S(1)}, u32[]{:S(2)}, u32[]{:S(2)}) %collective-permute-start) | collective-permute-done | bytes 180256 | tf_op jit(solution)/shard_map/ppermute | solution.py:309
  17.2 2.4 %collective-permute-start.1 = (bf16[64,128]{1,0:T(8,128)(2,1)S(1)}, bf16[64,128]{1,0:T(8,128)(2,1)S(1)}, u32[]{:S(2)}, u32[]{:S(2)}) collective-permute-start(bf16[64,128]{1,0:T(8,128)(2,1)S(1)} %get-tuple-element.46), channel_id=1, source_target_pairs={{0,4},{4,0},{8,12},{12,8},{16,20},{20,16},{24,28},{28,24},{2,6},{6... | collective-permute-start | bytes 49160 | tf_op jit(solution)/shard_map/ppermute | solution.py:309
  19.7 6.5 %collective-permute-start.2 = (bf16[64,128]{1,0:T(8,128)(2,1)S(1)}, bf16[64,128]{1,0:T(8,128)(2,1)S(1)}, u32[]{:S(2)}, u32[]{:S(2)}) collective-permute-start(bf16[64,128]{1,0:T(8,128)(2,1)S(1)} %get-tuple-element.47), channel_id=1, source_target_pairs={{4,8},{8,4},{12,16},{16,12},{20,24},{24,20},{28,2},{2,28},{6,10},{... | collective-permute-start | bytes 49160 | tf_op jit(solution)/shard_map/ppermute | solution.py:309
  26.1 1.4 %collective-permute-done.2.r3 = bf16[64,128]{1,0:T(8,128)(2,1)S(1)} collective-permute-done((bf16[64,128]{1,0:T(8,128)(2,1)S(1)}, bf16[64,128]{1,0:T(8,128)(2,1)S(1)}, u32[]{:S(2)}, u32[]{:S(2)}) %collective-permute-start.2) | collective-permute-done | bytes 16416 | tf_op jit(solution)/shard_map/ppermute | solution.py:309
  27.7 3.8 %collective-permute-start.3 = (bf16[64,128]{1,0:T(8,128)(2,1)S(1)}, bf16[64,128]{1,0:T(8,128)(2,1)S(1)}, u32[]{:S(2)}, u32[]{:S(2)}) collective-permute-start(bf16[64,128]{1,0:T(8,128)(2,1)S(1)} %get-tuple-element.84), channel_id=1, source_target_pairs={{0,2},{2,0},{4,6},{6,4},{8,10},{10,8},{12,14},{14,12},{16,18},{18,... | collective-permute-start | bytes 49160 | tf_op jit(solution)/shard_map/ppermute | solution.py:309
  31.4 1.6 %prepare.1 = (bf16[64,1408]{1,0:T(8,128)(2,1)S(1)}, bf16[64,1152]{1,0:T(8,128)(2,1)S(1)}, f32[64,1152]{1,0:T(8,128)S(1)}, bf16[64,576]{1,0:T(8,128)(2,1)S(1)}, bf16[64,576]{1,0:T(8,128)(2,1)S(1)}) custom-call(bf16[64,1408]{1,0:T(8,128)(2,1)S(1)} %collective-permute-done.load, bf16[64,256]{1,0:T(8,128)(2,1)S(1)} %copy-done, bf16[64,576]{1,0:T(8,128)(2,1)S(1)} %copy-done.2, ...), custom_call_target="tpu_custom_call" | custom-call | flops 84934656 | bytes 1130496 | tf_op jit(solution)/shard_map/prepare/pallas_call | solution.py:36
  33.1 1.4 %first.1 = (bf16[64,1408]{1,0:T(8,128)(2,1)S(1)}, bf16[64,1152]{1,0:T(8,128)(2,1)S(1)}, f32[64,1152]{1,0:T(8,128)S(1)}, bf16[64,128]{1,0:T(8,128)(2,1)S(1)}, bf1...) custom-call(s32[8,128]{1,0:T(8,128)S(1)} %get-tuple-element.43.facts.refs_0_, ...), custom_call_target="tpu_custom_call" | custom-call | flops 169869312 | bytes 1011712 | tf_op jit(solution)/shard_map/first/pallas_call | solution.py:36
  34.5 2.0 %collective-permute-start.6 = (bf16[64,128]{1,0:T(8,128)(2,1)S(1)}, bf16[64,128]{1,0:T(8,128)(2,1)S(1)}, u32[]{:S(2)}, u32[]{:S(2)}) collective-permute-start(bf16[64,128]{1,0:T(8,128)(2,1)S(1)} %get-tuple-element.52), channel_id=1, source_target_pairs={{4,8},{8,4},{12,16},{16,12},{20,24},{24,20},{28,2},{2,28},{6,10},{... | collective-permute-start | bytes 49160 | tf_op jit(solution)/shard_map/ppermute | solution.py:309
  37.1 1.9 %collective-permute-done.6.r3 = bf16[64,128]{1,0:T(8,128)(2,1)S(1)} collective-permute-done((bf16[64,128]{1,0:T(8,128)(2,1)S(1)}, bf16[64,128]{1,0:T(8,128)(2,1)S(1)}, u32[]{:S(2)}, u32[]{:S(2)}) %collective-permute-start.6) | collective-permute-done | bytes 16416 | tf_op jit(solution)/shard_map/ppermute | solution.py:309
  39.1 2.7 %collective-permute-start.7 = (bf16[64,128]{1,0:T(8,128)(2,1)S(1)}, bf16[64,128]{1,0:T(8,128)(2,1)S(1)}, u32[]{:S(2)}, u32[]{:S(2)}) collective-permute-start(bf16[64,128]{1,0:T(8,128)(2,1)S(1)} %get-tuple-element.82), channel_id=1, source_target_pairs={{0,2},{2,0},{4,6},{6,4},{8,10},{10,8},{12,14},{14,12},{16,18},{18,... | collective-permute-start | bytes 49160 | tf_op jit(solution)/shard_map/ppermute | solution.py:309
  42.6 1.9 %second.1 = (bf16[64,1408]{1,0:T(8,128)(2,1)S(1)}, bf16[64,1152]{1,0:T(8,128)(2,1)S(1)}, bf16[64,1152]{1,0:T(8,128)(2,1)S(1)}, f32[64,1152]{1,0:T(8,128)S(1)}, b...) custom-call(s32[8,128]{1,0:T(8,128)S(1)} %get-tuple-element.43.facts, ...), custom_call_target="tpu_custom_call" | custom-call | flops 254803968 | bytes 1495040 | tf_op jit(solution)/shard_map/second/pallas_call | solution.py:36
  44.6 3.0 %collective-permute-start.9 = (bf16[64,128]{1,0:T(8,128)(2,1)S(1)}, bf16[64,128]{1,0:T(8,128)(2,1)S(1)}, u32[]{:S(2)}, u32[]{:S(2)}) collective-permute-start(bf16[64,128]{1,0:T(8,128)(2,1)S(1)} %get-tuple-element.57), channel_id=1, source_target_pairs={{0,2},{2,0},{4,6},{6,4},{8,10},{10,8},{12,14},{14,12},{16,18},{18,... | collective-permute-start | bytes 49160 | tf_op jit(solution)/shard_map/ppermute | solution.py:309
  47.6 0.8 collective-permute-done.9.refs_2_
  48.4 2.3 %collective-permute-done.10.refs_3_ = bf16[64,128]{1,0:T(8,128)(2,1)S(1)} collective-permute-done((bf16[64,128]{1,0:T(8,128)(2,1)S(1)}, bf16[64,128]{1,0:T(8,128)(2,1)S(1)}, u32[]{:S(2)}, u32[]{:S(2)}) %collective-permute-start.10) | collective-permute-done | bytes 16416 | tf_op jit(solution)/shard_map/ppermute | solution.py:309
  50.8 1.5 %collective-permute-start.12 = (bf16[64,128]{1,0:T(8,128)(2,1)S(1)}, bf16[64,128]{1,0:T(8,128)(2,1)S(1)}, u32[]{:S(2)}, u32[]{:S(2)}) collective-permute-start(bf16[64,128]{1,0:T(8,128)(2,1)S(1)} %get-tuple-element.87), channel_id=1, source_target_pairs={{4,8},{8,4},{12,16},{16,12},{20,24},{24,20},{28,2},{2,28},{6,10},{... | collective-permute-start | bytes 49160 | tf_op jit(solution)/shard_map/ppermute | solution.py:309
  52.3 1.0 second_sums.1
  53.3 1.9 %collective-permute-done.12.refs_5_ = bf16[64,128]{1,0:T(8,128)(2,1)S(1)} collective-permute-done((bf16[64,128]{1,0:T(8,128)(2,1)S(1)}, bf16[64,128]{1,0:T(8,128)(2,1)S(1)}, u32[]{:S(2)}, u32[]{:S(2)}) %collective-permute-start.12) | collective-permute-done | bytes 16416 | tf_op jit(solution)/shard_map/ppermute | solution.py:309
  55.2 1.6 %third.1 = (bf16[64,1152]{1,0:T(8,128)(2,1)S(1)}, bf16[768,128]{1,0:T(8,128)(2,1)}) custom-call(s32[8,128]{1,0:T(8,128)S(1)} %get-tuple-element.43.facts.refs_0_, f32[64,1152]{1,0:T(8,128)S(1)} %get-tuple-element.56.refs_1_, bf16[64,128]{1,0:T(8,128)(2,1)S(1)} %collective-permute-done.9.refs_2_, bf16[64,128]{1,0:T(8,128)(2,1)S(1)} %collective-permute-done.10.refs_3_, ...), custom_call_target="tpu_custom_call" | custom-call | flops 169869312 | bytes 1396736 | tf_op jit(solution)/shard_map/third/pallas_call | solution.py:36
  56.9 6.8 %all-to-all-start = ((bf16[16,48,128]{2,1,0:T(8,128)(2,1)}), bf16[16,48,128]{2,1,0:T(8,128)(2,1)S(1)}, u32[]{:S(2)}, u32[]{:S(2)}) async-start(bf16[16,48,128]{2,1,0:T(8,128)(2,1)} %bitcast.4), calls=%async_computation | async-start | bytes 393216 | tf_op jit(solution)/shard_map/all_to_all | solution.py:348
  63.7 0.9 fourth.1
  64.9 1.0 collective-permute-done.13.r0
  65.9 2.5 %collective-permute-done.14.r1 = bf16[64,128]{1,0:T(8,128)(2,1)S(1)} collective-permute-done((bf16[64,128]{1,0:T(8,128)(2,1)S(1)}, bf16[64,128]{1,0:T(8,128)(2,1)S(1)}, u32[]{:S(2)}, u32[]{:S(2)}) %collective-permute-start.14) | collective-permute-done | bytes 16416 | tf_op jit(solution)/shard_map/ppermute | solution.py:309
  68.4 3.9 %collective-permute-start.16 = (bf16[64,128]{1,0:T(8,128)(2,1)S(1)}, bf16[64,128]{1,0:T(8,128)(2,1)S(1)}, u32[]{:S(2)}, u32[]{:S(2)}) collective-permute-start(bf16[64,128]{1,0:T(8,128)(2,1)S(1)} %get-tuple-element.85), channel_id=1, source_target_pairs={{4,8},{8,4},{12,16},{16,12},{20,24},{24,20},{28,2},{2,28},{6,10},{... | collective-permute-start | bytes 49160 | tf_op jit(solution)/shard_map/ppermute | solution.py:309
  72.2 1.8 %all-to-all-done = bf16[16,48,128]{2,1,0:T(8,128)(2,1)S(1)} async-done(((bf16[16,48,128]{2,1,0:T(8,128)(2,1)}), bf16[16,48,128]{2,1,0:T(8,128)(2,1)S(1)}, u32[]{:S(2)}, u32[]{:S(2)}) %all-to-all-start) | async-done | bytes 196640 | tf_op jit(solution)/shard_map/all_to_all | solution.py:348
  74.8 5.0 %all-to-all-start.1 = ((bf16[16,48,128]{2,1,0:T(8,128)(2,1)}), bf16[16,48,128]{2,1,0:T(8,128)(2,1)S(1)}, u32[]{:S(2)}, u32[]{:S(2)}) async-start(bf16[16,48,128]{2,1,0:T(8,128)(2,1)} %broadcast_in_dim.4), calls=%async_computation.1 | async-start | bytes 393216 | tf_op jit(solution)/shard_map/all_to_all | solution.py:348
  80.5 3.5 %collective-permute-start.17 = (bf16[64,1280]{1,0:T(8,128)(2,1)S(1)}, bf16[64,1280]{1,0:T(8,128)(2,1)S(1)}, u32[]{:S(2)}, u32[]{:S(2)}) collective-permute-start(bf16[64,1280]{1,0:T(8,128)(2,1)S(1)} %last.1), channel_id=1, source_target_pairs={{0,0},{4,2},{8,4},{12,6},{16,8},{20,10},{24,12},{28,14},{2,16},{6,... | collective-permute-start | bytes 491528 | tf_op jit(solution)/shard_map/ppermute | solution.py:309
  84.0 3.7 %all-to-all-done.1 = bf16[16,48,128]{2,1,0:T(8,128)(2,1)S(1)} async-done(((bf16[16,48,128]{2,1,0:T(8,128)(2,1)}), bf16[16,48,128]{2,1,0:T(8,128)(2,1)S(1)}, u32[]{:S(2)}, u32[]{:S(2)}) %all-to-all-start.1) | async-done | bytes 196640 | tf_op jit(solution)/shard_map/all_to_all | solution.py:348
  88.4 4.5 %all-to-all-start.2 = ((bf16[16,48,128]{2,1,0:T(8,128)(2,1)}), bf16[16,48,128]{2,1,0:T(8,128)(2,1)S(1)}, u32[]{:S(2)}, u32[]{:S(2)}) async-start(bf16[16,48,128]{2,1,0:T(8,128)(2,1)} %broadcast_in_dim.5), calls=%async_computation.2 | async-start | bytes 393216 | tf_op jit(solution)/shard_map/all_to_all | solution.py:348
  94.2 9.1 %all-to-all-done.2 = bf16[16,48,128]{2,1,0:T(8,128)(2,1)S(1)} async-done(((bf16[16,48,128]{2,1,0:T(8,128)(2,1)}), bf16[16,48,128]{2,1,0:T(8,128)(2,1)S(1)}, u32[]{:S(2)}, u32[]{:S(2)}) %all-to-all-start.2) | async-done | bytes 196640 | tf_op jit(solution)/shard_map/all_to_all | solution.py:348
  103.3 0.8 unpack.1
  (43 shorter events, 7.8 us)
Async XLA Ops:
  0.6 0.7 copy-start.5
  1.3 0.9 copy-start.1
  2.2 0.8 copy-start.4
  3.5 13.4 %collective-permute-start = (bf16[64,1408]{1,0:T(8,128)(2,1)S(1)}, bf16[64,1408]{1,0:T(8,128)(2,1)S(1)}, u32[]{:S(2)}, u32[]{:S(2)}) collective-permute-start(bf16[64,1408]{1,0:T(8,128)(2,1)S(1)} %load.1), channel_id=1, source_target_pairs={{0,0},{2,4},{4,8},{6,12},{8,16},{10,20},{12,24},{14,28},{16,2},{18... | collective-permute-start | bytes 540680 | tf_op jit(solution)/shard_map/ppermute | solution.py:309
  16.9 14.5 %copy-start.3 = (bf16[64,576]{1,0:T(8,128)(2,1)S(1)}, bf16[64,576]{1,0:T(8,128)(2,1)}, u32[]{:S(2)}) copy-start(bf16[64,576]{1,0:T(8,128)(2,1)} %w.3) | copy-start | bytes 221188
  17.2 14.2 %copy-start.2 = (bf16[64,576]{1,0:T(8,128)(2,1)S(1)}, bf16[64,576]{1,0:T(8,128)(2,1)}, u32[]{:S(2)}) copy-start(bf16[64,576]{1,0:T(8,128)(2,1)} %w.2) | copy-start | bytes 221188
  17.2 8.9 %collective-permute-start.1 = (bf16[64,128]{1,0:T(8,128)(2,1)S(1)}, bf16[64,128]{1,0:T(8,128)(2,1)S(1)}, u32[]{:S(2)}, u32[]{:S(2)}) collective-permute-start(bf16[64,128]{1,0:T(8,128)(2,1)S(1)} %get-tuple-element.46), channel_id=1, source_target_pairs={{0,4},{4,0},{8,12},{12,8},{16,20},{20,16},{24,28},{28,24},{2,6},{6... | collective-permute-start | bytes 49160 | tf_op jit(solution)/shard_map/ppermute | solution.py:309
  19.7 7.9 %collective-permute-start.2 = (bf16[64,128]{1,0:T(8,128)(2,1)S(1)}, bf16[64,128]{1,0:T(8,128)(2,1)S(1)}, u32[]{:S(2)}, u32[]{:S(2)}) collective-permute-start(bf16[64,128]{1,0:T(8,128)(2,1)S(1)} %get-tuple-element.47), channel_id=1, source_target_pairs={{4,8},{8,4},{12,16},{16,12},{20,24},{24,20},{28,2},{2,28},{6,10},{... | collective-permute-start | bytes 49160 | tf_op jit(solution)/shard_map/ppermute | solution.py:309
  27.5 3.9 %copy-start = (bf16[64,256]{1,0:T(8,128)(2,1)S(1)}, bf16[64,256]{1,0:T(8,128)(2,1)}, u32[]{:S(2)}) copy-start(bf16[64,256]{1,0:T(8,128)(2,1)} %refs_4_.1) | copy-start | bytes 98308
  27.6 5.5 %collective-permute-start.4 = (bf16[64,128]{1,0:T(8,128)(2,1)S(1)}, bf16[64,128]{1,0:T(8,128)(2,1)S(1)}, u32[]{:S(2)}, u32[]{:S(2)}) collective-permute-start(bf16[64,128]{1,0:T(8,128)(2,1)S(1)} %get-tuple-element.83), channel_id=1, source_target_pairs={{2,32},{32,2},{6,36},{36,6},{10,40},{40,10},{14,44},{44,14},{18,48... | collective-permute-start | bytes 49160 | tf_op jit(solution)/shard_map/ppermute | solution.py:309
  27.7 5.4 %collective-permute-start.3 = (bf16[64,128]{1,0:T(8,128)(2,1)S(1)}, bf16[64,128]{1,0:T(8,128)(2,1)S(1)}, u32[]{:S(2)}, u32[]{:S(2)}) collective-permute-start(bf16[64,128]{1,0:T(8,128)(2,1)S(1)} %get-tuple-element.84), channel_id=1, source_target_pairs={{0,2},{2,0},{4,6},{6,4},{8,10},{10,8},{12,14},{14,12},{16,18},{18,... | collective-permute-start | bytes 49160 | tf_op jit(solution)/shard_map/ppermute | solution.py:309
  34.4 2.7 %collective-permute-start.5 = (bf16[64,128]{1,0:T(8,128)(2,1)S(1)}, bf16[64,128]{1,0:T(8,128)(2,1)S(1)}, u32[]{:S(2)}, u32[]{:S(2)}) collective-permute-start(bf16[64,128]{1,0:T(8,128)(2,1)S(1)} %get-tuple-element.51), channel_id=1, source_target_pairs={{0,4},{4,0},{8,12},{12,8},{16,20},{20,16},{24,28},{28,24},{2,6},{6... | collective-permute-start | bytes 49160 | tf_op jit(solution)/shard_map/ppermute | solution.py:309
  34.5 4.5 %collective-permute-start.6 = (bf16[64,128]{1,0:T(8,128)(2,1)S(1)}, bf16[64,128]{1,0:T(8,128)(2,1)S(1)}, u32[]{:S(2)}, u32[]{:S(2)}) collective-permute-start(bf16[64,128]{1,0:T(8,128)(2,1)S(1)} %get-tuple-element.52), channel_id=1, source_target_pairs={{4,8},{8,4},{12,16},{16,12},{20,24},{24,20},{28,2},{2,28},{6,10},{... | collective-permute-start | bytes 49160 | tf_op jit(solution)/shard_map/ppermute | solution.py:309
  39.0 3.3 %collective-permute-start.8 = (bf16[64,128]{1,0:T(8,128)(2,1)S(1)}, bf16[64,128]{1,0:T(8,128)(2,1)S(1)}, u32[]{:S(2)}, u32[]{:S(2)}) collective-permute-start(bf16[64,128]{1,0:T(8,128)(2,1)S(1)} %get-tuple-element.81), channel_id=1, source_target_pairs={{2,32},{32,2},{6,36},{36,6},{10,40},{40,10},{14,44},{44,14},{18,48... | collective-permute-start | bytes 49160 | tf_op jit(solution)/shard_map/ppermute | solution.py:309
  39.1 3.5 %collective-permute-start.7 = (bf16[64,128]{1,0:T(8,128)(2,1)S(1)}, bf16[64,128]{1,0:T(8,128)(2,1)S(1)}, u32[]{:S(2)}, u32[]{:S(2)}) collective-permute-start(bf16[64,128]{1,0:T(8,128)(2,1)S(1)} %get-tuple-element.82), channel_id=1, source_target_pairs={{0,2},{2,0},{4,6},{6,4},{8,10},{10,8},{12,14},{14,12},{16,18},{18,... | collective-permute-start | bytes 49160 | tf_op jit(solution)/shard_map/ppermute | solution.py:309
  44.6 3.9 %collective-permute-start.9 = (bf16[64,128]{1,0:T(8,128)(2,1)S(1)}, bf16[64,128]{1,0:T(8,128)(2,1)S(1)}, u32[]{:S(2)}, u32[]{:S(2)}) collective-permute-start(bf16[64,128]{1,0:T(8,128)(2,1)S(1)} %get-tuple-element.57), channel_id=1, source_target_pairs={{0,2},{2,0},{4,6},{6,4},{8,10},{10,8},{12,14},{14,12},{16,18},{18,... | collective-permute-start | bytes 49160 | tf_op jit(solution)/shard_map/ppermute | solution.py:309
  47.6 3.2 %collective-permute-start.10 = (bf16[64,128]{1,0:T(8,128)(2,1)S(1)}, bf16[64,128]{1,0:T(8,128)(2,1)S(1)}, u32[]{:S(2)}, u32[]{:S(2)}) collective-permute-start(bf16[64,128]{1,0:T(8,128)(2,1)S(1)} %get-tuple-element.58), channel_id=1, source_target_pairs={{2,32},{32,2},{6,36},{36,6},{10,40},{40,10},{14,44},{44,14},{18,48... | collective-permute-start | bytes 49160 | tf_op jit(solution)/shard_map/ppermute | solution.py:309
  50.8 4.5 %collective-permute-start.12 = (bf16[64,128]{1,0:T(8,128)(2,1)S(1)}, bf16[64,128]{1,0:T(8,128)(2,1)S(1)}, u32[]{:S(2)}, u32[]{:S(2)}) collective-permute-start(bf16[64,128]{1,0:T(8,128)(2,1)S(1)} %get-tuple-element.87), channel_id=1, source_target_pairs={{4,8},{8,4},{12,16},{16,12},{20,24},{24,20},{28,2},{2,28},{6,10},{... | collective-permute-start | bytes 49160 | tf_op jit(solution)/shard_map/ppermute | solution.py:309
  52.3 3.0 %collective-permute-start.11 = (bf16[64,128]{1,0:T(8,128)(2,1)S(1)}, bf16[64,128]{1,0:T(8,128)(2,1)S(1)}, u32[]{:S(2)}, u32[]{:S(2)}) collective-permute-start(bf16[64,128]{1,0:T(8,128)(2,1)S(1)} %get-tuple-element.88), channel_id=1, source_target_pairs={{0,4},{4,0},{8,12},{12,8},{16,20},{20,16},{24,28},{28,24},{2,6},{6... | collective-permute-start | bytes 49160 | tf_op jit(solution)/shard_map/ppermute | solution.py:309
  56.9 17.2 %all-to-all-start = ((bf16[16,48,128]{2,1,0:T(8,128)(2,1)}), bf16[16,48,128]{2,1,0:T(8,128)(2,1)S(1)}, u32[]{:S(2)}, u32[]{:S(2)}) async-start(bf16[16,48,128]{2,1,0:T(8,128)(2,1)} %bitcast.4), calls=%async_computation | async-start | bytes 393216 | tf_op jit(solution)/shard_map/all_to_all | solution.py:348
  64.6 1.3 %collective-permute-start.13 = (bf16[64,128]{1,0:T(8,128)(2,1)S(1)}, bf16[64,128]{1,0:T(8,128)(2,1)S(1)}, u32[]{:S(2)}, u32[]{:S(2)}) collective-permute-start(bf16[64,128]{1,0:T(8,128)(2,1)S(1)} %get-tuple-element.72), channel_id=1, source_target_pairs={{0,2},{2,0},{4,6},{6,4},{8,10},{10,8},{12,14},{14,12},{16,18},{18,... | collective-permute-start | bytes 49160 | tf_op jit(solution)/shard_map/ppermute | solution.py:309
  64.9 3.5 %collective-permute-start.14 = (bf16[64,128]{1,0:T(8,128)(2,1)S(1)}, bf16[64,128]{1,0:T(8,128)(2,1)S(1)}, u32[]{:S(2)}, u32[]{:S(2)}) collective-permute-start(bf16[64,128]{1,0:T(8,128)(2,1)S(1)} %get-tuple-element.73), channel_id=1, source_target_pairs={{2,32},{32,2},{6,36},{36,6},{10,40},{40,10},{14,44},{44,14},{18,48... | collective-permute-start | bytes 49160 | tf_op jit(solution)/shard_map/ppermute | solution.py:309
  68.4 11.4 %collective-permute-start.16 = (bf16[64,128]{1,0:T(8,128)(2,1)S(1)}, bf16[64,128]{1,0:T(8,128)(2,1)S(1)}, u32[]{:S(2)}, u32[]{:S(2)}) collective-permute-start(bf16[64,128]{1,0:T(8,128)(2,1)S(1)} %get-tuple-element.85), channel_id=1, source_target_pairs={{4,8},{8,4},{12,16},{16,12},{20,24},{24,20},{28,2},{2,28},{6,10},{... | collective-permute-start | bytes 49160 | tf_op jit(solution)/shard_map/ppermute | solution.py:309
  72.2 7.6 %collective-permute-start.15 = (bf16[64,128]{1,0:T(8,128)(2,1)S(1)}, bf16[64,128]{1,0:T(8,128)(2,1)S(1)}, u32[]{:S(2)}, u32[]{:S(2)}) collective-permute-start(bf16[64,128]{1,0:T(8,128)(2,1)S(1)} %get-tuple-element.86), channel_id=1, source_target_pairs={{0,4},{4,0},{8,12},{12,8},{16,20},{20,16},{24,28},{28,24},{2,6},{6... | collective-permute-start | bytes 49160 | tf_op jit(solution)/shard_map/ppermute | solution.py:309
  74.8 12.9 %all-to-all-start.1 = ((bf16[16,48,128]{2,1,0:T(8,128)(2,1)}), bf16[16,48,128]{2,1,0:T(8,128)(2,1)S(1)}, u32[]{:S(2)}, u32[]{:S(2)}) async-start(bf16[16,48,128]{2,1,0:T(8,128)(2,1)} %broadcast_in_dim.4), calls=%async_computation.1 | async-start | bytes 393216 | tf_op jit(solution)/shard_map/all_to_all | solution.py:348
  80.5 12.4 %collective-permute-start.17 = (bf16[64,1280]{1,0:T(8,128)(2,1)S(1)}, bf16[64,1280]{1,0:T(8,128)(2,1)S(1)}, u32[]{:S(2)}, u32[]{:S(2)}) collective-permute-start(bf16[64,1280]{1,0:T(8,128)(2,1)S(1)} %last.1), channel_id=1, source_target_pairs={{0,0},{4,2},{8,4},{12,6},{16,8},{20,10},{24,12},{28,14},{2,16},{6,... | collective-permute-start | bytes 491528 | tf_op jit(solution)/shard_map/ppermute | solution.py:309
  88.4 14.9 %all-to-all-start.2 = ((bf16[16,48,128]{2,1,0:T(8,128)(2,1)}), bf16[16,48,128]{2,1,0:T(8,128)(2,1)S(1)}, u32[]{:S(2)}, u32[]{:S(2)}) async-start(bf16[16,48,128]{2,1,0:T(8,128)(2,1)} %broadcast_in_dim.5), calls=%async_computation.2 | async-start | bytes 393216 | tf_op jit(solution)/shard_map/all_to_all | solution.py:348

commit v2 on v1

--- a/solution.py
+++ b/solution.py
@@ -21,17 +21,15 @@
 MEMBER = ("member",)
 NEAR = ("z", "core")
 FAR = ("x", "y", "member")
-CODES = S * S + 256
-LOAD = CODES + SLOT
+LOAD = S * S + 256
+RING = ((1, 0), (0, 0), (0, 1), (1, 1), (2, 1), (3, 1), (3, 0), (2, 0))
 CORNER = 64
 BF = jnp.bfloat16
 F32 = jnp.float32
 
 
-def call(body, outs, scratch, args, flops, name):
-    specs = [
-        pl.BlockSpec(memory_space=pltpu.SMEM if a.shape == (1, 4) else pltpu.VMEM) for a in args
-    ]
+def call(body, outs, scratch, args, flops, name, space=pltpu.VMEM, limit=24):
+    specs = [pl.BlockSpec(memory_space=space) for a in args]
     moved = sum(math.prod(o.shape) * o.dtype.itemsize for o in list(outs) + list(args))
     return pl.pallas_call(
         body,
@@ -39,7 +37,7 @@
         in_specs=specs,
         out_specs=[pl.BlockSpec(memory_space=pltpu.VMEM)] * len(outs),
         scratch_shapes=scratch,
-        compiler_params=pltpu.CompilerParams(vmem_limit_bytes=24 * 2**20),
+        compiler_params=pltpu.CompilerParams(vmem_limit_bytes=limit * 2**20),
         cost_estimate=pl.CostEstimate(flops=flops, bytes_accessed=moved, transcendentals=0),
         name=name,
     )(*args)
@@ -126,7 +124,7 @@
 
 
 def write_slots(refs, messages):
-    for g, ref in enumerate(refs):
+    for g, ref in zip((3, 2, 1, 0), refs, strict=True):
         ref[...] = messages[:, g * SLOT : (g + 1) * SLOT].astype(BF)
 
 
@@ -164,16 +162,49 @@
     return jnp.where(place == 72 * (m >> 4) + 2 * (m & 15), 1.0, 0.0).astype(BF)
 
 
-def load_body(codes, x, cot, load):
-    load[:, : S * S] = x[...]
-    load[:, S * S : CODES] = cot[...]
+def load_body(codes_hbm, x_hbm, cot_hbm, one_hbm, two_hbm, down_hbm, edges, load, one, two, down, codes, sems):
+    later = [
+        pltpu.make_async_copy(one_hbm, one, sems.at[3]),
+        pltpu.make_async_copy(two_hbm, two, sems.at[4]),
+        pltpu.make_async_copy(down_hbm, down, sems.at[5]),
+    ]
+    copies = [
+        pltpu.make_async_copy(codes_hbm, codes, sems.at[0]),
+        pltpu.make_async_copy(x_hbm, load.at[:, pl.ds(0, S * S)], sems.at[1]),
+        pltpu.make_async_copy(cot_hbm, load.at[:, pl.ds(S * S, 256)], sems.at[2]),
+    ]
+    for copy in copies + later:
+        copy.start()
+    lane, edge, along = lanes_of()[:3]
+    y = jnp.where((edge & 1) == 0, jnp.where(edge == 0, 0, S - 1), along)
+    x = jnp.where((edge & 1) == 0, along, jnp.where(edge == 1, S - 1, 0))
+    hot = pick([S * y + x], 0, S * S)
+    for copy in copies:
+        copy.wait()
+    edges[:, :SLOT] = mm(load[:, : S * S], hot).astype(BF)
     row = lax.broadcasted_iota(jnp.int32, (C, SLOT), 0)
     value = jnp.where(row == 0, codes[0, 0], jnp.where(row == 1, codes[0, 1], jnp.where(row == 2, codes[0, 2], codes[0, 3])))
-    load[:, CODES:] = value.astype(F32).astype(BF)
-
-
-def send_inputs_body(load, facts, *slots):
-    codes = load[:16, CODES:].astype(F32).astype(jnp.int32)
+    edges[:, SLOT:] = value.astype(F32).astype(BF)
+    for copy in later:
+        copy.wait()
+
+
+def edge_row(facts, group):
+    lane, _, along, part, kind, j = lanes_of()
+    side, code = facts[group : group + 1, :], facts[4 + group : 5 + group, :]
+    along = jnp.where((code & 1) == 1, 31 - along, along)
+    place = S * ((side - code + 4) & 3) + along
+    valid = lane < S
+    if group >= 2:
+        mine = (part >= 0) & (kind < 4) & ((kind & 1) == group - 2) & (j == 0)
+        corner = jnp.where(kind >= 2, 2 * S, 0) + jnp.where(side == 1, S - 1, 0)
+        place = jnp.where(mine, corner, place)
+        valid = valid | mine
+    return jnp.where(valid, place, -1)
+
+
+def send_inputs_body(edges, facts, *slots):
+    codes = edges[:16, SLOT:].astype(F32).astype(jnp.int32)
     row, column = lax.axis_index("core"), lax.axis_index("z") & 1
     sides = [2 - 2 * row, 2 * row, 1 + 2 * column, 3 - 2 * column]
     for g, side in enumerate(sides):
@@ -182,8 +213,21 @@
         code = jnp.where(side == 0, codes[0:1, :], code)
         facts[g : g + 1, :] = jnp.full((1, SLOT), side, jnp.int32)
         facts[4 + g : 5 + g, :] = code
-    hot = pick(sources(facts, 1, S, 0), 0, S * S)
-    write_slots(slots, mm(load[:, : S * S], hot))
+    hot = pick([edge_row(facts, g) for g in range(4)], 0, SLOT)
+    write_slots(slots, mm(edges[:, :SLOT], hot))
+
+
+def hots_body(facts, rim_one, rim_two, source_one, source_two):
+    rim_one[...] = pick(rims(facts, 1), 0, FULL)
+    rim_two[...] = pick(rims(facts, 2), 0, FULL)
+    source_one[...] = pick(sources(facts, 1), BASE, INNER)
+    source_two[...] = pick(sources(facts, 2), BASE, INNER)
+
+
+def spread_body(load, spread):
+    spread[...] = jnp.zeros_like(spread)
+    for y in range(S):
+        spread[:, BASE + PITCH * y : BASE + PITCH * y + S] = load[:, S * y : S * y + S]
 
 
 def transpose_taps(src, dst, count):
@@ -192,15 +236,12 @@
         dst[:, C * n : C * (n + 1)] = jnp.transpose(block).astype(BF)
 
 
-def prepare_body(load, down, one, two, spread, upstream, grad_two, one_t, two_t, wide, col, down_t):
+def prepare_body(load, down, one, two, upstream, grad_two, one_t, two_t, wide, col, down_t):
     transpose_taps(one, one_t, 9)
     transpose_taps(two, two_t, 9)
     transpose_taps(down, down_t, 4)
-    spread[...] = jnp.zeros_like(spread)
-    for y in range(S):
-        spread[:, BASE + PITCH * y : BASE + PITCH * y + S] = load[:, S * y : S * y + S]
     wide[...] = jnp.zeros_like(wide)
-    wide[:, BASE : BASE + INNER] = nt(load[:, S * S : CODES], up_matrix()).astype(BF)
+    wide[:, BASE : BASE + INNER] = nt(load[:, S * S :], up_matrix()).astype(BF)
     for n in range(4):
         lo = BASE - (n // 2) * PITCH - n % 2
         col[C * n : C * (n + 1), :] = wide[:, lo : lo + INNER]
@@ -208,27 +249,22 @@
     grad_two[...] = mm(down_t[...], col[...])
 
 
-def first_body(facts, spread, r0, r1, r2, r3, w, ext, hidden, slope, m0, m1, m2, m3, wide, col):
-    halo = nt(read_slots((r0, r1, r2, r3)), pick(rims(facts, 1), 0, FULL)).astype(BF)
-    full = spread[...] + halo
-    ext[...] = full
-    wide[...] = jnp.zeros_like(wide)
-    wide[:, BASE : BASE + FULL] = full
+def first_body(rim, source, spread, r0, r1, r2, r3, w, col, hidden, slope, m3, m2, m1, m0, wide):
+    halo = nt(read_slots((r0, r1, r2, r3)), rim[...]).astype(BF)
+    wide[:, BASE : BASE + FULL] = spread[...] + halo
     gather_taps(col, wide, 1, 1, BASE, INNER)
     value, grad = gelu_parts(mm(w[...], col[...]))
     value = jnp.where(columns_mask(), value, 0.0).astype(BF)
     hidden[...] = value
     slope[...] = grad
-    write_slots((m0, m1, m2, m3), mm(value, pick(sources(facts, 2), BASE, INNER)))
+    write_slots((m3, m2, m1, m0), mm(value, source[...]))
 
 
 def second_body(
-    facts, hidden, r0, r1, r2, r3, w, wt, grad_two,
-    ext, hidden_two, delta, grad_mid, m0, m1, m2, m3, wide, col, col_full,
+    rim, hidden, r0, r1, r2, r3, w, wt, grad_two,
+    ext, hidden_two, delta, grad_mid, m3, m2, m1, m0, wide, col, col_full,
 ):
-    rim = pick(rims(facts, 2), 0, FULL)
-    halo = nt(read_slots((r0, r1, r2, r3)), rim).astype(BF)
-    wide[...] = jnp.zeros_like(wide)
+    halo = nt(read_slots((r0, r1, r2, r3)), rim[...]).astype(BF)
     wide[:, BASE : BASE + FULL] = halo
     wide[:, 2 * BASE : 2 * BASE + INNER] = halo[:, BASE : BASE + INNER] + hidden[...]
     ext[...] = wide[:, BASE : BASE + FULL]
@@ -242,11 +278,10 @@
     gather_taps(col_full, wide, 2, -1, 0, FULL)
     pad = mm(wt[...], col_full[...])
     grad_mid[...] = pad[:, BASE : BASE + INNER]
-    write_slots((m0, m1, m2, m3), mm(pad.astype(BF), rim))
+    write_slots((m3, m2, m1, m0), mm(pad.astype(BF), rim[...]))
 
 
 def second_sums_body(scale, ext, hidden_two, delta, upstream, down, encoded, grad, grad_down, wide, col):
-    wide[...] = jnp.zeros_like(wide)
     wide[:, BASE : BASE + FULL] = ext[...]
     gather_taps(col, wide, 2, 1, BASE, INNER)
     grad[...] = nt(delta[...], col[...]) * scale
@@ -259,14 +294,11 @@
     encoded[...] = mm(mm(down[...], four).astype(BF), up_matrix()).astype(BF)
 
 
-def third_body(scale, facts, grad_mid, r0, r1, r2, r3, slope, ext, sum_two, sum_down, delta, packed, wide, col):
-    back = nt(read_slots((r0, r1, r2, r3)), pick(sources(facts, 2), BASE, INNER))
+def third_body(scale, source, grad_mid, r0, r1, r2, r3, slope, col, sum_two, sum_down, delta, packed):
+    back = nt(read_slots((r0, r1, r2, r3)), source[...])
     back = (grad_mid[...] + back) * slope[...]
     back = jnp.where(columns_mask(), back, 0.0).astype(BF)
     delta[...] = back
-    wide[...] = jnp.zeros_like(wide)
-    wide[:, BASE : BASE + FULL] = ext[...]
-    gather_taps(col, wide, 1, 1, BASE, INNER)
     sums = [nt(back, col[...]) * scale, sum_two[...], sum_down[...], jnp.zeros((C, SLOT), F32)]
     sums = jnp.concatenate(sums, axis=1)
     for n in range(PACKED // C):
@@ -281,18 +313,18 @@
     down[...] = sums[:, 18 * C :]
 
 
-def fourth_body(facts, delta, wt, grad, m0, m1, m2, m3, wide, col_full):
+def fourth_body(rim, delta, wt, grad, m3, m2, m1, m0, wide, col_full):
     wide[...] = jnp.zeros_like(wide)
     wide[:, 2 * BASE : 2 * BASE + INNER] = delta[...]
     gather_taps(col_full, wide, 1, -1, 0, FULL)
     pad = mm(wt[...], col_full[...])
     grad[...] = pad[:, BASE : BASE + INNER]
-    write_slots((m0, m1, m2, m3), mm(pad.astype(BF), pick(rims(facts, 1), 0, FULL)))
-
-
-def last_body(facts, grad, r0, r1, r2, r3, encoded, o):
+    write_slots((m3, m2, m1, m0), mm(pad.astype(BF), rim[...]))
+
+
+def last_body(source, grad, r0, r1, r2, r3, encoded, o):
     o[:, S * S :] = encoded[...]
-    back = nt(read_slots((r0, r1, r2, r3)), pick(sources(facts, 1), BASE, INNER))
+    back = nt(read_slots((r0, r1, r2, r3)), source[...])
     back = (grad[...] + back).astype(BF)
     for y in range(S):
         o[:, S * y : S * y + S] = back[:, PITCH * y : PITCH * y + S]
@@ -300,8 +332,7 @@
 
 def home(t):
     row, column = t // ROW_TILES, t % ROW_TILES
-    x = row // 4
-    y = (row // 2 % 2) ^ (x % 2)
+    x, y = RING[row // 2]
     return ((x * 2 + y) * 8 + column) * 2 + row % 2
 
 
@@ -323,39 +354,52 @@
     return lax.broadcasted_iota(jnp.int32, (C, SLOT), 1)
 
 
+def used(message):
+    return jnp.where(lane() < CORNER + 16, message, 0)
+
+
 def exchange(m):
-    r3 = swap(m[3], 1, 1)
-    r2 = swap(m[2], 1, 0)
+    r3 = swap(used(m[3]), 1, 1)
+    r2 = swap(used(m[2]), 1, 0)
     corners = jnp.where(((lane() >> 2) & 1) == 0, r2, r3)
     r1 = swap(jnp.where(lane() < CORNER, m[1], corners), ROW_TILES, 1)
     r0 = swap(jnp.where(lane() < CORNER, m[0], corners), ROW_TILES, 0)
     return r0, r1, r2, r3
 
 
-def exchange_back(m):
-    r1 = swap(m[1], ROW_TILES, 1)
-    r0 = swap(m[0], ROW_TILES, 0)
-    corners = r0 + r1
+def north_south_back(m):
+    r1 = swap(used(m[1]), ROW_TILES, 1)
+    r0 = swap(used(m[0]), ROW_TILES, 0)
+    return r0, r1, r0 + r1
+
+
+def east_west_back(m, corners):
     r3 = swap(jnp.where(lane() < CORNER, m[3], corners), 1, 1)
     r2 = swap(jnp.where(lane() < CORNER, m[2], corners), 1, 0)
-    return r0, r1, r2, r3
-
-
-def add_up(packed):
-    share = PACKED // lax.axis_size(NEAR)
-
-    def trade(v, axes):
-        return lax.all_to_all(v, axes, 0, 0, tiled=True)
-
-    def total(v):
-        return jnp.sum(v.astype(F32), axis=0).astype(BF)
-
-    def everyone(v, axes):
-        return jnp.broadcast_to(v[None], (lax.axis_size(axes),) + v.shape)
-
-    part = total(trade(packed.reshape(-1, share, SLOT), NEAR))
-    part = total(trade(everyone(part, FAR), FAR))
-    return trade(everyone(part, NEAR), NEAR).reshape(PACKED, SLOT)
+    return r2, r3
+
+
+def exchange_back(m):
+    r0, r1, corners = north_south_back(m)
+    return (r0, r1) + east_west_back(m, corners)
+
+
+def fold_body(parts, o):
+    total = parts[0].astype(F32)
+    for n in range(1, parts.shape[0]):
+        total = total + parts[n].astype(F32)
+    total = total.astype(BF)
+    for n in range(o.shape[0]):
+        o[n] = total
+
+
+def trade(parts, axes):
+    return lax.all_to_all(parts, axes, 0, 0, tiled=True)
+
+
+def fold(parts):
+    (spread,) = call(fold_body, [out(parts.shape, BF)], [], [parts], C * C, "fold")
+    return spread
 
 
 def per_device(inputs, cotangent, seam_codes, conv_one, conv_two, down_weight):
@@ -368,38 +412,57 @@
     col_full = pltpu.VMEM((9 * C, FULL), BF)
     dense = 2 * C * 9 * C * INNER
 
-    (load,) = call(load_body, [out((C, LOAD), BF)], [], [seam_codes, x, cot], C * LOAD, "load")
-    load = move(load, [(t, home(t)) for t in range(128)])
+    edges, load, conv_one, conv_two, down_weight = call(
+        load_body,
+        [out((C, 2 * SLOT), BF), out((C, LOAD), BF), out((C, 9 * C), BF), out((C, 9 * C), BF), out((C, 4 * C), BF)],
+        [pltpu.SMEM((1, 4), jnp.int32), pltpu.SemaphoreType.DMA((6,))],
+        [seam_codes, x, cot, conv_one, conv_two, down_weight],
+        C * LOAD,
+        "load",
+        pltpu.HBM,
+        60,
+    )
+    there = [(t, home(t)) for t in range(128)]
+    edges, load = move(edges, there), move(load, there)
     facts, *sent = call(
-        send_inputs_body, [out((8, SLOT), jnp.int32)] + slots, [], [load], 2 * C * 1024 * 512, "send_inputs"
-    )
-    spread, upstream, grad_two, one_t, two_t = call(
+        send_inputs_body, [out((8, SLOT), jnp.int32)] + slots, [], [edges], 2 * C * SLOT * 512, "send_inputs"
+    )
+    rim_one, rim_two, source_one, source_two = call(
+        hots_body,
+        [out((FULL, 512), BF)] * 2 + [out((INNER, 512), BF)] * 2,
+        [],
+        [facts],
+        dense,
+        "hots",
+    )
+    (spread,) = call(spread_body, [out((C, FULL), BF)], [], [load], C * FULL, "spread")
+    upstream, grad_two, one_t, two_t = call(
         prepare_body,
-        [out((C, FULL), BF), out((C, INNER), BF), out((C, INNER), F32)] + [out((C, 9 * C), BF)] * 2,
+        [out((C, INNER), BF), out((C, INNER), F32)] + [out((C, 9 * C), BF)] * 2,
         [wide, pltpu.VMEM((4 * C, INNER), BF), pltpu.VMEM((C, 4 * C), BF)],
         [load, down_weight, conv_one, conv_two],
         dense,
         "prepare",
     )
-    got = exchange(sent)
-    ext, hidden, slope, *sent = call(
+    got = exchange(sent[::-1])
+    taps_one, hidden, slope, *sent = call(
         first_body,
-        [out((C, FULL), BF), out((C, INNER), BF), out((C, INNER), F32)] + slots,
-        [wide, col],
-        [facts, spread, *got, conv_one],
+        [out((9 * C, INNER), BF), out((C, INNER), BF), out((C, INNER), F32)] + slots,
+        [wide],
+        [rim_one, source_two, spread, *got, conv_one],
         2 * dense,
         "first",
     )
-    got = exchange(sent)
+    got = exchange(sent[::-1])
     ext_two, hidden_two, delta_two, grad_mid, *sent = call(
         second_body,
         [out((C, FULL), BF), out((C, INNER), BF), out((C, INNER), BF), out((C, INNER), F32)] + slots,
         [wide, col, col_full],
-        [facts, hidden, *got, conv_two, two_t, grad_two],
+        [rim_two, hidden, *got, conv_two, two_t, grad_two],
         3 * dense,
         "second",
     )
-    got = exchange_back(sent)
+    got = exchange_back(sent[::-1])
     encoded, sum_two, sum_down = call(
         lambda *refs: second_sums_body(scale, *refs),
         [out((C, 256), BF), out((C, 9 * C), F32), out((C, 4 * C), F32)],
@@ -411,8 +474,8 @@
     delta_one, packed = call(
         lambda *refs: third_body(scale, *refs),
         [out((C, INNER), BF), out((PACKED, SLOT), BF)],
-        [wide, col],
-        [facts, grad_mid, *got, slope, ext, sum_two, sum_down],
+        [],
+        [source_two, grad_mid, *got, slope, taps_one, sum_two, sum_down],
         2 * dense,
         "third",
     )
@@ -420,20 +483,26 @@
         fourth_body,
         [out((C, INNER), F32)] + slots,
         [wide, col_full],
-        [facts, delta_one, one_t],
+        [rim_one, delta_one, one_t],
         2 * dense,
         "fourth",
     )
-    got = exchange_back(sent)
+    assert lax.axis_size(NEAR) == lax.axis_size(FAR) == 16
+    parts = trade(packed.reshape(16, PACKED // 16, SLOT), NEAR)
+    sent = sent[::-1]
+    r0, r1, corners = north_south_back(sent)
+    parts = trade(fold(parts), FAR)
+    r2, r3 = east_west_back(sent, corners)
+    parts = trade(fold(parts), NEAR)
     (results,) = call(
-        last_body, [out((C, CODES), BF)], [], [facts, grad_in, *got, encoded], dense, "last"
+        last_body, [out((C, LOAD), BF)], [], [source_one, grad_in, r0, r1, r2, r3, encoded], dense, "last"
     )
     results = move(results, [(home(t), t) for t in range(128)])
     sums = call(
         unpack_body,
         [out((C, 9 * C), F32), out((C, 9 * C), F32), out((C, 4 * C), F32)],
         [],
-        [add_up(packed)],
+        [parts.reshape(PACKED, SLOT)],
         C * C,
         "unpack",
     )

time: 105 us -> 97.6 us (0.930)
  waiting for transfers between devices: 36.4 us -> 29.8 us
  Pallas kernels: 10.7 us -> 14.1 us
  local copies, waits for them, and re-layouts: 4.99 us -> 2.18 us
    ppermute x18 -> x19, waiting for transfers between devices: 21.7 us -> 15.1 us  [move(): return lax.ppermute(value, TILE, pairs)]
    pallas_call x10 -> x14, Pallas kernels: 10.7 us -> 14.1 us  [call(): pl.pallas_call(body, out_shape=outs, in_specs=specs, out_specs=[pl.BlockS...]
    ppermute x18 -> x19, starting transfers between devices: 34.7 us -> 32.3 us  [move(): return lax.ppermute(value, TILE, pairs)]
    unnamed x12 -> x6, local copies, waits for them, and re-layouts: 2.32 us -> 0.9 us
    broadcast_in_dim x2 -> x0, local copies, waits for them, and re-layouts: 1.39 us -> none  [everyone(): return jnp.broadcast_to(v[None], (lax.axis_size(axes),) + v.shape)]
    all_to_all x3, starting transfers between devices: 16.3 us -> 17.7 us  [trade(): return lax.all_to_all(parts, axes, 0, 0, tiled=True)]
  transfers between devices with their start and end apart: 21 -> 22, of which waited for: 14 -> 14; matrix products, arithmetic and copies ran while one was open for 3% -> 1% of each run, Pallas kernels for 4% -> 7%
where the time goes in v2:
time: 97.6 us; the launch traced here: 97 us
  starting transfers between devices  50 us (51%)
  waiting for transfers between devices  29.8 us (31%)
  Pallas kernels  14.1 us (14%)
  local copies, waits for them, and re-layouts  2.18 us (2%)
    ppermute x19, starting transfers between devices, move(): return lax.ppermute(value, TILE, pairs)  32.3 us
    all_to_all x3, starting transfers between devices, trade(): return lax.all_to_all(parts, axes, 0, 0, tiled=True)  17.7 us
    ppermute x19, waiting for transfers between devices, move(): return lax.ppermute(value, TILE, pairs)  15.1 us
    all_to_all x3, waiting for transfers between devices, trade(): return lax.all_to_all(parts, axes, 0, 0, tiled=True)  14.8 us
    pallas_call x14, Pallas kernels, call(): pl.pallas_call(body, out_shape=outs, in_specs=specs, out_specs=[pl.BlockS...  14.1 us
  transfers between devices with their start and end apart: 22, of which 14 were waited for; matrix products, arithmetic and copies ran while one was open for 1% of the time, Pallas kernels for 7%

profile of v2, /device:TPU:1, one launch (start us, length us, event | category | flops | bytes accessed | tf_op | source)
XLA Modules:
  0.0 97.0 jit_solution(5885400400632602881)
XLA Ops:
  0.6 1.9 %load.1 = (bf16[64,256]{1,0:T(8,128)(2,1)}, bf16[64,1280]{1,0:T(8,128)(2,1)}, bf16[64,576]{1,0:T(8,128)(2,1)}, bf16[64,576]{1,0:T(8,128)(2,1)}, bf16[64,256]{1,0:T(8,128)(2,1)}) custom-call(s32[1,4]{1,0:T(1,128)} %codes_hbm.1, bf16[64,1024]{1,0:T(8,128)(2,1)} %bitcast.9, bf16[64,256]{1,0:T(8,128)(2,1)} %bitcast.10, bf16[64,576]{1,0:T(8,128)(2,1)} %one_hbm.1, ...), custom_call_target="tpu_custom_call" | custom-call | flops 81920 | bytes 720912 | tf_op jit(solution)/shard_map/load/pallas_call | solution.py:34
  2.5 5.9 %collective-permute-start = (bf16[64,256]{1,0:T(8,128)(2,1)}, bf16[64,256]{1,0:T(8,128)(2,1)S(1)}, u32[]{:S(2)}, u32[]{:S(2)}) collective-permute-start(bf16[64,256]{1,0:T(8,128)(2,1)} %get-tuple-element.51), channel_id=1, source_target_pairs={{0,64},{2,68},{4,72},{6,76},{8,80},{10,84},{12,88},{14,92},{16,66}... | collective-permute-start | bytes 98312 | tf_op jit(solution)/shard_map/ppermute | solution.py:340
  8.4 4.8 %collective-permute-start.1 = (bf16[64,1280]{1,0:T(8,128)(2,1)}, bf16[64,1280]{1,0:T(8,128)(2,1)S(1)}, u32[]{:S(2)}, u32[]{:S(2)}) collective-permute-start(bf16[64,1280]{1,0:T(8,128)(2,1)} %get-tuple-element.57), channel_id=1, source_target_pairs={{0,64},{2,68},{4,72},{6,76},{8,80},{10,84},{12,88},{14,92},{16,66}... | collective-permute-start | bytes 491528 | tf_op jit(solution)/shard_map/ppermute | solution.py:340
  13.2 2.3 %collective-permute-done.edges = bf16[64,256]{1,0:T(8,128)(2,1)S(1)} collective-permute-done((bf16[64,256]{1,0:T(8,128)(2,1)}, bf16[64,256]{1,0:T(8,128)(2,1)S(1)}, u32[]{:S(2)}, u32[]{:S(2)}) %collective-permute-start) | collective-permute-done | bytes 32800 | tf_op jit(solution)/shard_map/ppermute | solution.py:340
  15.7 4.3 %collective-permute-start.3 = (bf16[64,128]{1,0:T(8,128)(2,1)S(1)}, bf16[64,128]{1,0:T(8,128)(2,1)S(1)}, u32[]{:S(2)}, u32[]{:S(2)}) collective-permute-start(bf16[64,128]{1,0:T(8,128)(2,1)S(1)} %get-tuple-element.111), channel_id=1, source_target_pairs={{68,72},{72,68},{76,80},{80,76},{84,88},{88,84},{92,66},{66,92},{7... | collective-permute-start | bytes 49160 | tf_op jit(solution)/shard_map/ppermute | solution.py:340
  20.0 1.4 %collective-permute-done.3.r3 = bf16[64,128]{1,0:T(8,128)(2,1)S(1)} collective-permute-done((bf16[64,128]{1,0:T(8,128)(2,1)S(1)}, bf16[64,128]{1,0:T(8,128)(2,1)S(1)}, u32[]{:S(2)}, u32[]{:S(2)}) %collective-permute-start.3) | collective-permute-done | bytes 16416 | tf_op jit(solution)/shard_map/ppermute | solution.py:340
  21.5 1.9 %collective-permute-done.2.r2 = bf16[64,128]{1,0:T(8,128)(2,1)S(1)} collective-permute-done((bf16[64,128]{1,0:T(8,128)(2,1)S(1)}, bf16[64,128]{1,0:T(8,128)(2,1)S(1)}, u32[]{:S(2)}, u32[]{:S(2)}) %collective-permute-start.2) | collective-permute-done | bytes 16416 | tf_op jit(solution)/shard_map/ppermute | solution.py:340
  24.3 1.0 %hots.1 = (bf16[1408,512]{1,0:T(8,128)(2,1)S(1)}, bf16[1408,512]{1,0:T(8,128)(2,1)S(1)}, bf16[1152,512]{1,0:T(8,128)(2,1)S(1)}, bf16[1152,512]{1,0:T(8,128)(2,1)S(1)}) custom-call(s32[8,128]{1,0:T(8,128)S(1)} %get-tuple-element.52.facts), custom_call_target="tpu_custom_call" | custom-call | flops 84934656 | bytes 5246976 | tf_op jit(solution)/shard_map/hots/pallas_call | solution.py:34
  25.7 0.9 collective-permute-done.5.r1
  26.7 0.9 copy-done.1
  27.5 1.2 %first.1 = (bf16[576,1152]{1,0:T(8,128)(2,1)S(1)}, bf16[64,1152]{1,0:T(8,128)(2,1)S(1)}, f32[64,1152]{1,0:T(8,128)S(1)}, bf16[64,128]{1,0:T(8,128)(2,1)S(1)}, bf...) custom-call(bf16[1408,512]{1,0:T(8,128)(2,1)S(1)} %get-tuple-element.54.rim, ...), custom_call_target="tpu_custom_call" | custom-call | flops 169869312 | bytes 4775936 | tf_op jit(solution)/shard_map/first/pallas_call | solution.py:34
  28.8 1.9 %collective-permute-start.7 = (bf16[64,128]{1,0:T(8,128)(2,1)S(1)}, bf16[64,128]{1,0:T(8,128)(2,1)S(1)}, u32[]{:S(2)}, u32[]{:S(2)}) collective-permute-start(bf16[64,128]{1,0:T(8,128)(2,1)S(1)} %get-tuple-element.109), channel_id=1, source_target_pairs={{68,72},{72,68},{76,80},{80,76},{84,88},{88,84},{92,66},{66,92},{7... | collective-permute-start | bytes 49160 | tf_op jit(solution)/shard_map/ppermute | solution.py:340
  30.7 2.5 %collective-permute-done.7.r3 = bf16[64,128]{1,0:T(8,128)(2,1)S(1)} collective-permute-done((bf16[64,128]{1,0:T(8,128)(2,1)S(1)}, bf16[64,128]{1,0:T(8,128)(2,1)S(1)}, u32[]{:S(2)}, u32[]{:S(2)}) %collective-permute-start.7) | collective-permute-done | bytes 16416 | tf_op jit(solution)/shard_map/ppermute | solution.py:340
  33.3 2.3 %collective-permute-start.9 = (bf16[64,128]{1,0:T(8,128)(2,1)S(1)}, bf16[64,128]{1,0:T(8,128)(2,1)S(1)}, u32[]{:S(2)}, u32[]{:S(2)}) collective-permute-start(bf16[64,128]{1,0:T(8,128)(2,1)S(1)} %get-tuple-element.97), channel_id=1, source_target_pairs={{66,0},{0,66},{70,4},{4,70},{74,8},{8,74},{78,12},{12,78},{82,16},... | collective-permute-start | bytes 49160 | tf_op jit(solution)/shard_map/ppermute | solution.py:340
  35.7 1.3 %prepare.1 = (bf16[64,1152]{1,0:T(8,128)(2,1)S(1)}, f32[64,1152]{1,0:T(8,128)S(1)}, bf16[64,576]{1,0:T(8,128)(2,1)S(1)}, bf16[64,576]{1,0:T(8,128)(2,1)S(1)}) custom-call(bf16[64,1280]{1,0:T(8,128)(2,1)S(1)} %collective-permute-done.1.load, bf16[64,256]{1,0:T(8,128)(2,1)S(1)} %copy-done.2, bf16[64,576]{1,0:T(8,128)(2,1)S(1)} %copy-done.1, ...), custom_call_target="tpu_custom_call" | custom-call | flops 84934656 | bytes 933888 | tf_op jit(solution)/shard_map/prepare/pallas_call | solution.py:34
  37.2 1.8 %second.1 = (bf16[64,1408]{1,0:T(8,128)(2,1)S(1)}, bf16[64,1152]{1,0:T(8,128)(2,1)S(1)}, bf16[64,1152]{1,0:T(8,128)(2,1)S(1)}, f32[64,1152]{1,0:T(8,128)S(1)}, b...) custom-call(bf16[1408,512]{1,0:T(8,128)(2,1)S(1)} %get-tuple-element, ...), custom_call_target="tpu_custom_call" | custom-call | flops 254803968 | bytes 2932736 | tf_op jit(solution)/shard_map/second/pallas_call | solution.py:34
  39.1 1.7 %collective-permute-start.11 = (bf16[64,128]{1,0:T(8,128)(2,1)S(1)}, bf16[64,128]{1,0:T(8,128)(2,1)S(1)}, u32[]{:S(2)}, u32[]{:S(2)}) collective-permute-start(bf16[64,128]{1,0:T(8,128)(2,1)S(1)} %get-tuple-element.107), channel_id=1, source_target_pairs={{66,0},{0,66},{70,4},{4,70},{74,8},{8,74},{78,12},{12,78},{82,16},... | collective-permute-start | bytes 49160 | tf_op jit(solution)/shard_map/ppermute | solution.py:340
  40.8 1.5 %collective-permute-done.11.refs_3_ = bf16[64,128]{1,0:T(8,128)(2,1)S(1)} collective-permute-done((bf16[64,128]{1,0:T(8,128)(2,1)S(1)}, bf16[64,128]{1,0:T(8,128)(2,1)S(1)}, u32[]{:S(2)}, u32[]{:S(2)}) %collective-permute-start.11) | collective-permute-done | bytes 16416 | tf_op jit(solution)/shard_map/ppermute | solution.py:340
  42.4 1.7 %collective-permute-start.13 = (bf16[64,128]{1,0:T(8,128)(2,1)S(1)}, bf16[64,128]{1,0:T(8,128)(2,1)S(1)}, u32[]{:S(2)}, u32[]{:S(2)}) collective-permute-start(bf16[64,128]{1,0:T(8,128)(2,1)S(1)} %get-tuple-element.103), channel_id=1, source_target_pairs={{68,72},{72,68},{76,80},{80,76},{84,88},{88,84},{92,66},{66,92},{7... | collective-permute-start | bytes 49160 | tf_op jit(solution)/shard_map/ppermute | solution.py:340
  44.1 1.0 %second_sums.1 = (bf16[64,256]{1,0:T(8,128)(2,1)S(1)}, f32[64,576]{1,0:T(8,128)S(1)}, f32[64,256]{1,0:T(8,128)S(1)}) custom-call(bf16[64,1408]{1,0:T(8,128)(2,1)S(1)} %get-tuple-element.79.refs_0_, bf16[64,1152]{1,0:T(8,128)(2,1)S(1)} %get-tuple-element.80.refs_1_, bf16[64,1152]{1,0:T(8,128)(2,1)S(1)} %get-tuple-element.81.refs_2_, ...), custom_call_target="tpu_custom_call" | custom-call | flops 169869312 | bytes 901120 | tf_op jit(solution)/shard_map/second_sums/pallas_call | solution.py:34
  45.1 1.7 %collective-permute-done.13.refs_5_ = bf16[64,128]{1,0:T(8,128)(2,1)S(1)} collective-permute-done((bf16[64,128]{1,0:T(8,128)(2,1)S(1)}, bf16[64,128]{1,0:T(8,128)(2,1)S(1)}, u32[]{:S(2)}, u32[]{:S(2)}) %collective-permute-start.13) | collective-permute-done | bytes 16416 | tf_op jit(solution)/shard_map/ppermute | solution.py:340
  47.0 1.6 %third.1 = (bf16[64,1152]{1,0:T(8,128)(2,1)S(1)}, bf16[768,128]{1,0:T(8,128)(2,1)}) custom-call(bf16[1152,512]{1,0:T(8,128)(2,1)S(1)} %get-tuple-element.55.source.refs_0_, f32[64,1152]{1,0:T(8,128)S(1)} %get-tuple-element.72.refs_1_, bf16[64,128]{1,0:T(8,128)(2,1)S(1)} %collective-permute-done.10.refs_2_, ...), custom_call_target="tpu_custom_call" | custom-call | flops 169869312 | bytes 3719168 | tf_op jit(solution)/shard_map/third/pallas_call | solution.py:34
  48.5 6.9 %all-to-all-start = ((bf16[16,48,128]{2,1,0:T(8,128)(2,1)}), bf16[16,48,128]{2,1,0:T(8,128)(2,1)S(1)}, u32[]{:S(2)}, u32[]{:S(2)}) async-start(bf16[16,48,128]{2,1,0:T(8,128)(2,1)} %bitcast.4), calls=%async_computation | async-start | bytes 393216 | tf_op jit(solution)/shard_map/all_to_all | solution.py:397
  56.6 0.9 collective-permute-start.14
  57.6 2.3 %collective-permute-done.15.r1 = bf16[64,128]{1,0:T(8,128)(2,1)S(1)} collective-permute-done((bf16[64,128]{1,0:T(8,128)(2,1)S(1)}, bf16[64,128]{1,0:T(8,128)(2,1)S(1)}, u32[]{:S(2)}, u32[]{:S(2)}) %collective-permute-start.15) | collective-permute-done | bytes 16416 | tf_op jit(solution)/shard_map/ppermute | solution.py:340
  59.9 2.6 %collective-permute-start.17 = (bf16[64,128]{1,0:T(8,128)(2,1)S(1)}, bf16[64,128]{1,0:T(8,128)(2,1)S(1)}, u32[]{:S(2)}, u32[]{:S(2)}) collective-permute-start(bf16[64,128]{1,0:T(8,128)(2,1)S(1)} %get-tuple-element.101), channel_id=1, source_target_pairs={{68,72},{72,68},{76,80},{80,76},{84,88},{88,84},{92,66},{66,92},{7... | collective-permute-start | bytes 49160 | tf_op jit(solution)/shard_map/ppermute | solution.py:340
  62.5 3.2 %all-to-all-done.parts = bf16[16,48,128]{2,1,0:T(8,128)(2,1)S(1)} async-done(((bf16[16,48,128]{2,1,0:T(8,128)(2,1)}), bf16[16,48,128]{2,1,0:T(8,128)(2,1)S(1)}, u32[]{:S(2)}, u32[]{:S(2)}) %all-to-all-start) | async-done | bytes 196640 | tf_op jit(solution)/shard_map/all_to_all | solution.py:397
  66.5 6.2 %all-to-all-start.1 = ((bf16[16,48,128]{2,1,0:T(8,128)(2,1)}), bf16[16,48,128]{2,1,0:T(8,128)(2,1)S(1)}, u32[]{:S(2)}, u32[]{:S(2)}) async-start(bf16[16,48,128]{2,1,0:T(8,128)(2,1)} %fold.2), calls=%async_computation.1 | async-start | bytes 393216 | tf_op jit(solution)/shard_map/all_to_all | solution.py:397
  73.3 4.7 %collective-permute-start.18 = (bf16[64,1280]{1,0:T(8,128)(2,1)S(1)}, bf16[64,1280]{1,0:T(8,128)(2,1)S(1)}, u32[]{:S(2)}, u32[]{:S(2)}) collective-permute-start(bf16[64,1280]{1,0:T(8,128)(2,1)S(1)} %last.1), channel_id=1, source_target_pairs={{64,0},{68,2},{72,4},{76,6},{80,8},{84,10},{88,12},{92,14},{66,16}... | collective-permute-start | bytes 491528 | tf_op jit(solution)/shard_map/ppermute | solution.py:340
  78.1 2.5 %all-to-all-done.1.parts = bf16[16,48,128]{2,1,0:T(8,128)(2,1)S(1)} async-done(((bf16[16,48,128]{2,1,0:T(8,128)(2,1)}), bf16[16,48,128]{2,1,0:T(8,128)(2,1)S(1)}, u32[]{:S(2)}, u32[]{:S(2)}) %all-to-all-start.1) | async-done | bytes 196640 | tf_op jit(solution)/shard_map/all_to_all | solution.py:397
  81.3 4.6 %all-to-all-start.2 = ((bf16[16,48,128]{2,1,0:T(8,128)(2,1)}), bf16[16,48,128]{2,1,0:T(8,128)(2,1)S(1)}, u32[]{:S(2)}, u32[]{:S(2)}) async-start(bf16[16,48,128]{2,1,0:T(8,128)(2,1)} %fold.3), calls=%async_computation.2 | async-start | bytes 393216 | tf_op jit(solution)/shard_map/all_to_all | solution.py:397
  87.2 9.1 %all-to-all-done.2 = bf16[16,48,128]{2,1,0:T(8,128)(2,1)S(1)} async-done(((bf16[16,48,128]{2,1,0:T(8,128)(2,1)}), bf16[16,48,128]{2,1,0:T(8,128)(2,1)S(1)}, u32[]{:S(2)}, u32[]{:S(2)}) %all-to-all-start.2) | async-done | bytes 196640 | tf_op jit(solution)/shard_map/all_to_all | solution.py:397
  (44 shorter events, 7.4 us)
Async XLA Ops:
  2.5 13.0 %collective-permute-start = (bf16[64,256]{1,0:T(8,128)(2,1)}, bf16[64,256]{1,0:T(8,128)(2,1)S(1)}, u32[]{:S(2)}, u32[]{:S(2)}) collective-permute-start(bf16[64,256]{1,0:T(8,128)(2,1)} %get-tuple-element.51), channel_id=1, source_target_pairs={{0,64},{2,68},{4,72},{6,76},{8,80},{10,84},{12,88},{14,92},{16,66}... | collective-permute-start | bytes 98312 | tf_op jit(solution)/shard_map/ppermute | solution.py:340
  8.4 17.0 %collective-permute-start.1 = (bf16[64,1280]{1,0:T(8,128)(2,1)}, bf16[64,1280]{1,0:T(8,128)(2,1)S(1)}, u32[]{:S(2)}, u32[]{:S(2)}) collective-permute-start(bf16[64,1280]{1,0:T(8,128)(2,1)} %get-tuple-element.57), channel_id=1, source_target_pairs={{0,64},{2,68},{4,72},{6,76},{8,80},{10,84},{12,88},{14,92},{16,66}... | collective-permute-start | bytes 491528 | tf_op jit(solution)/shard_map/ppermute | solution.py:340
  15.7 5.7 %collective-permute-start.3 = (bf16[64,128]{1,0:T(8,128)(2,1)S(1)}, bf16[64,128]{1,0:T(8,128)(2,1)S(1)}, u32[]{:S(2)}, u32[]{:S(2)}) collective-permute-start(bf16[64,128]{1,0:T(8,128)(2,1)S(1)} %get-tuple-element.111), channel_id=1, source_target_pairs={{68,72},{72,68},{76,80},{80,76},{84,88},{88,84},{92,66},{66,92},{7... | collective-permute-start | bytes 49160 | tf_op jit(solution)/shard_map/ppermute | solution.py:340
  20.0 3.4 %collective-permute-start.2 = (bf16[64,128]{1,0:T(8,128)(2,1)S(1)}, bf16[64,128]{1,0:T(8,128)(2,1)S(1)}, u32[]{:S(2)}, u32[]{:S(2)}) collective-permute-start(bf16[64,128]{1,0:T(8,128)(2,1)S(1)} %get-tuple-element.112), channel_id=1, source_target_pairs={{64,68},{68,64},{72,76},{76,72},{80,84},{84,80},{88,92},{92,88},{6... | collective-permute-start | bytes 49160 | tf_op jit(solution)/shard_map/ppermute | solution.py:340
  23.4 3.3 %collective-permute-start.5 = (bf16[64,128]{1,0:T(8,128)(2,1)S(1)}, bf16[64,128]{1,0:T(8,128)(2,1)S(1)}, u32[]{:S(2)}, u32[]{:S(2)}) collective-permute-start(bf16[64,128]{1,0:T(8,128)(2,1)S(1)} %get-tuple-element.99), channel_id=1, source_target_pairs={{66,0},{0,66},{70,4},{4,70},{74,8},{8,74},{78,12},{12,78},{82,16},... | collective-permute-start | bytes 49160 | tf_op jit(solution)/shard_map/ppermute | solution.py:340
  23.5 3.2 %collective-permute-start.4 = (bf16[64,128]{1,0:T(8,128)(2,1)S(1)}, bf16[64,128]{1,0:T(8,128)(2,1)S(1)}, u32[]{:S(2)}, u32[]{:S(2)}) collective-permute-start(bf16[64,128]{1,0:T(8,128)(2,1)S(1)} %get-tuple-element.100), channel_id=1, source_target_pairs={{64,66},{66,64},{68,70},{70,68},{72,74},{74,72},{76,78},{78,76},{8... | collective-permute-start | bytes 49160 | tf_op jit(solution)/shard_map/ppermute | solution.py:340
  26.6 0.9 copy-start.1
  27.5 8.1 %copy-start = (bf16[64,576]{1,0:T(8,128)(2,1)S(1)}, bf16[64,576]{1,0:T(8,128)(2,1)}, u32[]{:S(2)}) copy-start(bf16[64,576]{1,0:T(8,128)(2,1)} %get-tuple-element.68.two.w) | copy-start | bytes 221188
  27.5 8.1 %copy-start.2 = (bf16[64,256]{1,0:T(8,128)(2,1)S(1)}, bf16[64,256]{1,0:T(8,128)(2,1)}, u32[]{:S(2)}) copy-start(bf16[64,256]{1,0:T(8,128)(2,1)} %get-tuple-element.69.down.refs_4_) | copy-start | bytes 98308
  28.8 4.5 %collective-permute-start.7 = (bf16[64,128]{1,0:T(8,128)(2,1)S(1)}, bf16[64,128]{1,0:T(8,128)(2,1)S(1)}, u32[]{:S(2)}, u32[]{:S(2)}) collective-permute-start(bf16[64,128]{1,0:T(8,128)(2,1)S(1)} %get-tuple-element.109), channel_id=1, source_target_pairs={{68,72},{72,68},{76,80},{80,76},{84,88},{88,84},{92,66},{66,92},{7... | collective-permute-start | bytes 49160 | tf_op jit(solution)/shard_map/ppermute | solution.py:340
  30.7 2.6 %collective-permute-start.6 = (bf16[64,128]{1,0:T(8,128)(2,1)S(1)}, bf16[64,128]{1,0:T(8,128)(2,1)S(1)}, u32[]{:S(2)}, u32[]{:S(2)}) collective-permute-start(bf16[64,128]{1,0:T(8,128)(2,1)S(1)} %get-tuple-element.110), channel_id=1, source_target_pairs={{64,68},{68,64},{72,76},{76,72},{80,84},{84,80},{88,92},{92,88},{6... | collective-permute-start | bytes 49160 | tf_op jit(solution)/shard_map/ppermute | solution.py:340
  33.3 3.9 %collective-permute-start.9 = (bf16[64,128]{1,0:T(8,128)(2,1)S(1)}, bf16[64,128]{1,0:T(8,128)(2,1)S(1)}, u32[]{:S(2)}, u32[]{:S(2)}) collective-permute-start(bf16[64,128]{1,0:T(8,128)(2,1)S(1)} %get-tuple-element.97), channel_id=1, source_target_pairs={{66,0},{0,66},{70,4},{4,70},{74,8},{8,74},{78,12},{12,78},{82,16},... | collective-permute-start | bytes 49160 | tf_op jit(solution)/shard_map/ppermute | solution.py:340
  35.7 1.6 %collective-permute-start.8 = (bf16[64,128]{1,0:T(8,128)(2,1)S(1)}, bf16[64,128]{1,0:T(8,128)(2,1)S(1)}, u32[]{:S(2)}, u32[]{:S(2)}) collective-permute-start(bf16[64,128]{1,0:T(8,128)(2,1)S(1)} %get-tuple-element.98), channel_id=1, source_target_pairs={{64,66},{66,64},{68,70},{70,68},{72,74},{74,72},{76,78},{78,76},{8... | collective-permute-start | bytes 49160 | tf_op jit(solution)/shard_map/ppermute | solution.py:340
  39.1 3.3 %collective-permute-start.11 = (bf16[64,128]{1,0:T(8,128)(2,1)S(1)}, bf16[64,128]{1,0:T(8,128)(2,1)S(1)}, u32[]{:S(2)}, u32[]{:S(2)}) collective-permute-start(bf16[64,128]{1,0:T(8,128)(2,1)S(1)} %get-tuple-element.107), channel_id=1, source_target_pairs={{66,0},{0,66},{70,4},{4,70},{74,8},{8,74},{78,12},{12,78},{82,16},... | collective-permute-start | bytes 49160 | tf_op jit(solution)/shard_map/ppermute | solution.py:340
  40.8 1.6 %collective-permute-start.10 = (bf16[64,128]{1,0:T(8,128)(2,1)S(1)}, bf16[64,128]{1,0:T(8,128)(2,1)S(1)}, u32[]{:S(2)}, u32[]{:S(2)}) collective-permute-start(bf16[64,128]{1,0:T(8,128)(2,1)S(1)} %get-tuple-element.108), channel_id=1, source_target_pairs={{64,66},{66,64},{68,70},{70,68},{72,74},{74,72},{76,78},{78,76},{8... | collective-permute-start | bytes 49160 | tf_op jit(solution)/shard_map/ppermute | solution.py:340
  42.4 4.5 %collective-permute-start.13 = (bf16[64,128]{1,0:T(8,128)(2,1)S(1)}, bf16[64,128]{1,0:T(8,128)(2,1)S(1)}, u32[]{:S(2)}, u32[]{:S(2)}) collective-permute-start(bf16[64,128]{1,0:T(8,128)(2,1)S(1)} %get-tuple-element.103), channel_id=1, source_target_pairs={{68,72},{72,68},{76,80},{80,76},{84,88},{88,84},{92,66},{66,92},{7... | collective-permute-start | bytes 49160 | tf_op jit(solution)/shard_map/ppermute | solution.py:340
  44.1 2.9 %collective-permute-start.12 = (bf16[64,128]{1,0:T(8,128)(2,1)S(1)}, bf16[64,128]{1,0:T(8,128)(2,1)S(1)}, u32[]{:S(2)}, u32[]{:S(2)}) collective-permute-start(bf16[64,128]{1,0:T(8,128)(2,1)S(1)} %get-tuple-element.104), channel_id=1, source_target_pairs={{64,68},{68,64},{72,76},{76,72},{80,84},{84,80},{88,92},{92,88},{6... | collective-permute-start | bytes 49160 | tf_op jit(solution)/shard_map/ppermute | solution.py:340
  48.5 17.2 %all-to-all-start = ((bf16[16,48,128]{2,1,0:T(8,128)(2,1)}), bf16[16,48,128]{2,1,0:T(8,128)(2,1)S(1)}, u32[]{:S(2)}, u32[]{:S(2)}) async-start(bf16[16,48,128]{2,1,0:T(8,128)(2,1)} %bitcast.4), calls=%async_computation | async-start | bytes 393216 | tf_op jit(solution)/shard_map/all_to_all | solution.py:397
  56.3 3.5 %collective-permute-start.15 = (bf16[64,128]{1,0:T(8,128)(2,1)S(1)}, bf16[64,128]{1,0:T(8,128)(2,1)S(1)}, u32[]{:S(2)}, u32[]{:S(2)}) collective-permute-start(bf16[64,128]{1,0:T(8,128)(2,1)S(1)} %get-tuple-element.105), channel_id=1, source_target_pairs={{66,0},{0,66},{70,4},{4,70},{74,8},{8,74},{78,12},{12,78},{82,16},... | collective-permute-start | bytes 49160 | tf_op jit(solution)/shard_map/ppermute | solution.py:340
  56.6 3.2 %collective-permute-start.14 = (bf16[64,128]{1,0:T(8,128)(2,1)S(1)}, bf16[64,128]{1,0:T(8,128)(2,1)S(1)}, u32[]{:S(2)}, u32[]{:S(2)}) collective-permute-start(bf16[64,128]{1,0:T(8,128)(2,1)S(1)} %get-tuple-element.106), channel_id=1, source_target_pairs={{64,66},{66,64},{68,70},{70,68},{72,74},{74,72},{76,78},{78,76},{8... | collective-permute-start | bytes 49160 | tf_op jit(solution)/shard_map/ppermute | solution.py:340
  59.9 12.8 %collective-permute-start.17 = (bf16[64,128]{1,0:T(8,128)(2,1)S(1)}, bf16[64,128]{1,0:T(8,128)(2,1)S(1)}, u32[]{:S(2)}, u32[]{:S(2)}) collective-permute-start(bf16[64,128]{1,0:T(8,128)(2,1)S(1)} %get-tuple-element.101), channel_id=1, source_target_pairs={{68,72},{72,68},{76,80},{80,76},{84,88},{88,84},{92,66},{66,92},{7... | collective-permute-start | bytes 49160 | tf_op jit(solution)/shard_map/ppermute | solution.py:340
  62.5 10.2 %collective-permute-start.16 = (bf16[64,128]{1,0:T(8,128)(2,1)S(1)}, bf16[64,128]{1,0:T(8,128)(2,1)S(1)}, u32[]{:S(2)}, u32[]{:S(2)}) collective-permute-start(bf16[64,128]{1,0:T(8,128)(2,1)S(1)} %get-tuple-element.102), channel_id=1, source_target_pairs={{64,68},{68,64},{72,76},{76,72},{80,84},{84,80},{88,92},{92,88},{6... | collective-permute-start | bytes 49160 | tf_op jit(solution)/shard_map/ppermute | solution.py:340
  66.5 14.1 %all-to-all-start.1 = ((bf16[16,48,128]{2,1,0:T(8,128)(2,1)}), bf16[16,48,128]{2,1,0:T(8,128)(2,1)S(1)}, u32[]{:S(2)}, u32[]{:S(2)}) async-start(bf16[16,48,128]{2,1,0:T(8,128)(2,1)} %fold.2), calls=%async_computation.1 | async-start | bytes 393216 | tf_op jit(solution)/shard_map/all_to_all | solution.py:397
  73.3 12.5 %collective-permute-start.18 = (bf16[64,1280]{1,0:T(8,128)(2,1)S(1)}, bf16[64,1280]{1,0:T(8,128)(2,1)S(1)}, u32[]{:S(2)}, u32[]{:S(2)}) collective-permute-start(bf16[64,1280]{1,0:T(8,128)(2,1)S(1)} %last.1), channel_id=1, source_target_pairs={{64,0},{68,2},{72,4},{76,6},{80,8},{84,10},{88,12},{92,14},{66,16}... | collective-permute-start | bytes 491528 | tf_op jit(solution)/shard_map/ppermute | solution.py:340
  81.3 15.0 %all-to-all-start.2 = ((bf16[16,48,128]{2,1,0:T(8,128)(2,1)}), bf16[16,48,128]{2,1,0:T(8,128)(2,1)S(1)}, u32[]{:S(2)}, u32[]{:S(2)}) async-start(bf16[16,48,128]{2,1,0:T(8,128)(2,1)} %fold.3), calls=%async_computation.2 | async-start | bytes 393216 | tf_op jit(solution)/shard_map/all_to_all | solution.py:397

commit v3 on v2

--- a/solution.py
+++ b/solution.py
@@ -162,18 +162,13 @@
     return jnp.where(place == 72 * (m >> 4) + 2 * (m & 15), 1.0, 0.0).astype(BF)
 
 
-def load_body(codes_hbm, x_hbm, cot_hbm, one_hbm, two_hbm, down_hbm, edges, load, one, two, down, codes, sems):
-    later = [
-        pltpu.make_async_copy(one_hbm, one, sems.at[3]),
-        pltpu.make_async_copy(two_hbm, two, sems.at[4]),
-        pltpu.make_async_copy(down_hbm, down, sems.at[5]),
-    ]
+def load_body(codes_hbm, x_hbm, cot_hbm, edges, load, codes, sems):
     copies = [
         pltpu.make_async_copy(codes_hbm, codes, sems.at[0]),
         pltpu.make_async_copy(x_hbm, load.at[:, pl.ds(0, S * S)], sems.at[1]),
         pltpu.make_async_copy(cot_hbm, load.at[:, pl.ds(S * S, 256)], sems.at[2]),
     ]
-    for copy in copies + later:
+    for copy in copies:
         copy.start()
     lane, edge, along = lanes_of()[:3]
     y = jnp.where((edge & 1) == 0, jnp.where(edge == 0, 0, S - 1), along)
@@ -185,8 +180,6 @@
     row = lax.broadcasted_iota(jnp.int32, (C, SLOT), 0)
     value = jnp.where(row == 0, codes[0, 0], jnp.where(row == 1, codes[0, 1], jnp.where(row == 2, codes[0, 2], codes[0, 3])))
     edges[:, SLOT:] = value.astype(F32).astype(BF)
-    for copy in later:
-        copy.wait()
 
 
 def edge_row(facts, group):
@@ -205,7 +198,7 @@
 
 def send_inputs_body(edges, facts, *slots):
     codes = edges[:16, SLOT:].astype(F32).astype(jnp.int32)
-    row, column = lax.axis_index("core"), lax.axis_index("z") & 1
+    row, column = lax.axis_index("core"), 1 - (lax.axis_index("z") & 1)
     sides = [2 - 2 * row, 2 * row, 1 + 2 * column, 3 - 2 * column]
     for g, side in enumerate(sides):
         code = jnp.where(side == 2, codes[2:3, :], codes[3:4, :])
@@ -224,7 +217,8 @@
     source_two[...] = pick(sources(facts, 2), BASE, INNER)
 
 
-def spread_body(load, spread):
+def spread_body(load, one, spread, one_here):
+    one_here[...] = one[...]
     spread[...] = jnp.zeros_like(spread)
     for y in range(S):
         spread[:, BASE + PITCH * y : BASE + PITCH * y + S] = load[:, S * y : S * y + S]
@@ -333,7 +327,7 @@
 def home(t):
     row, column = t // ROW_TILES, t % ROW_TILES
     x, y = RING[row // 2]
-    return ((x * 2 + y) * 8 + column) * 2 + row % 2
+    return ((x * 2 + y) * 8 + 7 - column) * 2 + row % 2
 
 
 def move(value, pairs):
@@ -358,13 +352,15 @@
     return jnp.where(lane() < CORNER + 16, message, 0)
 
 
-def exchange(m):
+def exchange(m, done=()):
     r3 = swap(used(m[3]), 1, 1)
     r2 = swap(used(m[2]), 1, 0)
     corners = jnp.where(((lane() >> 2) & 1) == 0, r2, r3)
+    if done:
+        corners, done = lax.optimization_barrier((corners, done))
     r1 = swap(jnp.where(lane() < CORNER, m[1], corners), ROW_TILES, 1)
     r0 = swap(jnp.where(lane() < CORNER, m[0], corners), ROW_TILES, 0)
-    return r0, r1, r2, r3
+    return (r0, r1, r2, r3), done
 
 
 def north_south_back(m):
@@ -412,11 +408,11 @@
     col_full = pltpu.VMEM((9 * C, FULL), BF)
     dense = 2 * C * 9 * C * INNER
 
-    edges, load, conv_one, conv_two, down_weight = call(
+    edges, load = call(
         load_body,
-        [out((C, 2 * SLOT), BF), out((C, LOAD), BF), out((C, 9 * C), BF), out((C, 9 * C), BF), out((C, 4 * C), BF)],
-        [pltpu.SMEM((1, 4), jnp.int32), pltpu.SemaphoreType.DMA((6,))],
-        [seam_codes, x, cot, conv_one, conv_two, down_weight],
+        [out((C, 2 * SLOT), BF), out((C, LOAD), BF)],
+        [pltpu.SMEM((1, 4), jnp.int32), pltpu.SemaphoreType.DMA((3,))],
+        [seam_codes, x, cot],
         C * LOAD,
         "load",
         pltpu.HBM,
@@ -427,7 +423,7 @@
     facts, *sent = call(
         send_inputs_body, [out((8, SLOT), jnp.int32)] + slots, [], [edges], 2 * C * SLOT * 512, "send_inputs"
     )
-    rim_one, rim_two, source_one, source_two = call(
+    hots = call(
         hots_body,
         [out((FULL, 512), BF)] * 2 + [out((INNER, 512), BF)] * 2,
         [],
@@ -435,7 +431,11 @@
         dense,
         "hots",
     )
-    (spread,) = call(spread_body, [out((C, FULL), BF)], [], [load], C * FULL, "spread")
+    got, hots = exchange(sent[::-1], hots)
+    rim_one, rim_two, source_one, source_two = hots
+    spread, conv_one = call(
+        spread_body, [out((C, FULL), BF), out((C, 9 * C), BF)], [], [load, conv_one], C * FULL, "spread"
+    )
     upstream, grad_two, one_t, two_t = call(
         prepare_body,
         [out((C, INNER), BF), out((C, INNER), F32)] + [out((C, 9 * C), BF)] * 2,
@@ -444,7 +444,6 @@
         dense,
         "prepare",
     )
-    got = exchange(sent[::-1])
     taps_one, hidden, slope, *sent = call(
         first_body,
         [out((9 * C, INNER), BF), out((C, INNER), BF), out((C, INNER), F32)] + slots,
@@ -453,7 +452,7 @@
         2 * dense,
         "first",
     )
-    got = exchange(sent[::-1])
+    got, _ = exchange(sent[::-1])
     ext_two, hidden_two, delta_two, grad_mid, *sent = call(
         second_body,
         [out((C, FULL), BF), out((C, INNER), BF), out((C, INNER), BF), out((C, INNER), F32)] + slots,

time: 97.6 us -> 94.8 us (0.971)
  starting transfers between devices: 50 us -> 48 us
    ppermute x19, waiting for transfers between devices: 15.1 us -> 11.7 us  [move(): return lax.ppermute(value, TILE, pairs)]
    all_to_all x3, waiting for transfers between devices: 14.8 us -> 17.5 us  [trade(): return lax.all_to_all(parts, axes, 0, 0, tiled=True)]
    all_to_all x3, starting transfers between devices: 17.7 us -> 16.5 us  [trade(): return lax.all_to_all(parts, axes, 0, 0, tiled=True)]
  transfers between devices with their start and end apart: 22 -> 22, of which waited for: 14 -> 12; matrix products, arithmetic and copies ran while one was open for 1% -> 1% of each run, Pallas kernels for 7% -> 7%
where the time goes in v3:
time: 94.8 us; the launch traced here: 94.3 us
  starting transfers between devices  48 us (51%)
  waiting for transfers between devices  29.3 us (31%)
  Pallas kernels  14 us (15%)
  local copies, waits for them, and re-layouts  2.17 us (2%)
    ppermute x19, starting transfers between devices, move(): return lax.ppermute(value, TILE, pairs)  31.5 us
    all_to_all x3, waiting for transfers between devices, trade(): return lax.all_to_all(parts, axes, 0, 0, tiled=True)  17.5 us
    all_to_all x3, starting transfers between devices, trade(): return lax.all_to_all(parts, axes, 0, 0, tiled=True)  16.5 us
    pallas_call x14, Pallas kernels, call(): pl.pallas_call(body, out_shape=outs, in_specs=specs, out_specs=[pl.BlockS...  14 us
    ppermute x19, waiting for transfers between devices, move(): return lax.ppermute(value, TILE, pairs)  11.7 us
  transfers between devices with their start and end apart: 22, of which 12 were waited for; matrix products, arithmetic and copies ran while one was open for 1% of the time, Pallas kernels for 7%

profile of v3, /device:TPU:1, one launch (start us, length us, event | category | flops | bytes accessed | tf_op | source)
XLA Modules:
  0.0 94.3 jit_solution(9540154423257327207)
XLA Ops:
  0.6 1.7 %load.1 = (bf16[64,256]{1,0:T(8,128)(2,1)}, bf16[64,1280]{1,0:T(8,128)(2,1)}) custom-call(s32[1,4]{1,0:T(1,128)} %codes_hbm.1, bf16[64,1024]{1,0:T(8,128)(2,1)} %bitcast.9, bf16[64,256]{1,0:T(8,128)(2,1)} %bitcast.10), custom_call_target="tpu_custom_call" | custom-call | flops 81920 | bytes 360464 | tf_op jit(solution)/shard_map/load/pallas_call | solution.py:34
  2.4 8.4 %collective-permute-start = (bf16[64,256]{1,0:T(8,128)(2,1)}, bf16[64,256]{1,0:T(8,128)(2,1)S(1)}, u32[]{:S(2)}, u32[]{:S(2)}) collective-permute-start(bf16[64,256]{1,0:T(8,128)(2,1)} %get-tuple-element.55), channel_id=1, source_target_pairs={{0,92},{2,88},{4,84},{6,80},{8,76},{10,72},{12,68},{14,64},{16,94}... | collective-permute-start | bytes 98312 | tf_op jit(solution)/shard_map/ppermute | solution.py:334
  10.8 1.4 %collective-permute-start.3 = (bf16[64,1280]{1,0:T(8,128)(2,1)}, bf16[64,1280]{1,0:T(8,128)(2,1)S(1)}, u32[]{:S(2)}, u32[]{:S(2)}) collective-permute-start(bf16[64,1280]{1,0:T(8,128)(2,1)} %get-tuple-element.67), channel_id=1, source_target_pairs={{0,92},{2,88},{4,84},{6,80},{8,76},{10,72},{12,68},{14,64},{16,94}... | collective-permute-start | bytes 491528 | tf_op jit(solution)/shard_map/ppermute | solution.py:334
  12.4 5.8 %collective-permute-start.2 = (bf16[64,128]{1,0:T(8,128)(2,1)S(1)}, bf16[64,128]{1,0:T(8,128)(2,1)S(1)}, u32[]{:S(2)}, u32[]{:S(2)}) collective-permute-start(bf16[64,128]{1,0:T(8,128)(2,1)S(1)} %get-tuple-element.119), channel_id=1, source_target_pairs={{88,84},{84,88},{80,76},{76,80},{72,68},{68,72},{64,94},{94,64},{9... | collective-permute-start | bytes 49160 | tf_op jit(solution)/shard_map/ppermute | solution.py:334
  18.2 1.1 %hots.1 = (bf16[1408,512]{1,0:T(8,128)(2,1)S(1)}, bf16[1408,512]{1,0:T(8,128)(2,1)S(1)}, bf16[1152,512]{1,0:T(8,128)(2,1)S(1)}, bf16[1152,512]{1,0:T(8,128)(2,1)S(1)}) custom-call(s32[8,128]{1,0:T(8,128)S(1)} %get-tuple-element.58.facts), custom_call_target="tpu_custom_call" | custom-call | flops 84934656 | bytes 5246976 | tf_op jit(solution)/shard_map/hots/pallas_call | solution.py:34
  19.6 1.2 %collective-permute-done.1.r2 = bf16[64,128]{1,0:T(8,128)(2,1)S(1)} collective-permute-done((bf16[64,128]{1,0:T(8,128)(2,1)S(1)}, bf16[64,128]{1,0:T(8,128)(2,1)S(1)}, u32[]{:S(2)}, u32[]{:S(2)}) %collective-permute-start.1) | collective-permute-done | bytes 16416 | tf_op jit(solution)/shard_map/ppermute | solution.py:334
  20.8 1.3 %collective-permute-start.5 = (bf16[64,128]{1,0:T(8,128)(2,1)S(1)}, bf16[64,128]{1,0:T(8,128)(2,1)S(1)}, u32[]{:S(2)}, u32[]{:S(2)}) collective-permute-start(bf16[64,128]{1,0:T(8,128)(2,1)S(1)} %get-tuple-element.111), channel_id=1, source_target_pairs={{94,28},{28,94},{90,24},{24,90},{86,20},{20,86},{82,16},{16,82},{7... | collective-permute-start | bytes 49160 | tf_op jit(solution)/shard_map/ppermute | solution.py:334
  22.1 0.9 copy-done.2
  24.1 1.2 %first.1 = (bf16[576,1152]{1,0:T(8,128)(2,1)S(1)}, bf16[64,1152]{1,0:T(8,128)(2,1)S(1)}, f32[64,1152]{1,0:T(8,128)S(1)}, bf16[64,128]{1,0:T(8,128)(2,1)S(1)}, bf...) custom-call(bf16[1408,512]{1,0:T(8,128)(2,1)S(1)} %get-tuple-element.64.rim, ...), custom_call_target="tpu_custom_call" | custom-call | flops 169869312 | bytes 4775936 | tf_op jit(solution)/shard_map/first/pallas_call | solution.py:34
  25.3 3.7 %collective-permute-start.7 = (bf16[64,128]{1,0:T(8,128)(2,1)S(1)}, bf16[64,128]{1,0:T(8,128)(2,1)S(1)}, u32[]{:S(2)}, u32[]{:S(2)}) collective-permute-start(bf16[64,128]{1,0:T(8,128)(2,1)S(1)} %get-tuple-element.117), channel_id=1, source_target_pairs={{88,84},{84,88},{80,76},{76,80},{72,68},{68,72},{64,94},{94,64},{9... | collective-permute-start | bytes 49160 | tf_op jit(solution)/shard_map/ppermute | solution.py:334
  29.0 1.7 %collective-permute-done.7.r3 = bf16[64,128]{1,0:T(8,128)(2,1)S(1)} collective-permute-done((bf16[64,128]{1,0:T(8,128)(2,1)S(1)}, bf16[64,128]{1,0:T(8,128)(2,1)S(1)}, u32[]{:S(2)}, u32[]{:S(2)}) %collective-permute-start.7) | collective-permute-done | bytes 16416 | tf_op jit(solution)/shard_map/ppermute | solution.py:334
  30.7 0.9 collective-permute-done.6.r2
  31.6 1.0 %collective-permute-start.9 = (bf16[64,128]{1,0:T(8,128)(2,1)S(1)}, bf16[64,128]{1,0:T(8,128)(2,1)S(1)}, u32[]{:S(2)}, u32[]{:S(2)}) collective-permute-start(bf16[64,128]{1,0:T(8,128)(2,1)S(1)} %get-tuple-element.105), channel_id=1, source_target_pairs={{94,28},{28,94},{90,24},{24,90},{86,20},{20,86},{82,16},{16,82},{7... | collective-permute-start | bytes 49160 | tf_op jit(solution)/shard_map/ppermute | solution.py:334
  32.6 1.3 %prepare.1 = (bf16[64,1152]{1,0:T(8,128)(2,1)S(1)}, f32[64,1152]{1,0:T(8,128)S(1)}, bf16[64,576]{1,0:T(8,128)(2,1)S(1)}, bf16[64,576]{1,0:T(8,128)(2,1)S(1)}) custom-call(bf16[64,1280]{1,0:T(8,128)(2,1)S(1)} %collective-permute-done.3.load, bf16[64,256]{1,0:T(8,128)(2,1)S(1)} %copy-done.1, bf16[64,576]{1,0:T(8,128)(2,1)S(1)} %get-tuple-element.72.w.one, ...), custom_call_target="tpu_custom_call" | custom-call | flops 84934656 | bytes 933888 | tf_op jit(solution)/shard_map/prepare/pallas_call | solution.py:34
  33.9 0.9 collective-permute-done.9.r1
  34.9 1.9 %second.1 = (bf16[64,1408]{1,0:T(8,128)(2,1)S(1)}, bf16[64,1152]{1,0:T(8,128)(2,1)S(1)}, bf16[64,1152]{1,0:T(8,128)(2,1)S(1)}, f32[64,1152]{1,0:T(8,128)S(1)}, b...) custom-call(bf16[1408,512]{1,0:T(8,128)(2,1)S(1)} %get-tuple-element, ...), custom_call_target="tpu_custom_call" | custom-call | flops 254803968 | bytes 2932736 | tf_op jit(solution)/shard_map/second/pallas_call | solution.py:34
  36.7 1.0 %collective-permute-start.11 = (bf16[64,128]{1,0:T(8,128)(2,1)S(1)}, bf16[64,128]{1,0:T(8,128)(2,1)S(1)}, u32[]{:S(2)}, u32[]{:S(2)}) collective-permute-start(bf16[64,128]{1,0:T(8,128)(2,1)S(1)} %get-tuple-element.115), channel_id=1, source_target_pairs={{94,28},{28,94},{90,24},{24,90},{86,20},{20,86},{82,16},{16,82},{7... | collective-permute-start | bytes 49160 | tf_op jit(solution)/shard_map/ppermute | solution.py:334
  37.7 2.3 %collective-permute-done.11.refs_3_ = bf16[64,128]{1,0:T(8,128)(2,1)S(1)} collective-permute-done((bf16[64,128]{1,0:T(8,128)(2,1)S(1)}, bf16[64,128]{1,0:T(8,128)(2,1)S(1)}, u32[]{:S(2)}, u32[]{:S(2)}) %collective-permute-start.11) | collective-permute-done | bytes 16416 | tf_op jit(solution)/shard_map/ppermute | solution.py:334
  40.0 3.0 %collective-permute-start.13 = (bf16[64,128]{1,0:T(8,128)(2,1)S(1)}, bf16[64,128]{1,0:T(8,128)(2,1)S(1)}, u32[]{:S(2)}, u32[]{:S(2)}) collective-permute-start(bf16[64,128]{1,0:T(8,128)(2,1)S(1)} %get-tuple-element.109), channel_id=1, source_target_pairs={{88,84},{84,88},{80,76},{76,80},{72,68},{68,72},{64,94},{94,64},{9... | collective-permute-start | bytes 49160 | tf_op jit(solution)/shard_map/ppermute | solution.py:334
  43.0 1.0 %second_sums.1 = (bf16[64,256]{1,0:T(8,128)(2,1)S(1)}, f32[64,576]{1,0:T(8,128)S(1)}, f32[64,256]{1,0:T(8,128)S(1)}) custom-call(bf16[64,1408]{1,0:T(8,128)(2,1)S(1)} %get-tuple-element.87.refs_0_, bf16[64,1152]{1,0:T(8,128)(2,1)S(1)} %get-tuple-element.88.refs_1_, bf16[64,1152]{1,0:T(8,128)(2,1)S(1)} %get-tuple-element.89.refs_2_, ...), custom_call_target="tpu_custom_call" | custom-call | flops 169869312 | bytes 901120 | tf_op jit(solution)/shard_map/second_sums/pallas_call | solution.py:34
  44.0 1.6 %collective-permute-done.13.refs_5_ = bf16[64,128]{1,0:T(8,128)(2,1)S(1)} collective-permute-done((bf16[64,128]{1,0:T(8,128)(2,1)S(1)}, bf16[64,128]{1,0:T(8,128)(2,1)S(1)}, u32[]{:S(2)}, u32[]{:S(2)}) %collective-permute-start.13) | collective-permute-done | bytes 16416 | tf_op jit(solution)/shard_map/ppermute | solution.py:334
  45.5 1.6 %third.1 = (bf16[64,1152]{1,0:T(8,128)(2,1)S(1)}, bf16[768,128]{1,0:T(8,128)(2,1)}) custom-call(bf16[1152,512]{1,0:T(8,128)(2,1)S(1)} %get-tuple-element.65.source.refs_0_, f32[64,1152]{1,0:T(8,128)S(1)} %get-tuple-element.80.refs_1_, bf16[64,128]{1,0:T(8,128)(2,1)S(1)} %collective-permute-done.10.refs_2_, ...), custom_call_target="tpu_custom_call" | custom-call | flops 169869312 | bytes 3719168 | tf_op jit(solution)/shard_map/third/pallas_call | solution.py:34
  47.1 6.1 %all-to-all-start = ((bf16[16,48,128]{2,1,0:T(8,128)(2,1)}), bf16[16,48,128]{2,1,0:T(8,128)(2,1)S(1)}, u32[]{:S(2)}, u32[]{:S(2)}) async-start(bf16[16,48,128]{2,1,0:T(8,128)(2,1)} %bitcast.4), calls=%async_computation | async-start | bytes 393216 | tf_op jit(solution)/shard_map/all_to_all | solution.py:393
  53.2 0.9 fourth.1
  54.2 1.5 %collective-permute-start.15 = (bf16[64,128]{1,0:T(8,128)(2,1)S(1)}, bf16[64,128]{1,0:T(8,128)(2,1)S(1)}, u32[]{:S(2)}, u32[]{:S(2)}) collective-permute-start(bf16[64,128]{1,0:T(8,128)(2,1)S(1)} %get-tuple-element.113), channel_id=1, source_target_pairs={{94,28},{28,94},{90,24},{24,90},{86,20},{20,86},{82,16},{16,82},{7... | collective-permute-start | bytes 49160 | tf_op jit(solution)/shard_map/ppermute | solution.py:334
  55.6 2.1 %collective-permute-done.15.r1 = bf16[64,128]{1,0:T(8,128)(2,1)S(1)} collective-permute-done((bf16[64,128]{1,0:T(8,128)(2,1)S(1)}, bf16[64,128]{1,0:T(8,128)(2,1)S(1)}, u32[]{:S(2)}, u32[]{:S(2)}) %collective-permute-start.15) | collective-permute-done | bytes 16416 | tf_op jit(solution)/shard_map/ppermute | solution.py:334
  57.7 3.8 %collective-permute-start.17 = (bf16[64,128]{1,0:T(8,128)(2,1)S(1)}, bf16[64,128]{1,0:T(8,128)(2,1)S(1)}, u32[]{:S(2)}, u32[]{:S(2)}) collective-permute-start(bf16[64,128]{1,0:T(8,128)(2,1)S(1)} %get-tuple-element.107), channel_id=1, source_target_pairs={{88,84},{84,88},{80,76},{76,80},{72,68},{68,72},{64,94},{94,64},{9... | collective-permute-start | bytes 49160 | tf_op jit(solution)/shard_map/ppermute | solution.py:334
  61.5 2.1 %all-to-all-done.parts = bf16[16,48,128]{2,1,0:T(8,128)(2,1)S(1)} async-done(((bf16[16,48,128]{2,1,0:T(8,128)(2,1)}), bf16[16,48,128]{2,1,0:T(8,128)(2,1)S(1)}, u32[]{:S(2)}, u32[]{:S(2)}) %all-to-all-start) | async-done | bytes 196640 | tf_op jit(solution)/shard_map/all_to_all | solution.py:393
  64.3 5.5 %all-to-all-start.1 = ((bf16[16,48,128]{2,1,0:T(8,128)(2,1)}), bf16[16,48,128]{2,1,0:T(8,128)(2,1)S(1)}, u32[]{:S(2)}, u32[]{:S(2)}) async-start(bf16[16,48,128]{2,1,0:T(8,128)(2,1)} %fold.2), calls=%async_computation.1 | async-start | bytes 393216 | tf_op jit(solution)/shard_map/all_to_all | solution.py:393
  71.3 6.4 %all-to-all-done.1.parts = bf16[16,48,128]{2,1,0:T(8,128)(2,1)S(1)} async-done(((bf16[16,48,128]{2,1,0:T(8,128)(2,1)}), bf16[16,48,128]{2,1,0:T(8,128)(2,1)S(1)}, u32[]{:S(2)}, u32[]{:S(2)}) %all-to-all-start.1) | async-done | bytes 196640 | tf_op jit(solution)/shard_map/all_to_all | solution.py:393
  78.4 4.9 %all-to-all-start.2 = ((bf16[16,48,128]{2,1,0:T(8,128)(2,1)}), bf16[16,48,128]{2,1,0:T(8,128)(2,1)S(1)}, u32[]{:S(2)}, u32[]{:S(2)}) async-start(bf16[16,48,128]{2,1,0:T(8,128)(2,1)} %fold.3), calls=%async_computation.2 | async-start | bytes 393216 | tf_op jit(solution)/shard_map/all_to_all | solution.py:393
  84.5 9.0 %all-to-all-done.2 = bf16[16,48,128]{2,1,0:T(8,128)(2,1)S(1)} async-done(((bf16[16,48,128]{2,1,0:T(8,128)(2,1)}), bf16[16,48,128]{2,1,0:T(8,128)(2,1)S(1)}, u32[]{:S(2)}, u32[]{:S(2)}) %all-to-all-start.2) | async-done | bytes 196640 | tf_op jit(solution)/shard_map/all_to_all | solution.py:393
  (46 shorter events, 6.8 us)
Async XLA Ops:
  2.4 9.9 %collective-permute-start = (bf16[64,256]{1,0:T(8,128)(2,1)}, bf16[64,256]{1,0:T(8,128)(2,1)S(1)}, u32[]{:S(2)}, u32[]{:S(2)}) collective-permute-start(bf16[64,256]{1,0:T(8,128)(2,1)} %get-tuple-element.55), channel_id=1, source_target_pairs={{0,92},{2,88},{4,84},{6,80},{8,76},{10,72},{12,68},{14,64},{16,94}... | collective-permute-start | bytes 98312 | tf_op jit(solution)/shard_map/ppermute | solution.py:334
  10.8 11.3 %collective-permute-start.3 = (bf16[64,1280]{1,0:T(8,128)(2,1)}, bf16[64,1280]{1,0:T(8,128)(2,1)S(1)}, u32[]{:S(2)}, u32[]{:S(2)}) collective-permute-start(bf16[64,1280]{1,0:T(8,128)(2,1)} %get-tuple-element.67), channel_id=1, source_target_pairs={{0,92},{2,88},{4,84},{6,80},{8,76},{10,72},{12,68},{14,64},{16,94}... | collective-permute-start | bytes 491528 | tf_op jit(solution)/shard_map/ppermute | solution.py:334
  12.4 7.2 %collective-permute-start.2 = (bf16[64,128]{1,0:T(8,128)(2,1)S(1)}, bf16[64,128]{1,0:T(8,128)(2,1)S(1)}, u32[]{:S(2)}, u32[]{:S(2)}) collective-permute-start(bf16[64,128]{1,0:T(8,128)(2,1)S(1)} %get-tuple-element.119), channel_id=1, source_target_pairs={{88,84},{84,88},{80,76},{76,80},{72,68},{68,72},{64,94},{94,64},{9... | collective-permute-start | bytes 49160 | tf_op jit(solution)/shard_map/ppermute | solution.py:334
  18.2 2.6 %collective-permute-start.1 = (bf16[64,128]{1,0:T(8,128)(2,1)S(1)}, bf16[64,128]{1,0:T(8,128)(2,1)S(1)}, u32[]{:S(2)}, u32[]{:S(2)}) collective-permute-start(bf16[64,128]{1,0:T(8,128)(2,1)S(1)} %get-tuple-element.120), channel_id=1, source_target_pairs={{92,88},{88,92},{84,80},{80,84},{76,72},{72,76},{68,64},{64,68},{9... | collective-permute-start | bytes 49160 | tf_op jit(solution)/shard_map/ppermute | solution.py:334
  20.8 3.2 %collective-permute-start.5 = (bf16[64,128]{1,0:T(8,128)(2,1)S(1)}, bf16[64,128]{1,0:T(8,128)(2,1)S(1)}, u32[]{:S(2)}, u32[]{:S(2)}) collective-permute-start(bf16[64,128]{1,0:T(8,128)(2,1)S(1)} %get-tuple-element.111), channel_id=1, source_target_pairs={{94,28},{28,94},{90,24},{24,90},{86,20},{20,86},{82,16},{16,82},{7... | collective-permute-start | bytes 49160 | tf_op jit(solution)/shard_map/ppermute | solution.py:334
  22.1 2.0 %collective-permute-start.4 = (bf16[64,128]{1,0:T(8,128)(2,1)S(1)}, bf16[64,128]{1,0:T(8,128)(2,1)S(1)}, u32[]{:S(2)}, u32[]{:S(2)}) collective-permute-start(bf16[64,128]{1,0:T(8,128)(2,1)S(1)} %get-tuple-element.112), channel_id=1, source_target_pairs={{92,94},{94,92},{88,90},{90,88},{84,86},{86,84},{80,82},{82,80},{7... | collective-permute-start | bytes 49160 | tf_op jit(solution)/shard_map/ppermute | solution.py:334
  22.1 0.9 copy-start.2
  24.1 8.5 %copy-start = (bf16[64,576]{1,0:T(8,128)(2,1)S(1)}, bf16[64,576]{1,0:T(8,128)(2,1)}, u32[]{:S(2)}) copy-start(bf16[64,576]{1,0:T(8,128)(2,1)} %w.1) | copy-start | bytes 221188
  24.1 8.5 %copy-start.1 = (bf16[64,256]{1,0:T(8,128)(2,1)S(1)}, bf16[64,256]{1,0:T(8,128)(2,1)}, u32[]{:S(2)}) copy-start(bf16[64,256]{1,0:T(8,128)(2,1)} %refs_4_.1) | copy-start | bytes 98308
  25.3 5.4 %collective-permute-start.7 = (bf16[64,128]{1,0:T(8,128)(2,1)S(1)}, bf16[64,128]{1,0:T(8,128)(2,1)S(1)}, u32[]{:S(2)}, u32[]{:S(2)}) collective-permute-start(bf16[64,128]{1,0:T(8,128)(2,1)S(1)} %get-tuple-element.117), channel_id=1, source_target_pairs={{88,84},{84,88},{80,76},{76,80},{72,68},{68,72},{64,94},{94,64},{9... | collective-permute-start | bytes 49160 | tf_op jit(solution)/shard_map/ppermute | solution.py:334
  29.0 2.6 %collective-permute-start.6 = (bf16[64,128]{1,0:T(8,128)(2,1)S(1)}, bf16[64,128]{1,0:T(8,128)(2,1)S(1)}, u32[]{:S(2)}, u32[]{:S(2)}) collective-permute-start(bf16[64,128]{1,0:T(8,128)(2,1)S(1)} %get-tuple-element.118), channel_id=1, source_target_pairs={{92,88},{88,92},{84,80},{80,84},{76,72},{72,76},{68,64},{64,68},{9... | collective-permute-start | bytes 49160 | tf_op jit(solution)/shard_map/ppermute | solution.py:334
  31.6 3.3 %collective-permute-start.9 = (bf16[64,128]{1,0:T(8,128)(2,1)S(1)}, bf16[64,128]{1,0:T(8,128)(2,1)S(1)}, u32[]{:S(2)}, u32[]{:S(2)}) collective-permute-start(bf16[64,128]{1,0:T(8,128)(2,1)S(1)} %get-tuple-element.105), channel_id=1, source_target_pairs={{94,28},{28,94},{90,24},{24,90},{86,20},{20,86},{82,16},{16,82},{7... | collective-permute-start | bytes 49160 | tf_op jit(solution)/shard_map/ppermute | solution.py:334
  32.6 2.3 %collective-permute-start.8 = (bf16[64,128]{1,0:T(8,128)(2,1)S(1)}, bf16[64,128]{1,0:T(8,128)(2,1)S(1)}, u32[]{:S(2)}, u32[]{:S(2)}) collective-permute-start(bf16[64,128]{1,0:T(8,128)(2,1)S(1)} %get-tuple-element.106), channel_id=1, source_target_pairs={{92,94},{94,92},{88,90},{90,88},{84,86},{86,84},{80,82},{82,80},{7... | collective-permute-start | bytes 49160 | tf_op jit(solution)/shard_map/ppermute | solution.py:334
  36.7 3.3 %collective-permute-start.11 = (bf16[64,128]{1,0:T(8,128)(2,1)S(1)}, bf16[64,128]{1,0:T(8,128)(2,1)S(1)}, u32[]{:S(2)}, u32[]{:S(2)}) collective-permute-start(bf16[64,128]{1,0:T(8,128)(2,1)S(1)} %get-tuple-element.115), channel_id=1, source_target_pairs={{94,28},{28,94},{90,24},{24,90},{86,20},{20,86},{82,16},{16,82},{7... | collective-permute-start | bytes 49160 | tf_op jit(solution)/shard_map/ppermute | solution.py:334
  37.7 2.3 %collective-permute-start.10 = (bf16[64,128]{1,0:T(8,128)(2,1)S(1)}, bf16[64,128]{1,0:T(8,128)(2,1)S(1)}, u32[]{:S(2)}, u32[]{:S(2)}) collective-permute-start(bf16[64,128]{1,0:T(8,128)(2,1)S(1)} %get-tuple-element.116), channel_id=1, source_target_pairs={{92,94},{94,92},{88,90},{90,88},{84,86},{86,84},{80,82},{82,80},{7... | collective-permute-start | bytes 49160 | tf_op jit(solution)/shard_map/ppermute | solution.py:334
  40.0 5.5 %collective-permute-start.13 = (bf16[64,128]{1,0:T(8,128)(2,1)S(1)}, bf16[64,128]{1,0:T(8,128)(2,1)S(1)}, u32[]{:S(2)}, u32[]{:S(2)}) collective-permute-start(bf16[64,128]{1,0:T(8,128)(2,1)S(1)} %get-tuple-element.109), channel_id=1, source_target_pairs={{88,84},{84,88},{80,76},{76,80},{72,68},{68,72},{64,94},{94,64},{9... | collective-permute-start | bytes 49160 | tf_op jit(solution)/shard_map/ppermute | solution.py:334
  43.0 2.6 %collective-permute-start.12 = (bf16[64,128]{1,0:T(8,128)(2,1)S(1)}, bf16[64,128]{1,0:T(8,128)(2,1)S(1)}, u32[]{:S(2)}, u32[]{:S(2)}) collective-permute-start(bf16[64,128]{1,0:T(8,128)(2,1)S(1)} %get-tuple-element.110), channel_id=1, source_target_pairs={{92,88},{88,92},{84,80},{80,84},{76,72},{72,76},{68,64},{64,68},{9... | collective-permute-start | bytes 49160 | tf_op jit(solution)/shard_map/ppermute | solution.py:334
  47.1 16.5 %all-to-all-start = ((bf16[16,48,128]{2,1,0:T(8,128)(2,1)}), bf16[16,48,128]{2,1,0:T(8,128)(2,1)S(1)}, u32[]{:S(2)}, u32[]{:S(2)}) async-start(bf16[16,48,128]{2,1,0:T(8,128)(2,1)} %bitcast.4), calls=%async_computation | async-start | bytes 393216 | tf_op jit(solution)/shard_map/all_to_all | solution.py:393
  54.2 3.5 %collective-permute-start.15 = (bf16[64,128]{1,0:T(8,128)(2,1)S(1)}, bf16[64,128]{1,0:T(8,128)(2,1)S(1)}, u32[]{:S(2)}, u32[]{:S(2)}) collective-permute-start(bf16[64,128]{1,0:T(8,128)(2,1)S(1)} %get-tuple-element.113), channel_id=1, source_target_pairs={{94,28},{28,94},{90,24},{24,90},{86,20},{20,86},{82,16},{16,82},{7... | collective-permute-start | bytes 49160 | tf_op jit(solution)/shard_map/ppermute | solution.py:334
  55.6 2.1 %collective-permute-start.14 = (bf16[64,128]{1,0:T(8,128)(2,1)S(1)}, bf16[64,128]{1,0:T(8,128)(2,1)S(1)}, u32[]{:S(2)}, u32[]{:S(2)}) collective-permute-start(bf16[64,128]{1,0:T(8,128)(2,1)S(1)} %get-tuple-element.114), channel_id=1, source_target_pairs={{92,94},{94,92},{88,90},{90,88},{84,86},{86,84},{80,82},{82,80},{7... | collective-permute-start | bytes 49160 | tf_op jit(solution)/shard_map/ppermute | solution.py:334
  57.7 12.0 %collective-permute-start.17 = (bf16[64,128]{1,0:T(8,128)(2,1)S(1)}, bf16[64,128]{1,0:T(8,128)(2,1)S(1)}, u32[]{:S(2)}, u32[]{:S(2)}) collective-permute-start(bf16[64,128]{1,0:T(8,128)(2,1)S(1)} %get-tuple-element.107), channel_id=1, source_target_pairs={{88,84},{84,88},{80,76},{76,80},{72,68},{68,72},{64,94},{94,64},{9... | collective-permute-start | bytes 49160 | tf_op jit(solution)/shard_map/ppermute | solution.py:334
  61.5 8.3 %collective-permute-start.16 = (bf16[64,128]{1,0:T(8,128)(2,1)S(1)}, bf16[64,128]{1,0:T(8,128)(2,1)S(1)}, u32[]{:S(2)}, u32[]{:S(2)}) collective-permute-start(bf16[64,128]{1,0:T(8,128)(2,1)S(1)} %get-tuple-element.108), channel_id=1, source_target_pairs={{92,88},{88,92},{84,80},{80,84},{76,72},{72,76},{68,64},{64,68},{9... | collective-permute-start | bytes 49160 | tf_op jit(solution)/shard_map/ppermute | solution.py:334
  64.3 13.4 %all-to-all-start.1 = ((bf16[16,48,128]{2,1,0:T(8,128)(2,1)}), bf16[16,48,128]{2,1,0:T(8,128)(2,1)S(1)}, u32[]{:S(2)}, u32[]{:S(2)}) async-start(bf16[16,48,128]{2,1,0:T(8,128)(2,1)} %fold.2), calls=%async_computation.1 | async-start | bytes 393216 | tf_op jit(solution)/shard_map/all_to_all | solution.py:393
  70.4 12.8 %collective-permute-start.18 = (bf16[64,1280]{1,0:T(8,128)(2,1)S(1)}, bf16[64,1280]{1,0:T(8,128)(2,1)S(1)}, u32[]{:S(2)}, u32[]{:S(2)}) collective-permute-start(bf16[64,1280]{1,0:T(8,128)(2,1)S(1)} %last.1), channel_id=1, source_target_pairs={{92,0},{88,2},{84,4},{80,6},{76,8},{72,10},{68,12},{64,14},{94,16}... | collective-permute-start | bytes 491528 | tf_op jit(solution)/shard_map/ppermute | solution.py:334
  78.4 15.2 %all-to-all-start.2 = ((bf16[16,48,128]{2,1,0:T(8,128)(2,1)}), bf16[16,48,128]{2,1,0:T(8,128)(2,1)S(1)}, u32[]{:S(2)}, u32[]{:S(2)}) async-start(bf16[16,48,128]{2,1,0:T(8,128)(2,1)} %fold.3), calls=%async_computation.2 | async-start | bytes 393216 | tf_op jit(solution)/shard_map/all_to_all | solution.py:393

commit v4 on v3

--- a/solution.py
+++ b/solution.py
@@ -19,8 +19,8 @@
 PACKED = 12 * C
 TILE = ("x", "y", "z", "core")
 MEMBER = ("member",)
-NEAR = ("z", "core")
-FAR = ("x", "y", "member")
+NEAR = ("core", "z")
+FAR = ("member", "x", "y")
 LOAD = S * S + 256
 RING = ((1, 0), (0, 0), (0, 1), (1, 1), (2, 1), (3, 1), (3, 0), (2, 0))
 CORNER = 64

time: 94.8 us -> 91.8 us (0.968)
  waiting for transfers between devices: 29.3 us -> 21.5 us
  starting transfers between devices: 48 us -> 52.7 us
    all_to_all x3, waiting for transfers between devices: 17.5 us -> 9.74 us  [trade(): return lax.all_to_all(parts, axes, 0, 0, tiled=True)]
    ppermute x19, starting transfers between devices: 31.5 us -> 34.4 us  [move(): return lax.ppermute(value, TILE, pairs)]
    all_to_all x3, starting transfers between devices: 16.5 us -> 18.4 us  [trade(): return lax.all_to_all(parts, axes, 0, 0, tiled=True)]
  transfers between devices with their start and end apart: 22 -> 22, of which waited for: 12 -> 12; matrix products, arithmetic and copies ran while one was open for 1% -> 1% of each run, Pallas kernels for 7% -> 8%
where the time goes in v4:
time: 91.8 us; the launch traced here: 91.3 us
  starting transfers between devices  52.7 us (57%)
  waiting for transfers between devices  21.5 us (23%)
  Pallas kernels  14 us (15%)
  local copies, waits for them, and re-layouts  2.17 us (2%)
    ppermute x19, starting transfers between devices, move(): return lax.ppermute(value, TILE, pairs)  34.4 us
    all_to_all x3, starting transfers between devices, trade(): return lax.all_to_all(parts, axes, 0, 0, tiled=True)  18.4 us
    pallas_call x14, Pallas kernels, call(): pl.pallas_call(body, out_shape=outs, in_specs=specs, out_specs=[pl.BlockS...  14 us
    ppermute x19, waiting for transfers between devices, move(): return lax.ppermute(value, TILE, pairs)  11.8 us
    all_to_all x3, waiting for transfers between devices, trade(): return lax.all_to_all(parts, axes, 0, 0, tiled=True)  9.74 us
  transfers between devices with their start and end apart: 22, of which 12 were waited for; matrix products, arithmetic and copies ran while one was open for 1% of the time, Pallas kernels for 8%

profile of v4, /device:TPU:1, one launch (start us, length us, event | category | flops | bytes accessed | tf_op | source)
XLA Modules:
  0.0 91.3 jit_solution(10499851700583252863)
XLA Ops:
  0.6 1.7 %load.1 = (bf16[64,256]{1,0:T(8,128)(2,1)}, bf16[64,1280]{1,0:T(8,128)(2,1)}) custom-call(s32[1,4]{1,0:T(1,128)} %codes_hbm.1, bf16[64,1024]{1,0:T(8,128)(2,1)} %bitcast.9, bf16[64,256]{1,0:T(8,128)(2,1)} %bitcast.10), custom_call_target="tpu_custom_call" | custom-call | flops 81920 | bytes 360464 | tf_op jit(solution)/shard_map/load/pallas_call | solution.py:34
  2.4 8.4 %collective-permute-start = (bf16[64,256]{1,0:T(8,128)(2,1)}, bf16[64,256]{1,0:T(8,128)(2,1)S(1)}, u32[]{:S(2)}, u32[]{:S(2)}) collective-permute-start(bf16[64,256]{1,0:T(8,128)(2,1)} %get-tuple-element.55), channel_id=1, source_target_pairs={{0,92},{2,88},{4,84},{6,80},{8,76},{10,72},{12,68},{14,64},{16,94}... | collective-permute-start | bytes 98312 | tf_op jit(solution)/shard_map/ppermute | solution.py:334
  10.8 1.4 %collective-permute-start.3 = (bf16[64,1280]{1,0:T(8,128)(2,1)}, bf16[64,1280]{1,0:T(8,128)(2,1)S(1)}, u32[]{:S(2)}, u32[]{:S(2)}) collective-permute-start(bf16[64,1280]{1,0:T(8,128)(2,1)} %get-tuple-element.67), channel_id=1, source_target_pairs={{0,92},{2,88},{4,84},{6,80},{8,76},{10,72},{12,68},{14,64},{16,94}... | collective-permute-start | bytes 491528 | tf_op jit(solution)/shard_map/ppermute | solution.py:334
  12.4 5.8 %collective-permute-start.2 = (bf16[64,128]{1,0:T(8,128)(2,1)S(1)}, bf16[64,128]{1,0:T(8,128)(2,1)S(1)}, u32[]{:S(2)}, u32[]{:S(2)}) collective-permute-start(bf16[64,128]{1,0:T(8,128)(2,1)S(1)} %get-tuple-element.119), channel_id=1, source_target_pairs={{88,84},{84,88},{80,76},{76,80},{72,68},{68,72},{64,94},{94,64},{9... | collective-permute-start | bytes 49160 | tf_op jit(solution)/shard_map/ppermute | solution.py:334
  18.2 1.1 %hots.1 = (bf16[1408,512]{1,0:T(8,128)(2,1)S(1)}, bf16[1408,512]{1,0:T(8,128)(2,1)S(1)}, bf16[1152,512]{1,0:T(8,128)(2,1)S(1)}, bf16[1152,512]{1,0:T(8,128)(2,1)S(1)}) custom-call(s32[8,128]{1,0:T(8,128)S(1)} %get-tuple-element.58.facts), custom_call_target="tpu_custom_call" | custom-call | flops 84934656 | bytes 5246976 | tf_op jit(solution)/shard_map/hots/pallas_call | solution.py:34
  19.6 1.2 %collective-permute-done.1.r2 = bf16[64,128]{1,0:T(8,128)(2,1)S(1)} collective-permute-done((bf16[64,128]{1,0:T(8,128)(2,1)S(1)}, bf16[64,128]{1,0:T(8,128)(2,1)S(1)}, u32[]{:S(2)}, u32[]{:S(2)}) %collective-permute-start.1) | collective-permute-done | bytes 16416 | tf_op jit(solution)/shard_map/ppermute | solution.py:334
  20.8 1.3 %collective-permute-start.5 = (bf16[64,128]{1,0:T(8,128)(2,1)S(1)}, bf16[64,128]{1,0:T(8,128)(2,1)S(1)}, u32[]{:S(2)}, u32[]{:S(2)}) collective-permute-start(bf16[64,128]{1,0:T(8,128)(2,1)S(1)} %get-tuple-element.111), channel_id=1, source_target_pairs={{94,28},{28,94},{90,24},{24,90},{86,20},{20,86},{82,16},{16,82},{7... | collective-permute-start | bytes 49160 | tf_op jit(solution)/shard_map/ppermute | solution.py:334
  22.1 0.9 copy-done.2
  24.1 1.2 %first.1 = (bf16[576,1152]{1,0:T(8,128)(2,1)S(1)}, bf16[64,1152]{1,0:T(8,128)(2,1)S(1)}, f32[64,1152]{1,0:T(8,128)S(1)}, bf16[64,128]{1,0:T(8,128)(2,1)S(1)}, bf...) custom-call(bf16[1408,512]{1,0:T(8,128)(2,1)S(1)} %get-tuple-element.64.rim, ...), custom_call_target="tpu_custom_call" | custom-call | flops 169869312 | bytes 4775936 | tf_op jit(solution)/shard_map/first/pallas_call | solution.py:34
  25.3 3.7 %collective-permute-start.7 = (bf16[64,128]{1,0:T(8,128)(2,1)S(1)}, bf16[64,128]{1,0:T(8,128)(2,1)S(1)}, u32[]{:S(2)}, u32[]{:S(2)}) collective-permute-start(bf16[64,128]{1,0:T(8,128)(2,1)S(1)} %get-tuple-element.117), channel_id=1, source_target_pairs={{88,84},{84,88},{80,76},{76,80},{72,68},{68,72},{64,94},{94,64},{9... | collective-permute-start | bytes 49160 | tf_op jit(solution)/shard_map/ppermute | solution.py:334
  29.0 1.7 %collective-permute-done.7.r3 = bf16[64,128]{1,0:T(8,128)(2,1)S(1)} collective-permute-done((bf16[64,128]{1,0:T(8,128)(2,1)S(1)}, bf16[64,128]{1,0:T(8,128)(2,1)S(1)}, u32[]{:S(2)}, u32[]{:S(2)}) %collective-permute-start.7) | collective-permute-done | bytes 16416 | tf_op jit(solution)/shard_map/ppermute | solution.py:334
  30.7 0.9 collective-permute-done.6.r2
  31.6 1.0 %collective-permute-start.9 = (bf16[64,128]{1,0:T(8,128)(2,1)S(1)}, bf16[64,128]{1,0:T(8,128)(2,1)S(1)}, u32[]{:S(2)}, u32[]{:S(2)}) collective-permute-start(bf16[64,128]{1,0:T(8,128)(2,1)S(1)} %get-tuple-element.105), channel_id=1, source_target_pairs={{94,28},{28,94},{90,24},{24,90},{86,20},{20,86},{82,16},{16,82},{7... | collective-permute-start | bytes 49160 | tf_op jit(solution)/shard_map/ppermute | solution.py:334
  32.6 1.3 %prepare.1 = (bf16[64,1152]{1,0:T(8,128)(2,1)S(1)}, f32[64,1152]{1,0:T(8,128)S(1)}, bf16[64,576]{1,0:T(8,128)(2,1)S(1)}, bf16[64,576]{1,0:T(8,128)(2,1)S(1)}) custom-call(bf16[64,1280]{1,0:T(8,128)(2,1)S(1)} %collective-permute-done.3.load, bf16[64,256]{1,0:T(8,128)(2,1)S(1)} %copy-done.1, bf16[64,576]{1,0:T(8,128)(2,1)S(1)} %get-tuple-element.72.w.one, ...), custom_call_target="tpu_custom_call" | custom-call | flops 84934656 | bytes 933888 | tf_op jit(solution)/shard_map/prepare/pallas_call | solution.py:34
  33.9 0.9 %collective-permute-done.9.r1 = bf16[64,128]{1,0:T(8,128)(2,1)S(1)} collective-permute-done((bf16[64,128]{1,0:T(8,128)(2,1)S(1)}, bf16[64,128]{1,0:T(8,128)(2,1)S(1)}, u32[]{:S(2)}, u32[]{:S(2)}) %collective-permute-start.9) | collective-permute-done | bytes 16416 | tf_op jit(solution)/shard_map/ppermute | solution.py:334
  34.9 1.9 %second.1 = (bf16[64,1408]{1,0:T(8,128)(2,1)S(1)}, bf16[64,1152]{1,0:T(8,128)(2,1)S(1)}, bf16[64,1152]{1,0:T(8,128)(2,1)S(1)}, f32[64,1152]{1,0:T(8,128)S(1)}, b...) custom-call(bf16[1408,512]{1,0:T(8,128)(2,1)S(1)} %get-tuple-element, ...), custom_call_target="tpu_custom_call" | custom-call | flops 254803968 | bytes 2932736 | tf_op jit(solution)/shard_map/second/pallas_call | solution.py:34
  36.7 1.0 %collective-permute-start.11 = (bf16[64,128]{1,0:T(8,128)(2,1)S(1)}, bf16[64,128]{1,0:T(8,128)(2,1)S(1)}, u32[]{:S(2)}, u32[]{:S(2)}) collective-permute-start(bf16[64,128]{1,0:T(8,128)(2,1)S(1)} %get-tuple-element.115), channel_id=1, source_target_pairs={{94,28},{28,94},{90,24},{24,90},{86,20},{20,86},{82,16},{16,82},{7... | collective-permute-start | bytes 49160 | tf_op jit(solution)/shard_map/ppermute | solution.py:334
  37.7 2.3 %collective-permute-done.11.refs_3_ = bf16[64,128]{1,0:T(8,128)(2,1)S(1)} collective-permute-done((bf16[64,128]{1,0:T(8,128)(2,1)S(1)}, bf16[64,128]{1,0:T(8,128)(2,1)S(1)}, u32[]{:S(2)}, u32[]{:S(2)}) %collective-permute-start.11) | collective-permute-done | bytes 16416 | tf_op jit(solution)/shard_map/ppermute | solution.py:334
  40.0 3.0 %collective-permute-start.13 = (bf16[64,128]{1,0:T(8,128)(2,1)S(1)}, bf16[64,128]{1,0:T(8,128)(2,1)S(1)}, u32[]{:S(2)}, u32[]{:S(2)}) collective-permute-start(bf16[64,128]{1,0:T(8,128)(2,1)S(1)} %get-tuple-element.109), channel_id=1, source_target_pairs={{88,84},{84,88},{80,76},{76,80},{72,68},{68,72},{64,94},{94,64},{9... | collective-permute-start | bytes 49160 | tf_op jit(solution)/shard_map/ppermute | solution.py:334
  43.0 1.0 %second_sums.1 = (bf16[64,256]{1,0:T(8,128)(2,1)S(1)}, f32[64,576]{1,0:T(8,128)S(1)}, f32[64,256]{1,0:T(8,128)S(1)}) custom-call(bf16[64,1408]{1,0:T(8,128)(2,1)S(1)} %get-tuple-element.87.refs_0_, bf16[64,1152]{1,0:T(8,128)(2,1)S(1)} %get-tuple-element.88.refs_1_, bf16[64,1152]{1,0:T(8,128)(2,1)S(1)} %get-tuple-element.89.refs_2_, ...), custom_call_target="tpu_custom_call" | custom-call | flops 169869312 | bytes 901120 | tf_op jit(solution)/shard_map/second_sums/pallas_call | solution.py:34
  44.0 1.6 %collective-permute-done.13.refs_5_ = bf16[64,128]{1,0:T(8,128)(2,1)S(1)} collective-permute-done((bf16[64,128]{1,0:T(8,128)(2,1)S(1)}, bf16[64,128]{1,0:T(8,128)(2,1)S(1)}, u32[]{:S(2)}, u32[]{:S(2)}) %collective-permute-start.13) | collective-permute-done | bytes 16416 | tf_op jit(solution)/shard_map/ppermute | solution.py:334
  45.5 1.6 %third.1 = (bf16[64,1152]{1,0:T(8,128)(2,1)S(1)}, bf16[768,128]{1,0:T(8,128)(2,1)}) custom-call(bf16[1152,512]{1,0:T(8,128)(2,1)S(1)} %get-tuple-element.65.source.refs_0_, f32[64,1152]{1,0:T(8,128)S(1)} %get-tuple-element.80.refs_1_, bf16[64,128]{1,0:T(8,128)(2,1)S(1)} %collective-permute-done.10.refs_2_, ...), custom_call_target="tpu_custom_call" | custom-call | flops 169869312 | bytes 3719168 | tf_op jit(solution)/shard_map/third/pallas_call | solution.py:34
  47.1 6.2 %all-to-all-start = ((bf16[16,48,128]{2,1,0:T(8,128)(2,1)}), bf16[16,48,128]{2,1,0:T(8,128)(2,1)S(1)}, u32[]{:S(2)}, u32[]{:S(2)}) async-start(bf16[16,48,128]{2,1,0:T(8,128)(2,1)} %bitcast.4), calls=%async_computation | async-start | bytes 393216 | tf_op jit(solution)/shard_map/all_to_all | solution.py:393
  53.3 0.9 fourth.1
  54.2 1.5 %collective-permute-start.15 = (bf16[64,128]{1,0:T(8,128)(2,1)S(1)}, bf16[64,128]{1,0:T(8,128)(2,1)S(1)}, u32[]{:S(2)}, u32[]{:S(2)}) collective-permute-start(bf16[64,128]{1,0:T(8,128)(2,1)S(1)} %get-tuple-element.113), channel_id=1, source_target_pairs={{94,28},{28,94},{90,24},{24,90},{86,20},{20,86},{82,16},{16,82},{7... | collective-permute-start | bytes 49160 | tf_op jit(solution)/shard_map/ppermute | solution.py:334
  55.6 2.1 %collective-permute-done.15.r1 = bf16[64,128]{1,0:T(8,128)(2,1)S(1)} collective-permute-done((bf16[64,128]{1,0:T(8,128)(2,1)S(1)}, bf16[64,128]{1,0:T(8,128)(2,1)S(1)}, u32[]{:S(2)}, u32[]{:S(2)}) %collective-permute-start.15) | collective-permute-done | bytes 16416 | tf_op jit(solution)/shard_map/ppermute | solution.py:334
  57.7 3.7 %collective-permute-start.17 = (bf16[64,128]{1,0:T(8,128)(2,1)S(1)}, bf16[64,128]{1,0:T(8,128)(2,1)S(1)}, u32[]{:S(2)}, u32[]{:S(2)}) collective-permute-start(bf16[64,128]{1,0:T(8,128)(2,1)S(1)} %get-tuple-element.107), channel_id=1, source_target_pairs={{88,84},{84,88},{80,76},{76,80},{72,68},{68,72},{64,94},{94,64},{9... | collective-permute-start | bytes 49160 | tf_op jit(solution)/shard_map/ppermute | solution.py:334
  62.2 5.5 %all-to-all-start.1 = ((bf16[16,48,128]{2,1,0:T(8,128)(2,1)}), bf16[16,48,128]{2,1,0:T(8,128)(2,1)S(1)}, u32[]{:S(2)}, u32[]{:S(2)}) async-start(bf16[16,48,128]{2,1,0:T(8,128)(2,1)} %fold.2), calls=%async_computation.1 | async-start | bytes 393216 | tf_op jit(solution)/shard_map/all_to_all | solution.py:393
  68.4 3.7 %collective-permute-start.18 = (bf16[64,1280]{1,0:T(8,128)(2,1)S(1)}, bf16[64,1280]{1,0:T(8,128)(2,1)S(1)}, u32[]{:S(2)}, u32[]{:S(2)}) collective-permute-start(bf16[64,1280]{1,0:T(8,128)(2,1)S(1)} %last.1), channel_id=1, source_target_pairs={{92,0},{88,2},{84,4},{80,6},{76,8},{72,10},{68,12},{64,14},{94,16}... | collective-permute-start | bytes 491528 | tf_op jit(solution)/shard_map/ppermute | solution.py:334
  72.1 2.7 %all-to-all-done.1.parts = bf16[16,48,128]{2,1,0:T(8,128)(2,1)S(1)} async-done(((bf16[16,48,128]{2,1,0:T(8,128)(2,1)}), bf16[16,48,128]{2,1,0:T(8,128)(2,1)S(1)}, u32[]{:S(2)}, u32[]{:S(2)}) %all-to-all-start.1) | async-done | bytes 196640 | tf_op jit(solution)/shard_map/all_to_all | solution.py:393
  75.5 6.8 %all-to-all-start.2 = ((bf16[16,48,128]{2,1,0:T(8,128)(2,1)}), bf16[16,48,128]{2,1,0:T(8,128)(2,1)S(1)}, u32[]{:S(2)}, u32[]{:S(2)}) async-start(bf16[16,48,128]{2,1,0:T(8,128)(2,1)} %fold.3), calls=%async_computation.2 | async-start | bytes 393216 | tf_op jit(solution)/shard_map/all_to_all | solution.py:393
  83.5 7.0 %all-to-all-done.2 = bf16[16,48,128]{2,1,0:T(8,128)(2,1)S(1)} async-done(((bf16[16,48,128]{2,1,0:T(8,128)(2,1)}), bf16[16,48,128]{2,1,0:T(8,128)(2,1)S(1)}, u32[]{:S(2)}, u32[]{:S(2)}) %all-to-all-start.2) | async-done | bytes 196640 | tf_op jit(solution)/shard_map/all_to_all | solution.py:393
  (46 shorter events, 6.0 us)
Async XLA Ops:
  2.4 9.9 %collective-permute-start = (bf16[64,256]{1,0:T(8,128)(2,1)}, bf16[64,256]{1,0:T(8,128)(2,1)S(1)}, u32[]{:S(2)}, u32[]{:S(2)}) collective-permute-start(bf16[64,256]{1,0:T(8,128)(2,1)} %get-tuple-element.55), channel_id=1, source_target_pairs={{0,92},{2,88},{4,84},{6,80},{8,76},{10,72},{12,68},{14,64},{16,94}... | collective-permute-start | bytes 98312 | tf_op jit(solution)/shard_map/ppermute | solution.py:334
  10.8 11.3 %collective-permute-start.3 = (bf16[64,1280]{1,0:T(8,128)(2,1)}, bf16[64,1280]{1,0:T(8,128)(2,1)S(1)}, u32[]{:S(2)}, u32[]{:S(2)}) collective-permute-start(bf16[64,1280]{1,0:T(8,128)(2,1)} %get-tuple-element.67), channel_id=1, source_target_pairs={{0,92},{2,88},{4,84},{6,80},{8,76},{10,72},{12,68},{14,64},{16,94}... | collective-permute-start | bytes 491528 | tf_op jit(solution)/shard_map/ppermute | solution.py:334
  12.4 7.2 %collective-permute-start.2 = (bf16[64,128]{1,0:T(8,128)(2,1)S(1)}, bf16[64,128]{1,0:T(8,128)(2,1)S(1)}, u32[]{:S(2)}, u32[]{:S(2)}) collective-permute-start(bf16[64,128]{1,0:T(8,128)(2,1)S(1)} %get-tuple-element.119), channel_id=1, source_target_pairs={{88,84},{84,88},{80,76},{76,80},{72,68},{68,72},{64,94},{94,64},{9... | collective-permute-start | bytes 49160 | tf_op jit(solution)/shard_map/ppermute | solution.py:334
  18.2 2.6 %collective-permute-start.1 = (bf16[64,128]{1,0:T(8,128)(2,1)S(1)}, bf16[64,128]{1,0:T(8,128)(2,1)S(1)}, u32[]{:S(2)}, u32[]{:S(2)}) collective-permute-start(bf16[64,128]{1,0:T(8,128)(2,1)S(1)} %get-tuple-element.120), channel_id=1, source_target_pairs={{92,88},{88,92},{84,80},{80,84},{76,72},{72,76},{68,64},{64,68},{9... | collective-permute-start | bytes 49160 | tf_op jit(solution)/shard_map/ppermute | solution.py:334
  20.8 3.2 %collective-permute-start.5 = (bf16[64,128]{1,0:T(8,128)(2,1)S(1)}, bf16[64,128]{1,0:T(8,128)(2,1)S(1)}, u32[]{:S(2)}, u32[]{:S(2)}) collective-permute-start(bf16[64,128]{1,0:T(8,128)(2,1)S(1)} %get-tuple-element.111), channel_id=1, source_target_pairs={{94,28},{28,94},{90,24},{24,90},{86,20},{20,86},{82,16},{16,82},{7... | collective-permute-start | bytes 49160 | tf_op jit(solution)/shard_map/ppermute | solution.py:334
  22.1 2.0 %collective-permute-start.4 = (bf16[64,128]{1,0:T(8,128)(2,1)S(1)}, bf16[64,128]{1,0:T(8,128)(2,1)S(1)}, u32[]{:S(2)}, u32[]{:S(2)}) collective-permute-start(bf16[64,128]{1,0:T(8,128)(2,1)S(1)} %get-tuple-element.112), channel_id=1, source_target_pairs={{92,94},{94,92},{88,90},{90,88},{84,86},{86,84},{80,82},{82,80},{7... | collective-permute-start | bytes 49160 | tf_op jit(solution)/shard_map/ppermute | solution.py:334
  22.1 0.9 copy-start.2
  24.1 8.5 %copy-start = (bf16[64,576]{1,0:T(8,128)(2,1)S(1)}, bf16[64,576]{1,0:T(8,128)(2,1)}, u32[]{:S(2)}) copy-start(bf16[64,576]{1,0:T(8,128)(2,1)} %w.1) | copy-start | bytes 221188
  24.1 8.5 %copy-start.1 = (bf16[64,256]{1,0:T(8,128)(2,1)S(1)}, bf16[64,256]{1,0:T(8,128)(2,1)}, u32[]{:S(2)}) copy-start(bf16[64,256]{1,0:T(8,128)(2,1)} %refs_4_.1) | copy-start | bytes 98308
  25.3 5.4 %collective-permute-start.7 = (bf16[64,128]{1,0:T(8,128)(2,1)S(1)}, bf16[64,128]{1,0:T(8,128)(2,1)S(1)}, u32[]{:S(2)}, u32[]{:S(2)}) collective-permute-start(bf16[64,128]{1,0:T(8,128)(2,1)S(1)} %get-tuple-element.117), channel_id=1, source_target_pairs={{88,84},{84,88},{80,76},{76,80},{72,68},{68,72},{64,94},{94,64},{9... | collective-permute-start | bytes 49160 | tf_op jit(solution)/shard_map/ppermute | solution.py:334
  29.0 2.6 %collective-permute-start.6 = (bf16[64,128]{1,0:T(8,128)(2,1)S(1)}, bf16[64,128]{1,0:T(8,128)(2,1)S(1)}, u32[]{:S(2)}, u32[]{:S(2)}) collective-permute-start(bf16[64,128]{1,0:T(8,128)(2,1)S(1)} %get-tuple-element.118), channel_id=1, source_target_pairs={{92,88},{88,92},{84,80},{80,84},{76,72},{72,76},{68,64},{64,68},{9... | collective-permute-start | bytes 49160 | tf_op jit(solution)/shard_map/ppermute | solution.py:334
  31.6 3.3 %collective-permute-start.9 = (bf16[64,128]{1,0:T(8,128)(2,1)S(1)}, bf16[64,128]{1,0:T(8,128)(2,1)S(1)}, u32[]{:S(2)}, u32[]{:S(2)}) collective-permute-start(bf16[64,128]{1,0:T(8,128)(2,1)S(1)} %get-tuple-element.105), channel_id=1, source_target_pairs={{94,28},{28,94},{90,24},{24,90},{86,20},{20,86},{82,16},{16,82},{7... | collective-permute-start | bytes 49160 | tf_op jit(solution)/shard_map/ppermute | solution.py:334
  32.6 2.3 %collective-permute-start.8 = (bf16[64,128]{1,0:T(8,128)(2,1)S(1)}, bf16[64,128]{1,0:T(8,128)(2,1)S(1)}, u32[]{:S(2)}, u32[]{:S(2)}) collective-permute-start(bf16[64,128]{1,0:T(8,128)(2,1)S(1)} %get-tuple-element.106), channel_id=1, source_target_pairs={{92,94},{94,92},{88,90},{90,88},{84,86},{86,84},{80,82},{82,80},{7... | collective-permute-start | bytes 49160 | tf_op jit(solution)/shard_map/ppermute | solution.py:334
  36.7 3.3 %collective-permute-start.11 = (bf16[64,128]{1,0:T(8,128)(2,1)S(1)}, bf16[64,128]{1,0:T(8,128)(2,1)S(1)}, u32[]{:S(2)}, u32[]{:S(2)}) collective-permute-start(bf16[64,128]{1,0:T(8,128)(2,1)S(1)} %get-tuple-element.115), channel_id=1, source_target_pairs={{94,28},{28,94},{90,24},{24,90},{86,20},{20,86},{82,16},{16,82},{7... | collective-permute-start | bytes 49160 | tf_op jit(solution)/shard_map/ppermute | solution.py:334
  37.7 2.3 %collective-permute-start.10 = (bf16[64,128]{1,0:T(8,128)(2,1)S(1)}, bf16[64,128]{1,0:T(8,128)(2,1)S(1)}, u32[]{:S(2)}, u32[]{:S(2)}) collective-permute-start(bf16[64,128]{1,0:T(8,128)(2,1)S(1)} %get-tuple-element.116), channel_id=1, source_target_pairs={{92,94},{94,92},{88,90},{90,88},{84,86},{86,84},{80,82},{82,80},{7... | collective-permute-start | bytes 49160 | tf_op jit(solution)/shard_map/ppermute | solution.py:334
  40.0 5.5 %collective-permute-start.13 = (bf16[64,128]{1,0:T(8,128)(2,1)S(1)}, bf16[64,128]{1,0:T(8,128)(2,1)S(1)}, u32[]{:S(2)}, u32[]{:S(2)}) collective-permute-start(bf16[64,128]{1,0:T(8,128)(2,1)S(1)} %get-tuple-element.109), channel_id=1, source_target_pairs={{88,84},{84,88},{80,76},{76,80},{72,68},{68,72},{64,94},{94,64},{9... | collective-permute-start | bytes 49160 | tf_op jit(solution)/shard_map/ppermute | solution.py:334
  43.0 2.6 %collective-permute-start.12 = (bf16[64,128]{1,0:T(8,128)(2,1)S(1)}, bf16[64,128]{1,0:T(8,128)(2,1)S(1)}, u32[]{:S(2)}, u32[]{:S(2)}) collective-permute-start(bf16[64,128]{1,0:T(8,128)(2,1)S(1)} %get-tuple-element.110), channel_id=1, source_target_pairs={{92,88},{88,92},{84,80},{80,84},{76,72},{72,76},{68,64},{64,68},{9... | collective-permute-start | bytes 49160 | tf_op jit(solution)/shard_map/ppermute | solution.py:334
  47.1 14.4 %all-to-all-start = ((bf16[16,48,128]{2,1,0:T(8,128)(2,1)}), bf16[16,48,128]{2,1,0:T(8,128)(2,1)S(1)}, u32[]{:S(2)}, u32[]{:S(2)}) async-start(bf16[16,48,128]{2,1,0:T(8,128)(2,1)} %bitcast.4), calls=%async_computation | async-start | bytes 393216 | tf_op jit(solution)/shard_map/all_to_all | solution.py:393
  54.2 3.5 %collective-permute-start.15 = (bf16[64,128]{1,0:T(8,128)(2,1)S(1)}, bf16[64,128]{1,0:T(8,128)(2,1)S(1)}, u32[]{:S(2)}, u32[]{:S(2)}) collective-permute-start(bf16[64,128]{1,0:T(8,128)(2,1)S(1)} %get-tuple-element.113), channel_id=1, source_target_pairs={{94,28},{28,94},{90,24},{24,90},{86,20},{20,86},{82,16},{16,82},{7... | collective-permute-start | bytes 49160 | tf_op jit(solution)/shard_map/ppermute | solution.py:334
  55.6 2.1 %collective-permute-start.14 = (bf16[64,128]{1,0:T(8,128)(2,1)S(1)}, bf16[64,128]{1,0:T(8,128)(2,1)S(1)}, u32[]{:S(2)}, u32[]{:S(2)}) collective-permute-start(bf16[64,128]{1,0:T(8,128)(2,1)S(1)} %get-tuple-element.114), channel_id=1, source_target_pairs={{92,94},{94,92},{88,90},{90,88},{84,86},{86,84},{80,82},{82,80},{7... | collective-permute-start | bytes 49160 | tf_op jit(solution)/shard_map/ppermute | solution.py:334
  57.7 10.0 %collective-permute-start.17 = (bf16[64,128]{1,0:T(8,128)(2,1)S(1)}, bf16[64,128]{1,0:T(8,128)(2,1)S(1)}, u32[]{:S(2)}, u32[]{:S(2)}) collective-permute-start(bf16[64,128]{1,0:T(8,128)(2,1)S(1)} %get-tuple-element.107), channel_id=1, source_target_pairs={{88,84},{84,88},{80,76},{76,80},{72,68},{68,72},{64,94},{94,64},{9... | collective-permute-start | bytes 49160 | tf_op jit(solution)/shard_map/ppermute | solution.py:334
  61.5 6.2 %collective-permute-start.16 = (bf16[64,128]{1,0:T(8,128)(2,1)S(1)}, bf16[64,128]{1,0:T(8,128)(2,1)S(1)}, u32[]{:S(2)}, u32[]{:S(2)}) collective-permute-start(bf16[64,128]{1,0:T(8,128)(2,1)S(1)} %get-tuple-element.108), channel_id=1, source_target_pairs={{92,88},{88,92},{84,80},{80,84},{76,72},{72,76},{68,64},{64,68},{9... | collective-permute-start | bytes 49160 | tf_op jit(solution)/shard_map/ppermute | solution.py:334
  62.2 12.5 %all-to-all-start.1 = ((bf16[16,48,128]{2,1,0:T(8,128)(2,1)}), bf16[16,48,128]{2,1,0:T(8,128)(2,1)S(1)}, u32[]{:S(2)}, u32[]{:S(2)}) async-start(bf16[16,48,128]{2,1,0:T(8,128)(2,1)} %fold.2), calls=%async_computation.1 | async-start | bytes 393216 | tf_op jit(solution)/shard_map/all_to_all | solution.py:393
  68.4 13.9 %collective-permute-start.18 = (bf16[64,1280]{1,0:T(8,128)(2,1)S(1)}, bf16[64,1280]{1,0:T(8,128)(2,1)S(1)}, u32[]{:S(2)}, u32[]{:S(2)}) collective-permute-start(bf16[64,1280]{1,0:T(8,128)(2,1)S(1)} %last.1), channel_id=1, source_target_pairs={{92,0},{88,2},{84,4},{80,6},{76,8},{72,10},{68,12},{64,14},{94,16}... | collective-permute-start | bytes 491528 | tf_op jit(solution)/shard_map/ppermute | solution.py:334
  75.5 15.1 %all-to-all-start.2 = ((bf16[16,48,128]{2,1,0:T(8,128)(2,1)}), bf16[16,48,128]{2,1,0:T(8,128)(2,1)S(1)}, u32[]{:S(2)}, u32[]{:S(2)}) async-start(bf16[16,48,128]{2,1,0:T(8,128)(2,1)} %fold.3), calls=%async_computation.2 | async-start | bytes 393216 | tf_op jit(solution)/shard_map/all_to_all | solution.py:393

commit v5 on v4

--- a/solution.py
+++ b/solution.py
@@ -28,14 +28,14 @@
 F32 = jnp.float32
 
 
-def call(body, outs, scratch, args, flops, name, space=pltpu.VMEM, limit=24):
+def call(body, outs, scratch, args, flops, name, space=pltpu.VMEM, limit=24, last=pltpu.VMEM):
     specs = [pl.BlockSpec(memory_space=space) for a in args]
     moved = sum(math.prod(o.shape) * o.dtype.itemsize for o in list(outs) + list(args))
     return pl.pallas_call(
         body,
         out_shape=outs,
         in_specs=specs,
-        out_specs=[pl.BlockSpec(memory_space=pltpu.VMEM)] * len(outs),
+        out_specs=[pl.BlockSpec(memory_space=pltpu.VMEM)] * (len(outs) - 1) + [pl.BlockSpec(memory_space=last)],
         scratch_shapes=scratch,
         compiler_params=pltpu.CompilerParams(vmem_limit_bytes=limit * 2**20),
         cost_estimate=pl.CostEstimate(flops=flops, bytes_accessed=moved, transcendentals=0),
@@ -162,24 +162,29 @@
     return jnp.where(place == 72 * (m >> 4) + 2 * (m & 15), 1.0, 0.0).astype(BF)
 
 
-def load_body(codes_hbm, x_hbm, cot_hbm, edges, load, codes, sems):
+def load_body(codes_hbm, x_hbm, cot_hbm, edges, load, codes, x, sems):
     copies = [
-        pltpu.make_async_copy(codes_hbm, codes, sems.at[0]),
-        pltpu.make_async_copy(x_hbm, load.at[:, pl.ds(0, S * S)], sems.at[1]),
-        pltpu.make_async_copy(cot_hbm, load.at[:, pl.ds(S * S, 256)], sems.at[2]),
+        pltpu.make_async_copy(x_hbm, x, sems.at[0]),
+        pltpu.make_async_copy(codes_hbm, codes, sems.at[1]),
     ]
-    for copy in copies:
+    beside = [
+        pltpu.make_async_copy(x_hbm, load.at[:, pl.ds(0, S * S)], sems.at[2]),
+        pltpu.make_async_copy(cot_hbm, load.at[:, pl.ds(S * S, 256)], sems.at[3]),
+    ]
+    for copy in copies + beside:
         copy.start()
     lane, edge, along = lanes_of()[:3]
     y = jnp.where((edge & 1) == 0, jnp.where(edge == 0, 0, S - 1), along)
-    x = jnp.where((edge & 1) == 0, along, jnp.where(edge == 1, S - 1, 0))
-    hot = pick([S * y + x], 0, S * S)
+    column = jnp.where((edge & 1) == 0, along, jnp.where(edge == 1, S - 1, 0))
+    hot = pick([S * y + column], 0, S * S)
     for copy in copies:
         copy.wait()
-    edges[:, :SLOT] = mm(load[:, : S * S], hot).astype(BF)
+    edges[:, :SLOT] = mm(x[...], hot).astype(BF)
     row = lax.broadcasted_iota(jnp.int32, (C, SLOT), 0)
     value = jnp.where(row == 0, codes[0, 0], jnp.where(row == 1, codes[0, 1], jnp.where(row == 2, codes[0, 2], codes[0, 3])))
     edges[:, SLOT:] = value.astype(F32).astype(BF)
+    for copy in beside:
+        copy.wait()
 
 
 def edge_row(facts, group):
@@ -411,12 +416,13 @@
     edges, load = call(
         load_body,
         [out((C, 2 * SLOT), BF), out((C, LOAD), BF)],
-        [pltpu.SMEM((1, 4), jnp.int32), pltpu.SemaphoreType.DMA((3,))],
+        [pltpu.SMEM((1, 4), jnp.int32), pltpu.VMEM((C, S * S), BF), pltpu.SemaphoreType.DMA((4,))],
         [seam_codes, x, cot],
         C * LOAD,
         "load",
         pltpu.HBM,
         60,
+        pl.ANY,
     )
     there = [(t, home(t)) for t in range(128)]
     edges, load = move(edges, there), move(load, there)

time: 91.8 us -> 96.7 us (1.053)
  Pallas kernels: 14 us -> 19 us
    pallas_call x14, Pallas kernels: 14 us -> 19 us  [call(): pl.pallas_call(body, out_shape=outs, in_specs=specs, out_specs=[pl.BlockS...]
  transfers between devices with their start and end apart: 22 -> 22, of which waited for: 12 -> 12; matrix products, arithmetic and copies ran while one was open for 1% -> 1% of each run, Pallas kernels for 8% -> 7%
where the time goes in v5:
time: 96.7 us; the launch traced here: 96.3 us
  starting transfers between devices  52.7 us (54%)
  waiting for transfers between devices  21.5 us (22%)
  Pallas kernels  19 us (20%)
  local copies, waits for them, and re-layouts  2.17 us (2%)
    ppermute x19, starting transfers between devices, move(): return lax.ppermute(value, TILE, pairs)  34.3 us
    pallas_call x14, Pallas kernels, call(): pl.pallas_call(body, out_shape=outs, in_specs=specs, out_specs=[pl.BlockS...  19 us
    all_to_all x3, starting transfers between devices, trade(): return lax.all_to_all(parts, axes, 0, 0, tiled=True)  18.4 us
    ppermute x19, waiting for transfers between devices, move(): return lax.ppermute(value, TILE, pairs)  11.8 us
    all_to_all x3, waiting for transfers between devices, trade(): return lax.all_to_all(parts, axes, 0, 0, tiled=True)  9.74 us
  transfers between devices with their start and end apart: 22, of which 12 were waited for; matrix products, arithmetic and copies ran while one was open for 1% of the time, Pallas kernels for 7%

profile of v5, /device:TPU:1, one launch (start us, length us, event | category | flops | bytes accessed | tf_op | source)
XLA Modules:
  0.0 96.3 jit_solution(4622049868072273832)
XLA Ops:
  0.6 6.7 %load.1 = (bf16[64,256]{1,0:T(8,128)(2,1)}, bf16[64,1280]{1,0:T(8,128)(2,1)}) custom-call(s32[1,4]{1,0:T(1,128)} %codes_hbm.1, bf16[64,1024]{1,0:T(8,128)(2,1)} %bitcast.9, bf16[64,256]{1,0:T(8,128)(2,1)} %bitcast.10), custom_call_target="tpu_custom_call" | custom-call | flops 81920 | bytes 360464 | tf_op jit(solution)/shard_map/load/pallas_call | solution.py:34
  7.4 8.4 %collective-permute-start = (bf16[64,256]{1,0:T(8,128)(2,1)}, bf16[64,256]{1,0:T(8,128)(2,1)S(1)}, u32[]{:S(2)}, u32[]{:S(2)}) collective-permute-start(bf16[64,256]{1,0:T(8,128)(2,1)} %get-tuple-element.55), channel_id=1, source_target_pairs={{0,92},{2,88},{4,84},{6,80},{8,76},{10,72},{12,68},{14,64},{16,94}... | collective-permute-start | bytes 98312 | tf_op jit(solution)/shard_map/ppermute | solution.py:339
  15.8 1.4 %collective-permute-start.3 = (bf16[64,1280]{1,0:T(8,128)(2,1)}, bf16[64,1280]{1,0:T(8,128)(2,1)S(1)}, u32[]{:S(2)}, u32[]{:S(2)}) collective-permute-start(bf16[64,1280]{1,0:T(8,128)(2,1)} %get-tuple-element.67), channel_id=1, source_target_pairs={{0,92},{2,88},{4,84},{6,80},{8,76},{10,72},{12,68},{14,64},{16,94}... | collective-permute-start | bytes 491528 | tf_op jit(solution)/shard_map/ppermute | solution.py:339
  17.4 5.8 %collective-permute-start.2 = (bf16[64,128]{1,0:T(8,128)(2,1)S(1)}, bf16[64,128]{1,0:T(8,128)(2,1)S(1)}, u32[]{:S(2)}, u32[]{:S(2)}) collective-permute-start(bf16[64,128]{1,0:T(8,128)(2,1)S(1)} %get-tuple-element.119), channel_id=1, source_target_pairs={{88,84},{84,88},{80,76},{76,80},{72,68},{68,72},{64,94},{94,64},{9... | collective-permute-start | bytes 49160 | tf_op jit(solution)/shard_map/ppermute | solution.py:339
  23.2 1.1 %hots.1 = (bf16[1408,512]{1,0:T(8,128)(2,1)S(1)}, bf16[1408,512]{1,0:T(8,128)(2,1)S(1)}, bf16[1152,512]{1,0:T(8,128)(2,1)S(1)}, bf16[1152,512]{1,0:T(8,128)(2,1)S(1)}) custom-call(s32[8,128]{1,0:T(8,128)S(1)} %get-tuple-element.58.facts), custom_call_target="tpu_custom_call" | custom-call | flops 84934656 | bytes 5246976 | tf_op jit(solution)/shard_map/hots/pallas_call | solution.py:34
  24.6 1.2 %collective-permute-done.1.r2 = bf16[64,128]{1,0:T(8,128)(2,1)S(1)} collective-permute-done((bf16[64,128]{1,0:T(8,128)(2,1)S(1)}, bf16[64,128]{1,0:T(8,128)(2,1)S(1)}, u32[]{:S(2)}, u32[]{:S(2)}) %collective-permute-start.1) | collective-permute-done | bytes 16416 | tf_op jit(solution)/shard_map/ppermute | solution.py:339
  25.8 1.3 %collective-permute-start.5 = (bf16[64,128]{1,0:T(8,128)(2,1)S(1)}, bf16[64,128]{1,0:T(8,128)(2,1)S(1)}, u32[]{:S(2)}, u32[]{:S(2)}) collective-permute-start(bf16[64,128]{1,0:T(8,128)(2,1)S(1)} %get-tuple-element.111), channel_id=1, source_target_pairs={{94,28},{28,94},{90,24},{24,90},{86,20},{20,86},{82,16},{16,82},{7... | collective-permute-start | bytes 49160 | tf_op jit(solution)/shard_map/ppermute | solution.py:339
  27.1 0.9 copy-done.2
  29.1 1.2 %first.1 = (bf16[576,1152]{1,0:T(8,128)(2,1)S(1)}, bf16[64,1152]{1,0:T(8,128)(2,1)S(1)}, f32[64,1152]{1,0:T(8,128)S(1)}, bf16[64,128]{1,0:T(8,128)(2,1)S(1)}, bf...) custom-call(bf16[1408,512]{1,0:T(8,128)(2,1)S(1)} %get-tuple-element.64.rim, ...), custom_call_target="tpu_custom_call" | custom-call | flops 169869312 | bytes 4775936 | tf_op jit(solution)/shard_map/first/pallas_call | solution.py:34
  30.3 3.7 %collective-permute-start.7 = (bf16[64,128]{1,0:T(8,128)(2,1)S(1)}, bf16[64,128]{1,0:T(8,128)(2,1)S(1)}, u32[]{:S(2)}, u32[]{:S(2)}) collective-permute-start(bf16[64,128]{1,0:T(8,128)(2,1)S(1)} %get-tuple-element.117), channel_id=1, source_target_pairs={{88,84},{84,88},{80,76},{76,80},{72,68},{68,72},{64,94},{94,64},{9... | collective-permute-start | bytes 49160 | tf_op jit(solution)/shard_map/ppermute | solution.py:339
  34.0 1.7 %collective-permute-done.7.r3 = bf16[64,128]{1,0:T(8,128)(2,1)S(1)} collective-permute-done((bf16[64,128]{1,0:T(8,128)(2,1)S(1)}, bf16[64,128]{1,0:T(8,128)(2,1)S(1)}, u32[]{:S(2)}, u32[]{:S(2)}) %collective-permute-start.7) | collective-permute-done | bytes 16416 | tf_op jit(solution)/shard_map/ppermute | solution.py:339
  35.7 0.9 collective-permute-done.6.r2
  36.6 1.0 collective-permute-start.9
  37.6 1.3 %prepare.1 = (bf16[64,1152]{1,0:T(8,128)(2,1)S(1)}, f32[64,1152]{1,0:T(8,128)S(1)}, bf16[64,576]{1,0:T(8,128)(2,1)S(1)}, bf16[64,576]{1,0:T(8,128)(2,1)S(1)}) custom-call(bf16[64,1280]{1,0:T(8,128)(2,1)S(1)} %collective-permute-done.3.load, bf16[64,256]{1,0:T(8,128)(2,1)S(1)} %copy-done.1, bf16[64,576]{1,0:T(8,128)(2,1)S(1)} %get-tuple-element.72.w.one, ...), custom_call_target="tpu_custom_call" | custom-call | flops 84934656 | bytes 933888 | tf_op jit(solution)/shard_map/prepare/pallas_call | solution.py:34
  38.9 0.9 collective-permute-done.9.r1
  39.8 1.9 %second.1 = (bf16[64,1408]{1,0:T(8,128)(2,1)S(1)}, bf16[64,1152]{1,0:T(8,128)(2,1)S(1)}, bf16[64,1152]{1,0:T(8,128)(2,1)S(1)}, f32[64,1152]{1,0:T(8,128)S(1)}, b...) custom-call(bf16[1408,512]{1,0:T(8,128)(2,1)S(1)} %get-tuple-element, ...), custom_call_target="tpu_custom_call" | custom-call | flops 254803968 | bytes 2932736 | tf_op jit(solution)/shard_map/second/pallas_call | solution.py:34
  41.7 1.0 collective-permute-start.11
  42.7 2.3 %collective-permute-done.11.refs_3_ = bf16[64,128]{1,0:T(8,128)(2,1)S(1)} collective-permute-done((bf16[64,128]{1,0:T(8,128)(2,1)S(1)}, bf16[64,128]{1,0:T(8,128)(2,1)S(1)}, u32[]{:S(2)}, u32[]{:S(2)}) %collective-permute-start.11) | collective-permute-done | bytes 16416 | tf_op jit(solution)/shard_map/ppermute | solution.py:339
  45.0 2.9 %collective-permute-start.13 = (bf16[64,128]{1,0:T(8,128)(2,1)S(1)}, bf16[64,128]{1,0:T(8,128)(2,1)S(1)}, u32[]{:S(2)}, u32[]{:S(2)}) collective-permute-start(bf16[64,128]{1,0:T(8,128)(2,1)S(1)} %get-tuple-element.109), channel_id=1, source_target_pairs={{88,84},{84,88},{80,76},{76,80},{72,68},{68,72},{64,94},{94,64},{9... | collective-permute-start | bytes 49160 | tf_op jit(solution)/shard_map/ppermute | solution.py:339
  47.9 1.0 %second_sums.1 = (bf16[64,256]{1,0:T(8,128)(2,1)S(1)}, f32[64,576]{1,0:T(8,128)S(1)}, f32[64,256]{1,0:T(8,128)S(1)}) custom-call(bf16[64,1408]{1,0:T(8,128)(2,1)S(1)} %get-tuple-element.87.refs_0_, bf16[64,1152]{1,0:T(8,128)(2,1)S(1)} %get-tuple-element.88.refs_1_, bf16[64,1152]{1,0:T(8,128)(2,1)S(1)} %get-tuple-element.89.refs_2_, ...), custom_call_target="tpu_custom_call" | custom-call | flops 169869312 | bytes 901120 | tf_op jit(solution)/shard_map/second_sums/pallas_call | solution.py:34
  48.9 1.6 %collective-permute-done.13.refs_5_ = bf16[64,128]{1,0:T(8,128)(2,1)S(1)} collective-permute-done((bf16[64,128]{1,0:T(8,128)(2,1)S(1)}, bf16[64,128]{1,0:T(8,128)(2,1)S(1)}, u32[]{:S(2)}, u32[]{:S(2)}) %collective-permute-start.13) | collective-permute-done | bytes 16416 | tf_op jit(solution)/shard_map/ppermute | solution.py:339
  50.5 1.6 %third.1 = (bf16[64,1152]{1,0:T(8,128)(2,1)S(1)}, bf16[768,128]{1,0:T(8,128)(2,1)}) custom-call(bf16[1152,512]{1,0:T(8,128)(2,1)S(1)} %get-tuple-element.65.source.refs_0_, f32[64,1152]{1,0:T(8,128)S(1)} %get-tuple-element.80.refs_1_, bf16[64,128]{1,0:T(8,128)(2,1)S(1)} %collective-permute-done.10.refs_2_, ...), custom_call_target="tpu_custom_call" | custom-call | flops 169869312 | bytes 3719168 | tf_op jit(solution)/shard_map/third/pallas_call | solution.py:34
  52.1 6.2 %all-to-all-start = ((bf16[16,48,128]{2,1,0:T(8,128)(2,1)}), bf16[16,48,128]{2,1,0:T(8,128)(2,1)S(1)}, u32[]{:S(2)}, u32[]{:S(2)}) async-start(bf16[16,48,128]{2,1,0:T(8,128)(2,1)} %bitcast.4), calls=%async_computation | async-start | bytes 393216 | tf_op jit(solution)/shard_map/all_to_all | solution.py:398
  58.2 0.9 fourth.1
  59.1 1.5 %collective-permute-start.15 = (bf16[64,128]{1,0:T(8,128)(2,1)S(1)}, bf16[64,128]{1,0:T(8,128)(2,1)S(1)}, u32[]{:S(2)}, u32[]{:S(2)}) collective-permute-start(bf16[64,128]{1,0:T(8,128)(2,1)S(1)} %get-tuple-element.113), channel_id=1, source_target_pairs={{94,28},{28,94},{90,24},{24,90},{86,20},{20,86},{82,16},{16,82},{7... | collective-permute-start | bytes 49160 | tf_op jit(solution)/shard_map/ppermute | solution.py:339
  60.6 2.1 %collective-permute-done.15.r1 = bf16[64,128]{1,0:T(8,128)(2,1)S(1)} collective-permute-done((bf16[64,128]{1,0:T(8,128)(2,1)S(1)}, bf16[64,128]{1,0:T(8,128)(2,1)S(1)}, u32[]{:S(2)}, u32[]{:S(2)}) %collective-permute-start.15) | collective-permute-done | bytes 16416 | tf_op jit(solution)/shard_map/ppermute | solution.py:339
  62.7 3.7 %collective-permute-start.17 = (bf16[64,128]{1,0:T(8,128)(2,1)S(1)}, bf16[64,128]{1,0:T(8,128)(2,1)S(1)}, u32[]{:S(2)}, u32[]{:S(2)}) collective-permute-start(bf16[64,128]{1,0:T(8,128)(2,1)S(1)} %get-tuple-element.107), channel_id=1, source_target_pairs={{88,84},{84,88},{80,76},{76,80},{72,68},{68,72},{64,94},{94,64},{9... | collective-permute-start | bytes 49160 | tf_op jit(solution)/shard_map/ppermute | solution.py:339
  67.2 5.5 %all-to-all-start.1 = ((bf16[16,48,128]{2,1,0:T(8,128)(2,1)}), bf16[16,48,128]{2,1,0:T(8,128)(2,1)S(1)}, u32[]{:S(2)}, u32[]{:S(2)}) async-start(bf16[16,48,128]{2,1,0:T(8,128)(2,1)} %fold.2), calls=%async_computation.1 | async-start | bytes 393216 | tf_op jit(solution)/shard_map/all_to_all | solution.py:398
  73.4 3.7 %collective-permute-start.18 = (bf16[64,1280]{1,0:T(8,128)(2,1)S(1)}, bf16[64,1280]{1,0:T(8,128)(2,1)S(1)}, u32[]{:S(2)}, u32[]{:S(2)}) collective-permute-start(bf16[64,1280]{1,0:T(8,128)(2,1)S(1)} %last.1), channel_id=1, source_target_pairs={{92,0},{88,2},{84,4},{80,6},{76,8},{72,10},{68,12},{64,14},{94,16}... | collective-permute-start | bytes 491528 | tf_op jit(solution)/shard_map/ppermute | solution.py:339
  77.1 2.7 %all-to-all-done.1.parts = bf16[16,48,128]{2,1,0:T(8,128)(2,1)S(1)} async-done(((bf16[16,48,128]{2,1,0:T(8,128)(2,1)}), bf16[16,48,128]{2,1,0:T(8,128)(2,1)S(1)}, u32[]{:S(2)}, u32[]{:S(2)}) %all-to-all-start.1) | async-done | bytes 196640 | tf_op jit(solution)/shard_map/all_to_all | solution.py:398
  80.5 6.8 %all-to-all-start.2 = ((bf16[16,48,128]{2,1,0:T(8,128)(2,1)}), bf16[16,48,128]{2,1,0:T(8,128)(2,1)S(1)}, u32[]{:S(2)}, u32[]{:S(2)}) async-start(bf16[16,48,128]{2,1,0:T(8,128)(2,1)} %fold.3), calls=%async_computation.2 | async-start | bytes 393216 | tf_op jit(solution)/shard_map/all_to_all | solution.py:398
  88.5 7.0 %all-to-all-done.2 = bf16[16,48,128]{2,1,0:T(8,128)(2,1)S(1)} async-done(((bf16[16,48,128]{2,1,0:T(8,128)(2,1)}), bf16[16,48,128]{2,1,0:T(8,128)(2,1)S(1)}, u32[]{:S(2)}, u32[]{:S(2)}) %all-to-all-start.2) | async-done | bytes 196640 | tf_op jit(solution)/shard_map/all_to_all | solution.py:398
  (46 shorter events, 6.0 us)
Async XLA Ops:
  7.4 9.9 %collective-permute-start = (bf16[64,256]{1,0:T(8,128)(2,1)}, bf16[64,256]{1,0:T(8,128)(2,1)S(1)}, u32[]{:S(2)}, u32[]{:S(2)}) collective-permute-start(bf16[64,256]{1,0:T(8,128)(2,1)} %get-tuple-element.55), channel_id=1, source_target_pairs={{0,92},{2,88},{4,84},{6,80},{8,76},{10,72},{12,68},{14,64},{16,94}... | collective-permute-start | bytes 98312 | tf_op jit(solution)/shard_map/ppermute | solution.py:339
  15.8 11.3 %collective-permute-start.3 = (bf16[64,1280]{1,0:T(8,128)(2,1)}, bf16[64,1280]{1,0:T(8,128)(2,1)S(1)}, u32[]{:S(2)}, u32[]{:S(2)}) collective-permute-start(bf16[64,1280]{1,0:T(8,128)(2,1)} %get-tuple-element.67), channel_id=1, source_target_pairs={{0,92},{2,88},{4,84},{6,80},{8,76},{10,72},{12,68},{14,64},{16,94}... | collective-permute-start | bytes 491528 | tf_op jit(solution)/shard_map/ppermute | solution.py:339
  17.4 7.2 %collective-permute-start.2 = (bf16[64,128]{1,0:T(8,128)(2,1)S(1)}, bf16[64,128]{1,0:T(8,128)(2,1)S(1)}, u32[]{:S(2)}, u32[]{:S(2)}) collective-permute-start(bf16[64,128]{1,0:T(8,128)(2,1)S(1)} %get-tuple-element.119), channel_id=1, source_target_pairs={{88,84},{84,88},{80,76},{76,80},{72,68},{68,72},{64,94},{94,64},{9... | collective-permute-start | bytes 49160 | tf_op jit(solution)/shard_map/ppermute | solution.py:339
  23.2 2.6 %collective-permute-start.1 = (bf16[64,128]{1,0:T(8,128)(2,1)S(1)}, bf16[64,128]{1,0:T(8,128)(2,1)S(1)}, u32[]{:S(2)}, u32[]{:S(2)}) collective-permute-start(bf16[64,128]{1,0:T(8,128)(2,1)S(1)} %get-tuple-element.120), channel_id=1, source_target_pairs={{92,88},{88,92},{84,80},{80,84},{76,72},{72,76},{68,64},{64,68},{9... | collective-permute-start | bytes 49160 | tf_op jit(solution)/shard_map/ppermute | solution.py:339
  25.8 3.2 %collective-permute-start.5 = (bf16[64,128]{1,0:T(8,128)(2,1)S(1)}, bf16[64,128]{1,0:T(8,128)(2,1)S(1)}, u32[]{:S(2)}, u32[]{:S(2)}) collective-permute-start(bf16[64,128]{1,0:T(8,128)(2,1)S(1)} %get-tuple-element.111), channel_id=1, source_target_pairs={{94,28},{28,94},{90,24},{24,90},{86,20},{20,86},{82,16},{16,82},{7... | collective-permute-start | bytes 49160 | tf_op jit(solution)/shard_map/ppermute | solution.py:339
  27.1 2.0 %collective-permute-start.4 = (bf16[64,128]{1,0:T(8,128)(2,1)S(1)}, bf16[64,128]{1,0:T(8,128)(2,1)S(1)}, u32[]{:S(2)}, u32[]{:S(2)}) collective-permute-start(bf16[64,128]{1,0:T(8,128)(2,1)S(1)} %get-tuple-element.112), channel_id=1, source_target_pairs={{92,94},{94,92},{88,90},{90,88},{84,86},{86,84},{80,82},{82,80},{7... | collective-permute-start | bytes 49160 | tf_op jit(solution)/shard_map/ppermute | solution.py:339
  27.1 0.9 copy-start.2
  29.1 8.5 %copy-start = (bf16[64,576]{1,0:T(8,128)(2,1)S(1)}, bf16[64,576]{1,0:T(8,128)(2,1)}, u32[]{:S(2)}) copy-start(bf16[64,576]{1,0:T(8,128)(2,1)} %w.1) | copy-start | bytes 221188
  29.1 8.5 %copy-start.1 = (bf16[64,256]{1,0:T(8,128)(2,1)S(1)}, bf16[64,256]{1,0:T(8,128)(2,1)}, u32[]{:S(2)}) copy-start(bf16[64,256]{1,0:T(8,128)(2,1)} %refs_4_.1) | copy-start | bytes 98308
  30.3 5.4 %collective-permute-start.7 = (bf16[64,128]{1,0:T(8,128)(2,1)S(1)}, bf16[64,128]{1,0:T(8,128)(2,1)S(1)}, u32[]{:S(2)}, u32[]{:S(2)}) collective-permute-start(bf16[64,128]{1,0:T(8,128)(2,1)S(1)} %get-tuple-element.117), channel_id=1, source_target_pairs={{88,84},{84,88},{80,76},{76,80},{72,68},{68,72},{64,94},{94,64},{9... | collective-permute-start | bytes 49160 | tf_op jit(solution)/shard_map/ppermute | solution.py:339
  34.0 2.6 %collective-permute-start.6 = (bf16[64,128]{1,0:T(8,128)(2,1)S(1)}, bf16[64,128]{1,0:T(8,128)(2,1)S(1)}, u32[]{:S(2)}, u32[]{:S(2)}) collective-permute-start(bf16[64,128]{1,0:T(8,128)(2,1)S(1)} %get-tuple-element.118), channel_id=1, source_target_pairs={{92,88},{88,92},{84,80},{80,84},{76,72},{72,76},{68,64},{64,68},{9... | collective-permute-start | bytes 49160 | tf_op jit(solution)/shard_map/ppermute | solution.py:339
  36.6 3.3 %collective-permute-start.9 = (bf16[64,128]{1,0:T(8,128)(2,1)S(1)}, bf16[64,128]{1,0:T(8,128)(2,1)S(1)}, u32[]{:S(2)}, u32[]{:S(2)}) collective-permute-start(bf16[64,128]{1,0:T(8,128)(2,1)S(1)} %get-tuple-element.105), channel_id=1, source_target_pairs={{94,28},{28,94},{90,24},{24,90},{86,20},{20,86},{82,16},{16,82},{7... | collective-permute-start | bytes 49160 | tf_op jit(solution)/shard_map/ppermute | solution.py:339
  37.5 2.3 %collective-permute-start.8 = (bf16[64,128]{1,0:T(8,128)(2,1)S(1)}, bf16[64,128]{1,0:T(8,128)(2,1)S(1)}, u32[]{:S(2)}, u32[]{:S(2)}) collective-permute-start(bf16[64,128]{1,0:T(8,128)(2,1)S(1)} %get-tuple-element.106), channel_id=1, source_target_pairs={{92,94},{94,92},{88,90},{90,88},{84,86},{86,84},{80,82},{82,80},{7... | collective-permute-start | bytes 49160 | tf_op jit(solution)/shard_map/ppermute | solution.py:339
  41.7 3.3 %collective-permute-start.11 = (bf16[64,128]{1,0:T(8,128)(2,1)S(1)}, bf16[64,128]{1,0:T(8,128)(2,1)S(1)}, u32[]{:S(2)}, u32[]{:S(2)}) collective-permute-start(bf16[64,128]{1,0:T(8,128)(2,1)S(1)} %get-tuple-element.115), channel_id=1, source_target_pairs={{94,28},{28,94},{90,24},{24,90},{86,20},{20,86},{82,16},{16,82},{7... | collective-permute-start | bytes 49160 | tf_op jit(solution)/shard_map/ppermute | solution.py:339
  42.7 2.3 %collective-permute-start.10 = (bf16[64,128]{1,0:T(8,128)(2,1)S(1)}, bf16[64,128]{1,0:T(8,128)(2,1)S(1)}, u32[]{:S(2)}, u32[]{:S(2)}) collective-permute-start(bf16[64,128]{1,0:T(8,128)(2,1)S(1)} %get-tuple-element.116), channel_id=1, source_target_pairs={{92,94},{94,92},{88,90},{90,88},{84,86},{86,84},{80,82},{82,80},{7... | collective-permute-start | bytes 49160 | tf_op jit(solution)/shard_map/ppermute | solution.py:339
  45.0 5.5 %collective-permute-start.13 = (bf16[64,128]{1,0:T(8,128)(2,1)S(1)}, bf16[64,128]{1,0:T(8,128)(2,1)S(1)}, u32[]{:S(2)}, u32[]{:S(2)}) collective-permute-start(bf16[64,128]{1,0:T(8,128)(2,1)S(1)} %get-tuple-element.109), channel_id=1, source_target_pairs={{88,84},{84,88},{80,76},{76,80},{72,68},{68,72},{64,94},{94,64},{9... | collective-permute-start | bytes 49160 | tf_op jit(solution)/shard_map/ppermute | solution.py:339
  47.9 2.6 %collective-permute-start.12 = (bf16[64,128]{1,0:T(8,128)(2,1)S(1)}, bf16[64,128]{1,0:T(8,128)(2,1)S(1)}, u32[]{:S(2)}, u32[]{:S(2)}) collective-permute-start(bf16[64,128]{1,0:T(8,128)(2,1)S(1)} %get-tuple-element.110), channel_id=1, source_target_pairs={{92,88},{88,92},{84,80},{80,84},{76,72},{72,76},{68,64},{64,68},{9... | collective-permute-start | bytes 49160 | tf_op jit(solution)/shard_map/ppermute | solution.py:339
  52.1 14.4 %all-to-all-start = ((bf16[16,48,128]{2,1,0:T(8,128)(2,1)}), bf16[16,48,128]{2,1,0:T(8,128)(2,1)S(1)}, u32[]{:S(2)}, u32[]{:S(2)}) async-start(bf16[16,48,128]{2,1,0:T(8,128)(2,1)} %bitcast.4), calls=%async_computation | async-start | bytes 393216 | tf_op jit(solution)/shard_map/all_to_all | solution.py:398
  59.1 3.5 %collective-permute-start.15 = (bf16[64,128]{1,0:T(8,128)(2,1)S(1)}, bf16[64,128]{1,0:T(8,128)(2,1)S(1)}, u32[]{:S(2)}, u32[]{:S(2)}) collective-permute-start(bf16[64,128]{1,0:T(8,128)(2,1)S(1)} %get-tuple-element.113), channel_id=1, source_target_pairs={{94,28},{28,94},{90,24},{24,90},{86,20},{20,86},{82,16},{16,82},{7... | collective-permute-start | bytes 49160 | tf_op jit(solution)/shard_map/ppermute | solution.py:339
  60.6 2.1 %collective-permute-start.14 = (bf16[64,128]{1,0:T(8,128)(2,1)S(1)}, bf16[64,128]{1,0:T(8,128)(2,1)S(1)}, u32[]{:S(2)}, u32[]{:S(2)}) collective-permute-start(bf16[64,128]{1,0:T(8,128)(2,1)S(1)} %get-tuple-element.114), channel_id=1, source_target_pairs={{92,94},{94,92},{88,90},{90,88},{84,86},{86,84},{80,82},{82,80},{7... | collective-permute-start | bytes 49160 | tf_op jit(solution)/shard_map/ppermute | solution.py:339
  62.7 10.0 %collective-permute-start.17 = (bf16[64,128]{1,0:T(8,128)(2,1)S(1)}, bf16[64,128]{1,0:T(8,128)(2,1)S(1)}, u32[]{:S(2)}, u32[]{:S(2)}) collective-permute-start(bf16[64,128]{1,0:T(8,128)(2,1)S(1)} %get-tuple-element.107), channel_id=1, source_target_pairs={{88,84},{84,88},{80,76},{76,80},{72,68},{68,72},{64,94},{94,64},{9... | collective-permute-start | bytes 49160 | tf_op jit(solution)/shard_map/ppermute | solution.py:339
  66.5 6.2 %collective-permute-start.16 = (bf16[64,128]{1,0:T(8,128)(2,1)S(1)}, bf16[64,128]{1,0:T(8,128)(2,1)S(1)}, u32[]{:S(2)}, u32[]{:S(2)}) collective-permute-start(bf16[64,128]{1,0:T(8,128)(2,1)S(1)} %get-tuple-element.108), channel_id=1, source_target_pairs={{92,88},{88,92},{84,80},{80,84},{76,72},{72,76},{68,64},{64,68},{9... | collective-permute-start | bytes 49160 | tf_op jit(solution)/shard_map/ppermute | solution.py:339
  67.2 12.5 %all-to-all-start.1 = ((bf16[16,48,128]{2,1,0:T(8,128)(2,1)}), bf16[16,48,128]{2,1,0:T(8,128)(2,1)S(1)}, u32[]{:S(2)}, u32[]{:S(2)}) async-start(bf16[16,48,128]{2,1,0:T(8,128)(2,1)} %fold.2), calls=%async_computation.1 | async-start | bytes 393216 | tf_op jit(solution)/shard_map/all_to_all | solution.py:398
  73.4 13.9 %collective-permute-start.18 = (bf16[64,1280]{1,0:T(8,128)(2,1)S(1)}, bf16[64,1280]{1,0:T(8,128)(2,1)S(1)}, u32[]{:S(2)}, u32[]{:S(2)}) collective-permute-start(bf16[64,1280]{1,0:T(8,128)(2,1)S(1)} %last.1), channel_id=1, source_target_pairs={{92,0},{88,2},{84,4},{80,6},{76,8},{72,10},{68,12},{64,14},{94,16}... | collective-permute-start | bytes 491528 | tf_op jit(solution)/shard_map/ppermute | solution.py:339
  80.5 15.1 %all-to-all-start.2 = ((bf16[16,48,128]{2,1,0:T(8,128)(2,1)}), bf16[16,48,128]{2,1,0:T(8,128)(2,1)S(1)}, u32[]{:S(2)}, u32[]{:S(2)}) async-start(bf16[16,48,128]{2,1,0:T(8,128)(2,1)} %fold.3), calls=%async_computation.2 | async-start | bytes 393216 | tf_op jit(solution)/shard_map/all_to_all | solution.py:398
